TPU v7x, 32 devices: a whole 2x2x4 slice. The times are simulated.
32 devices in a mesh: rx: 4 (over y, x), ry: 8 (over z, core).
Axes of the slice: x: 2, y: 2, z: 4, core: 2. Of those that a mesh axis runs over, the one named last changes fastest.
Arguments:
- propagator: float32 [64, 256, 256], P(('rx', 'ry')), may hold values from -1 to 1, as said below
- forcing: float32 [64, 256, 384], P(('rx', 'ry')), may hold values from -0.9 to 0.9
Outputs:
- solution: float32 [64, 256, 384], P(('rx', 'ry'))
- radial_slope: float32 [64, 256, 384], P(('rx', 'ry'))
Inputs may be any that keep to these rules, and one draw needn't show every extreme that they name: Every propagator has spectral norm below 1.
All inputs are finite; a program needn't handle non-finite values.
Results may differ from a plain program's by a relative error of at most 0.00029.
Values sent between devices are 32-bit elements; how exact they have to be, the bound alone decides.
No kernel may reach another device: no remote copies, remote signals or barrier semaphores. Data moves between devices by JAX's collectives and lax.ppermute only.
A program may use at most 64 MiB of HBM per device.

v0:
```python
import jax
import jax.numpy as jnp
from jax import lax
from jax.sharding import PartitionSpec as P


def carried_in(part, axis, combine, identity):
    place = lax.axis_index(axis)
    gathered = jax.tree.map(lambda a: lax.all_gather(a, axis), part)
    state = jax.tree.map(lambda a, e: jnp.zeros_like(a) + jnp.asarray(e, a.dtype), part, identity)

    def one(hop, state):
        return combine(
            state, jax.tree.map(lambda a: lax.dynamic_index_in_dim(a, hop, 0, False), gathered)
        )

    return lax.fori_loop(0, place, one, state)


def from_root(value, axis, source):
    kept = jnp.where(lax.axis_index(axis) == source, value, 0).astype(value.dtype)
    return lax.psum(kept, axis)


def shifted_2(value, axis, by):
    peers = lax.axis_size(axis)
    pairs = [(i, i + by) for i in range(peers) if 0 <= i + by < peers]
    return lax.ppermute(value, axis, pairs)


def product(left, right):
    return jnp.dot(left, right, precision=lax.Precision.HIGHEST, preferred_element_type=jnp.float32)


def combine(earlier, following):
    return (product(following[0], earlier[0]), product(following[0], earlier[1]) + following[1])


def on_device(propagator, forcing):
    interval_count = propagator.shape[0]
    block_total = (propagator[0], forcing[0])
    position = 1
    block_total = combine(block_total, (propagator[position], forcing[position]))
    identity = (
        jnp.eye(propagator.shape[1], dtype=jnp.float32),
        jnp.zeros(forcing.shape[1:], jnp.float32),
    )
    inner_prefix = carried_in(block_total, "ry", combine, identity)
    inclusive = combine(inner_prefix, block_total)
    group_total = (
        from_root(inclusive[0], "ry", lax.axis_size("ry") - 1),
        from_root(inclusive[1], "ry", lax.axis_size("ry") - 1),
    )
    outer_prefix = carried_in(group_total, "rx", combine, identity)
    prefix = combine(outer_prefix, inner_prefix)
    carried = prefix[1]
    states = []
    for position in range(interval_count):
        carried = product(propagator[position], carried) + forcing[position]
        states.append(carried)
    solution = jnp.stack(states, axis=0)
    next_first = shifted_2(solution[0], ("rx", "ry"), -1)
    shifted = jnp.concatenate([solution[1:], next_first[None]], axis=0)
    return (solution, shifted - solution)


def solution(mesh):
    return jax.shard_map(
        on_device,
        mesh=mesh,
        in_specs=(P(("rx", "ry"), None, None), P(("rx", "ry"), None, None)),
        out_specs=(P(("rx", "ry"), None, None), P(("rx", "ry"), None, None)),
        check_vma=False,
    )
```

profile of v0, /device:TPU:7, one launch (start us, length us, event | category | flops | bytes accessed | tf_op | source)
XLA Modules:
  0.0 243.5 jit_solution(4884775422831849863)
XLA Ops:
  7.2 2.1 fusion.19
  9.4 2.5 %convolution_add_fusion.4 = f32[256,384]{1,0:T(8,128)} fusion(f32[2,256,384]{2,1,0:T(8,128)} %param.7, f32[2,256,256]{2,1,0:T(8,128)} %param.6), kind=kOutput, calls=%fused_computation.21 | convolution fusion | flops 302088192 | bytes 1441792 | tf_op jit(solution)/shard_map/dot_general | solution.py:32
  12.0 0.0 all-reduce.3.cloned.1.call-start
  12.0 28.8 %all-gather.11.cloned.1.call-done = f32[2048,256]{1,0:T(8,128)} async-done(((f32[256,256]{1,0:T(8,128)}), f32[2048,256]{1,0:T(8,128)}) %all-gather.11.cloned.1.call-update) | async-done | bytes 2097168 | tf_op jit(solution)/shard_map/all_gather | solution.py:9
  40.9 40.0 %all-gather.13.cloned.1.call-done = f32[2048,384]{1,0:T(8,128)} async-done(((f32[256,384]{1,0:T(8,128)}), f32[2048,384]{1,0:T(8,128)}) %all-gather.13.cloned.1.call-update) | async-done | bytes 3145744 | tf_op jit(solution)/shard_map/all_gather | solution.py:9
  81.0 3.2 %while.24 = (s32[]{:T(128)}, f32[256,256]{1,0:T(8,128)S(1)}, f32[256,384]{1,0:T(8,128)S(1)}, s32[]{:T(128)}, f32[8,256,256]{2,1,0:T(8,128)}, /*index=5*/f32[8,256,384]{2,1,0:T(8,128)}, s32[]{:T(128)}, s32[]{:T(128)}, s32[]{:T(128)}) while((s32[]{:T(128)}, f32[256,256]{1,0:T(8,128)S(1)}, f32[256,384]{1,0:T(8,128)S(1)}, s32[]{:T(128)}, ...), condition=%wide.region_1.2_spmd, body=%wide.region_0.1_spmd.sunk | while | flops 503414784 | bytes 3540099 | solution.py:17
  81.0 1.7 convolution_add_fusion.7
  82.8 1.3 fusion.52
  84.2 1.4 fusion.14
  85.5 1.1 fusion.15
  86.7 72.3 %all-reduce.3.cloned.1.call-done = (f32[1,256,256]{2,1,0:T(8,128)}, f32[1,256,384]{2,1,0:T(8,128)}) async-done(((f32[1,256,256]{2,1,0:T(8,128)}, f32[1,256,384]{2,1,0:T(8,128)}), (f32[1,256,256]{2,1,0:T(8,128)}, f32[1,256,384]{2,1,0:T(8,128)})) %all-reduce.3.cloned.1.call-update) | async-done | bytes 655376 | tf_op jit(solution)/shard_map/psum | solution.py:22
  159.1 0.5 all-gather.9.cloned.1.call-update
  159.6 27.6 %all-gather.7.cloned.1.call-done = f32[4,256,256]{2,1,0:T(8,128)} async-done(((f32[1,256,256]{2,1,0:T(8,128)}), f32[4,256,256]{2,1,0:T(8,128)}) %all-gather.7.cloned.1.call-update) | async-done | bytes 1048592 | tf_op jit(solution)/shard_map/all_gather | solution.py:9
  187.2 32.7 %all-gather.9.cloned.1.call-done = f32[4,256,384]{2,1,0:T(8,128)} async-done(((f32[1,256,384]{2,1,0:T(8,128)}), f32[4,256,384]{2,1,0:T(8,128)}) %all-gather.9.cloned.1.call-update) | async-done | bytes 1572880 | tf_op jit(solution)/shard_map/all_gather | solution.py:9
  220.0 5.3 %while.25 = (s32[]{:T(128)}, f32[256,384]{1,0:T(8,128)S(1)}, s32[]{:T(128)}, f32[4,256,256]{2,1,0:T(8,128)}, f32[4,256,384]{2,1,0:T(8,128)}, /*index=5*/s32[]{:T(128)}, s32[]{:T(128)}, s32[]{:T(128)}) while((s32[]{:T(128)}, f32[256,384]{1,0:T(8,128)S(1)}, s32[]{:T(128)}, f32[4,256,256]{2,1,0:T(8,128)}, f32[4,256,384]{2,1,0:T(8,128)}, ...), condition=%wide.region_5.6_spmd, body=%wide.region_4.5_spmd.sunk | while | flops 302088192 | bytes 2229367 | solution.py:17
  220.0 1.8 convolution_add_fusion.8
  221.9 1.7 convolution_add_fusion.8
  223.6 1.7 convolution_add_fusion.8
  225.3 0.6 convolution_add_fusion.2
  225.9 0.6 fusion.10
  226.6 2.6 %collective-permute-start = (f32[256,384]{1,0:T(8,128)S(1)}, f32[256,384]{1,0:T(8,128)S(1)}, u32[]{:S(2)}, u32[]{:S(2)}) collective-permute-start(f32[256,384]{1,0:T(8,128)S(1)} %fusion.10), channel_id=1, source_target_pairs={{1,0},{2,1},{3,2},{4,3},{5,4},{6,5},{7,6},{8,7},{9,8},{10,9},{11,1... | collective-permute-start | bytes 1179656 | tf_op jit(solution)/shard_map/ppermute | solution.py:28
  229.2 0.6 fusion.12
  229.8 5.9 %collective-permute-done = f32[256,384]{1,0:T(8,128)S(1)} collective-permute-done((f32[256,384]{1,0:T(8,128)S(1)}, f32[256,384]{1,0:T(8,128)S(1)}, u32[]{:S(2)}, u32[]{:S(2)}) %collective-permute-start) | collective-permute-done | bytes 393248 | tf_op jit(solution)/shard_map/ppermute | solution.py:28
  235.7 1.2 maximum_subtract_fusion
  (24 shorter events, 0.4 us)
Async XLA Ops:
  7.2 33.7 %all-gather.11.cloned.1.call-start = ((), (), s32[]{:S(2)}) async-start(), calls=%async_computation.2 | async-start | bytes 2359296 | tf_op jit(solution)/shard_map/all_gather | solution.py:9
  9.3 71.6 %all-gather.13.cloned.1.call-start = ((), (), s32[]{:S(2)}) async-start(), calls=%async_computation.3 | async-start | bytes 3538944 | tf_op jit(solution)/shard_map/all_gather | solution.py:9
  12.0 147.1 %all-reduce.3.cloned.1.call-start = ((), (), s32[]{:S(2)}) async-start(), calls=%async_computation.4 | async-start | bytes 1310720 | tf_op jit(solution)/shard_map/psum | solution.py:22
  80.9 3.2 %copy-start = (f32[256,256]{1,0:T(8,128)S(1)}, f32[256,256]{1,0:T(8,128)}, u32[]{:S(2)}) copy-start(f32[256,256]{1,0:T(8,128)} %fusion.19) | copy-start | bytes 786436
  81.0 3.2 %copy-start.1 = (f32[256,384]{1,0:T(8,128)S(1)}, f32[256,384]{1,0:T(8,128)}, u32[]{:S(2)}) copy-start(f32[256,384]{1,0:T(8,128)} %convolution_add_fusion.4) | copy-start | bytes 1179652
  86.6 100.6 %all-gather.7.cloned.1.call-start = ((), (), s32[]{:S(2)}) async-start(), calls=%async_computation | async-start | bytes 1310720 | tf_op jit(solution)/shard_map/all_gather | solution.py:9
  159.0 60.9 %all-gather.9.cloned.1.call-start = ((), (), s32[]{:S(2)}) async-start(), calls=%async_computation.1 | async-start | bytes 1966080 | tf_op jit(solution)/shard_map/all_gather | solution.py:9
  220.0 6.0 %copy-start.2 = (f32[2,256,256]{2,1,0:T(8,128)S(1)}, f32[2,256,256]{2,1,0:T(8,128)}, u32[]{:S(2)}) copy-start(f32[2,256,256]{2,1,0:T(8,128)} %param.6) | copy-start | bytes 1572868
  220.0 6.0 %copy-start.3 = (f32[2,256,384]{2,1,0:T(8,128)S(1)}, f32[2,256,384]{2,1,0:T(8,128)}, u32[]{:S(2)}) copy-start(f32[2,256,384]{2,1,0:T(8,128)} %param.7) | copy-start | bytes 2359300
  226.6 9.1 %collective-permute-start = (f32[256,384]{1,0:T(8,128)S(1)}, f32[256,384]{1,0:T(8,128)S(1)}, u32[]{:S(2)}, u32[]{:S(2)}) collective-permute-start(f32[256,384]{1,0:T(8,128)S(1)} %fusion.10), channel_id=1, source_target_pairs={{1,0},{2,1},{3,2},{4,3},{5,4},{6,5},{7,6},{8,7},{9,8},{10,9},{11,1... | collective-permute-start | bytes 1179656 | tf_op jit(solution)/shard_map/ppermute | solution.py:28
Sparse Core Ops, SparseCore 0:
  10.2 30.6 all-gather.10
  43.1 37.7 all-gather.12
  86.8 72.2 all-reduce.2
  160.7 26.4 all-gather.6
  188.9 30.9 all-gather.8
where the time goes:
time: 246 us; the launch traced here: 243 us
  waiting for transfers between devices  208 us (85%)
  matrix products  17.1 us (7%)
  between operations  13.9 us (6%)
  starting transfers between devices  2.79 us (1%)
    all_gather x4, waiting for transfers between devices, carried_in(): gathered = jax.tree.map(lambda a: lax.all_gather(a, axis), part)  129 us
    psum x1, waiting for transfers between devices, from_root(): return lax.psum(kept, axis)  72.3 us
    dot_general x12, matrix products, product(): jnp.dot(left, right, precision=lax.Precision.HIGHEST, preferred_element_t...  17.1 us
    ppermute x1, waiting for transfers between devices, shifted_2(): return lax.ppermute(value, axis, pairs)  5.92 us
  transfers between devices with their start and end apart: 6, of which 6 were waited for; matrix products, arithmetic and copies ran while one was open for 1% of the time, Pallas kernels for 0%

commit v1 on v0

v1 whole, which is shorter than its diff:
```python
import functools

import jax
import jax.numpy as jnp
from jax import lax
from jax.experimental import pallas as pl
from jax.experimental.pallas import tpu as pltpu
from jax.sharding import PartitionSpec as P

F32 = jnp.float32
NN = (((1,), (0,)), ((), ()))
NT = (((1,), (1,)), ((), ()))


def split(value):
    high = value.astype(jnp.bfloat16)
    return high, (value - high.astype(F32)).astype(jnp.bfloat16)


def product(left, right, dims=NN):
    dot = functools.partial(lax.dot_general, dimension_numbers=dims, preferred_element_type=F32)
    return dot(left[0], right[0]) + (dot(left[0], right[1]) + dot(left[1], right[0]))


def call(kernel, outs, scratch=()):
    spec = pl.BlockSpec(memory_space=pltpu.VMEM)

    def run(*args):
        return pl.pallas_call(
            kernel,
            in_specs=[spec] * len(args),
            out_specs=[spec] * len(outs),
            out_shape=[jax.ShapeDtypeStruct(shape, F32) for shape in outs],
            scratch_shapes=list(scratch),
            compiler_params=pltpu.CompilerParams(vmem_limit_bytes=32 * 1024 * 1024),
        )(*args)

    return run


def local_kernel(a_ref, f_ref, own_ref, first_ref):
    b = a_ref.shape[1]
    first_ref[:, :b] = a_ref[0]
    first_ref[:, b:] = f_ref[0]
    total_a, total_f = a_ref[0], f_ref[0]
    for i in range(1, a_ref.shape[0]):
        step = split(a_ref[i])
        total_a = product(step, split(total_a))
        total_f = product(step, split(total_f)) + f_ref[i]
    own_ref[:, :b] = total_a
    own_ref[:, b:] = total_f


def chip_kernel(heads, own_ref, other_ref, *outs):
    place = lax.axis_index("ry")
    z = place // 2
    b = own_ref.shape[0]
    part = outs[0].shape[0] - b

    @pl.when(place % 2 == 0)
    def _():
        later = split(other_ref[:, :b])
        total_a = product(later, split(own_ref[:, :b])).T
        total_f = (product(later, split(own_ref[:, b:])) + other_ref[:, b:]).T
        for d, out in enumerate(outs):
            for j, head in enumerate(heads):

                @pl.when(z ^ d == head)
                def _():
                    out[:b] = total_a
                    out[b:] = total_f[j * part : (j + 1) * part]


def line_kernel(heads, *refs):
    n = (len(refs) - 3) // 1
    chips = n
    ins, (pre_ref, p_ref, f_ref) = refs[:chips], refs[chips:]
    place = lax.axis_index("ry")
    z = place // 2
    b = p_ref.shape[0]
    is_head = functools.reduce(jnp.logical_or, [z == head for head in heads])

    @pl.when(jnp.logical_and(place % 2 == 0, is_head))
    def _():
        for d in range(chips):
            pre_ref[z ^ d] = ins[d][...]
        total = pre_ref[0]
        for c in range(1, chips):
            here = pre_ref[c]
            pre_ref[c] = total
            step = split(here[:b])
            total = product(split(total), step)
            total = jnp.concatenate([total[:b], total[b:] + here[b:]], axis=0)
        p_ref[...] = total[:b]
        f_ref[...] = total[b:]


def total_kernel(with_map, preP_ref, preF_ref, p_ref, f_ref, outF_ref, *outP):
    step = split(p_ref[...])
    outF_ref[...] = product(split(preF_ref[...]), step) + f_ref[...]
    if with_map:
        outP[0][...] = product(split(preP_ref[...]), step)


def merge(first, state, preP, preF):
    return jnp.where(first, state, product(split(state), split(preP)) + preF)


def prefix_kernel(width, with_map, count, *refs):
    states, maps = refs[:count], refs[count : 2 * count]
    preP_ref, preF_ref, outP_ref, outF_ref = refs[2 * count :]
    g = lax.axis_index("rx")
    upper = (g // width) % 2 == 1
    first = g % (2 * width) == width

    @pl.when(upper)
    def _():
        state = sum(ref[...] for ref in states[1:]) + states[0][...]
        outF_ref[...] = merge(first, state, preP_ref[...], preF_ref[...])
        earlier = sum(ref[...] for ref in maps[1:]) + maps[0][...]
        outP_ref[...] = jnp.where(first, earlier, product(split(earlier), split(preP_ref[...])))

    @pl.when(jnp.logical_not(upper))
    def _():
        outF_ref[...] = preF_ref[...]
        outP_ref[...] = preP_ref[...]


def enter_kernel(width, count, *refs):
    states = refs[:count]
    preP_ref, preF_ref, pre_ref = refs[count : count + 3]
    outs = refs[count + 3 : -1]
    start_ref = refs[-1]
    place = lax.axis_index("ry")
    z = place // 2
    b = preP_ref.shape[0]
    g = lax.axis_index("rx")
    upper = (g // width) % 2 == 1
    first = g % (2 * width) == width
    start_ref[...] = preF_ref[...]
    if count:

        @pl.when(upper)
        def _():
            state = sum(ref[...] for ref in states[1:]) + states[0][...]
            start_ref[...] = merge(first, state, preP_ref[...], preF_ref[...])

    start = split(start_ref[...])
    for c in range(len(outs)):
        state = start_ref[...]
        if c:
            state = product(start, split(pre_ref[c, :b])) + pre_ref[c, b:]
        for d in range(len(outs)):

            @pl.when(z ^ d == c)
            def _():
                outs[d][...] = state


def run_kernel(heads, count, *refs):
    parts, shared = refs[:count], refs[count : 2 * count]
    other_ref, next_ref, a_ref, f_ref, x_ref, s_ref, in_ref, now_ref = refs[2 * count :]
    place = lax.axis_index("ry")
    z = place // 2
    b = a_ref.shape[1]
    part = parts[0].shape[0]
    for core, sources in enumerate((parts, shared)):
        for j, head in enumerate(heads):
            for d in range(count):

                @pl.when(jnp.logical_and(place % 2 == core, z ^ d == head))
                def _():
                    in_ref[j * part : (j + 1) * part] = sources[d][...]

    entering = split(in_ref[...])
    first = split(a_ref[0])

    @pl.when(place % 2 == 0)
    def _():
        now_ref[...] = product(first, entering, NT) + f_ref[0]

    @pl.when(place % 2 == 1)
    def _():
        state = product(split(other_ref[:, :b]), entering, NT) + other_ref[:, b:]
        now_ref[...] = product(first, split(state)) + f_ref[0]

    now = now_ref[...]
    x_ref[0] = now
    for i in range(1, a_ref.shape[0] + 1):
        if i < a_ref.shape[0]:
            later = product(split(a_ref[i]), split(now)) + f_ref[i]
            x_ref[i] = later
        else:
            later = product(split(next_ref[:, :b]), split(now)) + next_ref[:, b:]
        s_ref[i - 1] = later - now
        now = later


def on_device(propagator, forcing):
    intervals, b, r = forcing.shape
    lines, places = lax.axis_size("rx"), lax.axis_size("ry")
    chips = places // 2
    heads = sorted({max(chips // 2 - 1, 0), chips // 2})
    part = r // len(heads)
    both = ("rx", "ry")

    own, first = call(local_kernel, [(b, b + r)] * 2)(propagator, forcing)
    other = lax.ppermute(own, "ry", [(i, i ^ 1) for i in range(places)])
    cuts = call(functools.partial(chip_kernel, heads), [(b + part, b)] * chips)(own, other)
    gathered = [cuts[0]] + [
        lax.ppermute(cuts[d], "ry", [(2 * (h ^ d), 2 * h) for h in heads]) for d in range(1, chips)
    ]
    gathered, first = lax.optimization_barrier((gathered, first))
    following = lax.ppermute(first, both, [(i + 1, i) for i in range(lines * places - 1)])
    prefixes, line_map, line_state = call(
        functools.partial(line_kernel, heads), [(chips, b + part, b), (b, b), (part, b)]
    )(*gathered)

    def hop(value, pairs):
        at = [2 * h for h in heads]
        return lax.ppermute(value, both, [(s * places + i, t * places + i) for s, t in pairs for i in at])

    preP, preF = jnp.zeros((b, b), F32), jnp.zeros((part, b), F32)
    total_map, total_state = line_map, line_state
    width, states = 1, []
    while width < lines:
        starts = range(0, lines, 2 * width)
        with_map = 2 * width < lines
        if width > 1:
            totals = call(functools.partial(total_kernel, with_map), [(part, b)] + [(b, b)] * with_map)(
                preP, preF, line_map, line_state
            )
            total_state, total_map = totals[0], totals[-1]
        sent = [[(s + width - 1, s + width + j) for s in starts] for j in range(width)]
        states = [hop(total_state, pairs) for pairs in sent]
        if not with_map:
            break
        maps = [hop(total_map, [p for p in pairs if p[0] >= width]) for pairs in sent]
        if width == 1:
            preP, preF = maps[0], states[0]
        else:
            preP, preF = call(
                functools.partial(prefix_kernel, width, with_map, len(states)), [(b, b), (part, b)]
            )(*states, *maps, preP, preF)
        width *= 2
    entering = call(
        functools.partial(enter_kernel, width, len(states)),
        [(part, b)] * chips,
        [pltpu.VMEM((part, b), F32)],
    )(*states, preP, preF, prefixes)
    parts = [entering[0]] + [
        lax.ppermute(entering[d], "ry", [(2 * h, 2 * (h ^ d)) for h in heads]) for d in range(1, chips)
    ]
    shared = [lax.ppermute(value, "ry", [(2 * c, 2 * c + 1) for c in range(chips)]) for value in parts]
    return tuple(
        call(
            functools.partial(run_kernel, heads, chips),
            [(intervals, b, r)] * 2,
            [pltpu.VMEM((r, b), F32), pltpu.VMEM((b, r), F32)],
        )(*parts, *shared, other, following, propagator, forcing)
    )


def solution(mesh):
    spec = P(("rx", "ry"), None, None)
    return jax.shard_map(
        on_device, mesh=mesh, in_specs=(spec, spec), out_specs=(spec, spec), check_vma=False
    )
```

time: 246 us -> 63 us (0.26)
  the two profiles are of different devices: /device:TPU:7 before, /device:TPU:21 now
where the time goes in v1:
time: 63 us; the launch traced here: 62.5 us
  starting transfers between devices  36.1 us (57%)
  waiting for transfers between devices  18.8 us (30%)
  Pallas kernels  4.54 us (7%)
  local copies, waits for them, and re-layouts  2.18 us (3%)
  between operations  0.89 us (1%)
    ppermute x1, starting transfers between devices, on_device(): lax.ppermute(first, both, [(i + 1, i) for i in range(lines * places - 1)])  23.3 us
    ppermute x4, waiting for transfers between devices, on_device(): lax.ppermute(value, 'ry', [(2 * c, 2 * c + 1) for c in range(chips)])  17.1 us
    ppermute x4, starting transfers between devices, on_device(): lax.ppermute(value, 'ry', [(2 * c, 2 * c + 1) for c in range(chips)])  5.17 us
    pallas_call x6, Pallas kernels, run(): pl.pallas_call(kernel, in_specs=[spec] * len(args), out_specs=[spec] * le...  4.54 us
    ppermute x4, starting transfers between devices, hop(): lax.ppermute(value, both, [(s * places + i, t * places + i) for s, t in p...  2.83 us
    unnamed x8, local copies, waits for them, and re-layouts  2.18 us
    ppermute x3, starting transfers between devices, on_device(): lax.ppermute(cuts[d], 'ry', [(2 * (h ^ d), 2 * h) for h in heads])  2.06 us
    ppermute x3, starting transfers between devices, on_device(): lax.ppermute(entering[d], 'ry', [(2 * h, 2 * (h ^ d)) for h in heads])  2.02 us
  transfers between devices with their start and end apart: 16, of which 5 were waited for; matrix products, arithmetic and copies ran while one was open for 0% of the time, Pallas kernels for 2%

profile of v1, /device:TPU:21, one launch (start us, length us, event | category | flops | bytes accessed | tf_op | source)
XLA Modules:
  0.0 62.5 jit_solution(15864809899352257353)
XLA Ops:
  0.6 1.1 %copy-done = f32[2,256,384]{2,1,0:T(8,128)S(1)} copy-done((f32[2,256,384]{2,1,0:T(8,128)S(1)}, f32[2,256,384]{2,1,0:T(8,128)}, u32[]{:S(2)}) %copy-start) | copy-done | bytes 786456
  1.8 1.0 %copy-done.2 = f32[2,256,256]{2,1,0:T(8,128)S(1)} copy-done((f32[2,256,256]{2,1,0:T(8,128)S(1)}, f32[2,256,256]{2,1,0:T(8,128)}, u32[]{:S(2)}) %copy-start.2) | copy-done | bytes 524312
  3.3 0.7 %collective-permute-start = (f32[256,640]{1,0:T(8,128)S(1)}, f32[256,640]{1,0:T(8,128)S(1)}, u32[]{:S(2)}, u32[]{:S(2)}) collective-permute-start(f32[256,640]{1,0:T(8,128)S(1)} %get-tuple-element.20.own_ref), channel_id=1, source_target_pairs={{0,1},{1,0},{2,3},{3,2},{4,5},{5,4},{6,7},{7,6},{8,9},{9,8},{10,11... | collective-permute-start | bytes 1966088 | tf_op jit(solution)/shard_map/ppermute | solution.py:208
  4.1 1.7 %collective-permute-done.other_ref.refs_8_ = f32[256,640]{1,0:T(8,128)S(1)} collective-permute-done((f32[256,640]{1,0:T(8,128)S(1)}, f32[256,640]{1,0:T(8,128)S(1)}, u32[]{:S(2)}, u32[]{:S(2)}) %collective-permute-start) | collective-permute-done | bytes 655392 | tf_op jit(solution)/shard_map/ppermute | solution.py:208
  5.8 0.7 %collective-permute-start.1 = (f32[448,256]{1,0:T(8,128)S(1)}, f32[448,256]{1,0:T(8,128)S(1)}, u32[]{:S(2)}, u32[]{:S(2)}) collective-permute-start(f32[448,256]{1,0:T(8,128)S(1)} %get-tuple-element.22), channel_id=1, source_target_pairs={{0,2},{6,4},{8,10},{14,12},{16,18},{22,20},{24,26},{30,28}} | collective-permute-start | bytes 1376264 | tf_op jit(solution)/shard_map/ppermute | solution.py:211
  6.5 0.7 %collective-permute-start.2 = (f32[448,256]{1,0:T(8,128)S(1)}, f32[448,256]{1,0:T(8,128)S(1)}, u32[]{:S(2)}, u32[]{:S(2)}) collective-permute-start(f32[448,256]{1,0:T(8,128)S(1)} %get-tuple-element.23), channel_id=1, source_target_pairs={{6,2},{0,4},{14,10},{8,12},{22,18},{16,20},{30,26},{24,28}} | collective-permute-start | bytes 1376264 | tf_op jit(solution)/shard_map/ppermute | solution.py:211
  7.2 0.7 %collective-permute-start.3 = (f32[448,256]{1,0:T(8,128)S(1)}, f32[448,256]{1,0:T(8,128)S(1)}, u32[]{:S(2)}, u32[]{:S(2)}) collective-permute-start(f32[448,256]{1,0:T(8,128)S(1)} %get-tuple-element.24), channel_id=1, source_target_pairs={{4,2},{2,4},{12,10},{10,12},{20,18},{18,20},{28,26},{26,28}} | collective-permute-start | bytes 1376264 | tf_op jit(solution)/shard_map/ppermute | solution.py:211
  7.9 0.7 %collective-permute-start.4 = (f32[256,256]{1,0:T(8,128)S(1)}, f32[256,256]{1,0:T(8,128)S(1)}, u32[]{:S(2)}, u32[]{:S(2)}) collective-permute-start(f32[256,256]{1,0:T(8,128)S(1)} %get-tuple-element.30.p_ref), channel_id=1, source_target_pairs={{18,26},{20,28}} | collective-permute-start | bytes 786440 | tf_op jit(solution)/shard_map/ppermute | solution.py:221
  8.7 0.8 %collective-permute-start.5 = (f32[192,256]{1,0:T(8,128)S(1)}, f32[192,256]{1,0:T(8,128)S(1)}, u32[]{:S(2)}, u32[]{:S(2)}) collective-permute-start(f32[192,256]{1,0:T(8,128)S(1)} %get-tuple-element.31.f_ref), channel_id=1, source_target_pairs={{2,10},{4,12},{18,26},{20,28}} | collective-permute-start | bytes 589832 | tf_op jit(solution)/shard_map/ppermute | solution.py:221
  9.5 23.3 %collective-permute-start.15 = (f32[256,640]{1,0:T(8,128)S(1)}, f32[256,640]{1,0:T(8,128)S(1)}, u32[]{:S(2)}, u32[]{:S(2)}) collective-permute-start(f32[256,640]{1,0:T(8,128)S(1)} %get-tuple-element.37), channel_id=1, source_target_pairs={{1,0},{2,1},{3,2},{4,3},{5,4},{6,5},{7,6},{8,7},{9,8},{10,9},{11,1... | collective-permute-start | bytes 1966088 | tf_op jit(solution)/shard_map/ppermute | solution.py:214
  33.0 0.7 %collective-permute-start.7 = (f32[192,256]{1,0:T(8,128)S(1)}, f32[192,256]{1,0:T(8,128)S(1)}, u32[]{:S(2)}, u32[]{:S(2)}) collective-permute-start(f32[192,256]{1,0:T(8,128)S(1)} %shard_map.44), channel_id=1, source_target_pairs={{10,26},{12,28}} | collective-permute-start | bytes 589832 | tf_op jit(solution)/shard_map/ppermute | solution.py:221
  33.7 0.7 %collective-permute-start.6 = (f32[192,256]{1,0:T(8,128)S(1)}, f32[192,256]{1,0:T(8,128)S(1)}, u32[]{:S(2)}, u32[]{:S(2)}) collective-permute-start(f32[192,256]{1,0:T(8,128)S(1)} %shard_map.44), channel_id=1, source_target_pairs={{10,18},{12,20}} | collective-permute-start | bytes 589832 | tf_op jit(solution)/shard_map/ppermute | solution.py:221
  34.4 1.2 %shard_map.45 = (f32[192,256]{1,0:T(8,128)S(1)}, f32[192,256]{1,0:T(8,128)S(1)}, f32[192,256]{1,0:T(8,128)S(1)}, f32[192,256]{1,0:T(8,128)S(1)}) custom-call(f32[192,256]{1,0:T(8,128)S(1)} %collective-permute-done.6.refs_0_, f32[192,256]{1,0:T(8,128)S(1)} %collective-permute-done.7.refs_1_, f32[256,256]{1,0:T(8,128)S(1)} %collective-permute-done.4.preP_ref.refs_2_, ...), custom_call_target="tpu_custom_call" | custom-call | tf_op jit(solution)/shard_map/pallas_call | solution.py:29
  36.3 0.7 %collective-permute-start.9 = (f32[192,256]{1,0:T(8,128)S(1)}, f32[192,256]{1,0:T(8,128)S(1)}, u32[]{:S(2)}, u32[]{:S(2)}) collective-permute-start(f32[192,256]{1,0:T(8,128)S(1)} %get-tuple-element.35), channel_id=1, source_target_pairs={{2,6},{4,0},{10,14},{12,8},{18,22},{20,16},{26,30},{28,24}} | collective-permute-start | bytes 589832 | tf_op jit(solution)/shard_map/ppermute | solution.py:252
  37.0 0.7 %collective-permute-start.10 = (f32[192,256]{1,0:T(8,128)S(1)}, f32[192,256]{1,0:T(8,128)S(1)}, u32[]{:S(2)}, u32[]{:S(2)}) collective-permute-start(f32[192,256]{1,0:T(8,128)S(1)} %get-tuple-element.36), channel_id=1, source_target_pairs={{2,4},{4,2},{10,12},{12,10},{18,20},{20,18},{26,28},{28,26}} | collective-permute-start | bytes 589832 | tf_op jit(solution)/shard_map/ppermute | solution.py:252
  37.7 1.3 %collective-permute-start.11 = (f32[192,256]{1,0:T(8,128)S(1)}, f32[192,256]{1,0:T(8,128)S(1)}, u32[]{:S(2)}, u32[]{:S(2)}) collective-permute-start(f32[192,256]{1,0:T(8,128)S(1)} %get-tuple-element.33.refs_0_), channel_id=1, source_target_pairs={{0,1},{2,3},{4,5},{6,7},{8,9},{10,11},{12,13},{14,15},{16,17},{18,... | collective-permute-start | bytes 589832 | tf_op jit(solution)/shard_map/ppermute | solution.py:254
  39.0 1.3 %collective-permute-start.12 = (f32[192,256]{1,0:T(8,128)S(1)}, f32[192,256]{1,0:T(8,128)S(1)}, u32[]{:S(2)}, u32[]{:S(2)}) collective-permute-start(f32[192,256]{1,0:T(8,128)S(1)} %collective-permute-done.8.refs_1_), channel_id=1, source_target_pairs={{0,1},{2,3},{4,5},{6,7},{8,9},{10,11},{12,13},{14,15},{16,17},{18,... | collective-permute-start | bytes 589832 | tf_op jit(solution)/shard_map/ppermute | solution.py:254
  40.3 1.3 %collective-permute-start.13 = (f32[192,256]{1,0:T(8,128)S(1)}, f32[192,256]{1,0:T(8,128)S(1)}, u32[]{:S(2)}, u32[]{:S(2)}) collective-permute-start(f32[192,256]{1,0:T(8,128)S(1)} %collective-permute-done.9.refs_2_), channel_id=1, source_target_pairs={{0,1},{2,3},{4,5},{6,7},{8,9},{10,11},{12,13},{14,15},{16,17},{18,... | collective-permute-start | bytes 589832 | tf_op jit(solution)/shard_map/ppermute | solution.py:254
  41.6 1.3 %collective-permute-start.14 = (f32[192,256]{1,0:T(8,128)S(1)}, f32[192,256]{1,0:T(8,128)S(1)}, u32[]{:S(2)}, u32[]{:S(2)}) collective-permute-start(f32[192,256]{1,0:T(8,128)S(1)} %collective-permute-done.10.refs_3_), channel_id=1, source_target_pairs={{0,1},{2,3},{4,5},{6,7},{8,9},{10,11},{12,13},{14,15},{16,17},{18,... | collective-permute-start | bytes 589832 | tf_op jit(solution)/shard_map/ppermute | solution.py:254
  42.9 11.9 %collective-permute-done.11.refs_4_ = f32[192,256]{1,0:T(8,128)S(1)} collective-permute-done((f32[192,256]{1,0:T(8,128)S(1)}, f32[192,256]{1,0:T(8,128)S(1)}, u32[]{:S(2)}, u32[]{:S(2)}) %collective-permute-start.11) | collective-permute-done | bytes 196640 | tf_op jit(solution)/shard_map/ppermute | solution.py:254
  54.8 1.6 %collective-permute-done.12.refs_5_ = f32[192,256]{1,0:T(8,128)S(1)} collective-permute-done((f32[192,256]{1,0:T(8,128)S(1)}, f32[192,256]{1,0:T(8,128)S(1)}, u32[]{:S(2)}, u32[]{:S(2)}) %collective-permute-start.12) | collective-permute-done | bytes 196640 | tf_op jit(solution)/shard_map/ppermute | solution.py:254
  56.4 1.3 %collective-permute-done.13.refs_6_ = f32[192,256]{1,0:T(8,128)S(1)} collective-permute-done((f32[192,256]{1,0:T(8,128)S(1)}, f32[192,256]{1,0:T(8,128)S(1)}, u32[]{:S(2)}, u32[]{:S(2)}) %collective-permute-start.13) | collective-permute-done | bytes 196640 | tf_op jit(solution)/shard_map/ppermute | solution.py:254
  57.7 2.3 %collective-permute-done.14.refs_7_ = f32[192,256]{1,0:T(8,128)S(1)} collective-permute-done((f32[192,256]{1,0:T(8,128)S(1)}, f32[192,256]{1,0:T(8,128)S(1)}, u32[]{:S(2)}, u32[]{:S(2)}) %collective-permute-start.14) | collective-permute-done | bytes 196640 | tf_op jit(solution)/shard_map/ppermute | solution.py:254
  60.0 2.5 %shard_map.46 = (f32[2,256,384]{2,1,0:T(8,128)}, f32[2,256,384]{2,1,0:T(8,128)}) custom-call(f32[192,256]{1,0:T(8,128)S(1)} %get-tuple-element.33.refs_0_, f32[192,256]{1,0:T(8,128)S(1)} %collective-permute-done.8.refs_1_, f32[192,256]{1,0:T(8,128)S(1)} %collective-permute-done.9.refs_2_, f32[192,256]{1,0:T(8,128)S(1)} %collective-permute-done.10.refs_3_, ...), custom_call_target="tpu_custom_call" | custom-call | tf_op jit(solution)/shard_map/pallas_call | solution.py:29
  (22 shorter events, 1.5 us)
Async XLA Ops:
  0.6 1.1 %copy-start = (f32[2,256,384]{2,1,0:T(8,128)S(1)}, f32[2,256,384]{2,1,0:T(8,128)}, u32[]{:S(2)}) copy-start(f32[2,256,384]{2,1,0:T(8,128)} %refs_11_.1) | copy-start | bytes 2359300
  1.8 1.0 %copy-start.2 = (f32[2,256,256]{2,1,0:T(8,128)S(1)}, f32[2,256,256]{2,1,0:T(8,128)}, u32[]{:S(2)}) copy-start(f32[2,256,256]{2,1,0:T(8,128)} %refs_10_.1) | copy-start | bytes 1572868
  3.3 2.5 %collective-permute-start = (f32[256,640]{1,0:T(8,128)S(1)}, f32[256,640]{1,0:T(8,128)S(1)}, u32[]{:S(2)}, u32[]{:S(2)}) collective-permute-start(f32[256,640]{1,0:T(8,128)S(1)} %get-tuple-element.20.own_ref), channel_id=1, source_target_pairs={{0,1},{1,0},{2,3},{3,2},{4,5},{5,4},{6,7},{7,6},{8,9},{9,8},{10,11... | collective-permute-start | bytes 1966088 | tf_op jit(solution)/shard_map/ppermute | solution.py:208
  5.8 2.1 %collective-permute-start.1 = (f32[448,256]{1,0:T(8,128)S(1)}, f32[448,256]{1,0:T(8,128)S(1)}, u32[]{:S(2)}, u32[]{:S(2)}) collective-permute-start(f32[448,256]{1,0:T(8,128)S(1)} %get-tuple-element.22), channel_id=1, source_target_pairs={{0,2},{6,4},{8,10},{14,12},{16,18},{22,20},{24,26},{30,28}} | collective-permute-start | bytes 1376264 | tf_op jit(solution)/shard_map/ppermute | solution.py:211
  6.5 1.4 %collective-permute-start.2 = (f32[448,256]{1,0:T(8,128)S(1)}, f32[448,256]{1,0:T(8,128)S(1)}, u32[]{:S(2)}, u32[]{:S(2)}) collective-permute-start(f32[448,256]{1,0:T(8,128)S(1)} %get-tuple-element.23), channel_id=1, source_target_pairs={{6,2},{0,4},{14,10},{8,12},{22,18},{16,20},{30,26},{24,28}} | collective-permute-start | bytes 1376264 | tf_op jit(solution)/shard_map/ppermute | solution.py:211
  7.2 0.7 %collective-permute-start.3 = (f32[448,256]{1,0:T(8,128)S(1)}, f32[448,256]{1,0:T(8,128)S(1)}, u32[]{:S(2)}, u32[]{:S(2)}) collective-permute-start(f32[448,256]{1,0:T(8,128)S(1)} %get-tuple-element.24), channel_id=1, source_target_pairs={{4,2},{2,4},{12,10},{10,12},{20,18},{18,20},{28,26},{26,28}} | collective-permute-start | bytes 1376264 | tf_op jit(solution)/shard_map/ppermute | solution.py:211
  7.9 24.8 %collective-permute-start.4 = (f32[256,256]{1,0:T(8,128)S(1)}, f32[256,256]{1,0:T(8,128)S(1)}, u32[]{:S(2)}, u32[]{:S(2)}) collective-permute-start(f32[256,256]{1,0:T(8,128)S(1)} %get-tuple-element.30.p_ref), channel_id=1, source_target_pairs={{18,26},{20,28}} | collective-permute-start | bytes 786440 | tf_op jit(solution)/shard_map/ppermute | solution.py:221
  8.6 51.4 %copy-start.1 = (f32[2,256,384]{2,1,0:T(8,128)S(1)}, f32[2,256,384]{2,1,0:T(8,128)}, u32[]{:S(2)}) copy-start(f32[2,256,384]{2,1,0:T(8,128)} %refs_11_.1) | copy-start | bytes 2359300
  8.6 51.4 %copy-start.3 = (f32[2,256,256]{2,1,0:T(8,128)S(1)}, f32[2,256,256]{2,1,0:T(8,128)}, u32[]{:S(2)}) copy-start(f32[2,256,256]{2,1,0:T(8,128)} %refs_10_.1) | copy-start | bytes 1572868
  8.7 24.1 %collective-permute-start.5 = (f32[192,256]{1,0:T(8,128)S(1)}, f32[192,256]{1,0:T(8,128)S(1)}, u32[]{:S(2)}, u32[]{:S(2)}) collective-permute-start(f32[192,256]{1,0:T(8,128)S(1)} %get-tuple-element.31.f_ref), channel_id=1, source_target_pairs={{2,10},{4,12},{18,26},{20,28}} | collective-permute-start | bytes 589832 | tf_op jit(solution)/shard_map/ppermute | solution.py:221
  9.5 45.3 %collective-permute-start.15 = (f32[256,640]{1,0:T(8,128)S(1)}, f32[256,640]{1,0:T(8,128)S(1)}, u32[]{:S(2)}, u32[]{:S(2)}) collective-permute-start(f32[256,640]{1,0:T(8,128)S(1)} %get-tuple-element.37), channel_id=1, source_target_pairs={{1,0},{2,1},{3,2},{4,3},{5,4},{6,5},{7,6},{8,7},{9,8},{10,9},{11,1... | collective-permute-start | bytes 1966088 | tf_op jit(solution)/shard_map/ppermute | solution.py:214
  33.0 1.4 %collective-permute-start.7 = (f32[192,256]{1,0:T(8,128)S(1)}, f32[192,256]{1,0:T(8,128)S(1)}, u32[]{:S(2)}, u32[]{:S(2)}) collective-permute-start(f32[192,256]{1,0:T(8,128)S(1)} %shard_map.44), channel_id=1, source_target_pairs={{10,26},{12,28}} | collective-permute-start | bytes 589832 | tf_op jit(solution)/shard_map/ppermute | solution.py:221
  33.7 0.7 %collective-permute-start.6 = (f32[192,256]{1,0:T(8,128)S(1)}, f32[192,256]{1,0:T(8,128)S(1)}, u32[]{:S(2)}, u32[]{:S(2)}) collective-permute-start(f32[192,256]{1,0:T(8,128)S(1)} %shard_map.44), channel_id=1, source_target_pairs={{10,18},{12,20}} | collective-permute-start | bytes 589832 | tf_op jit(solution)/shard_map/ppermute | solution.py:221
  35.7 3.3 %collective-permute-start.8 = (f32[192,256]{1,0:T(8,128)S(1)}, f32[192,256]{1,0:T(8,128)S(1)}, u32[]{:S(2)}, u32[]{:S(2)}) collective-permute-start(f32[192,256]{1,0:T(8,128)S(1)} %get-tuple-element.34), channel_id=1, source_target_pairs={{2,0},{4,6},{10,8},{12,14},{18,16},{20,22},{26,24},{28,30}} | collective-permute-start | bytes 589832 | tf_op jit(solution)/shard_map/ppermute | solution.py:252
  36.3 4.0 %collective-permute-start.9 = (f32[192,256]{1,0:T(8,128)S(1)}, f32[192,256]{1,0:T(8,128)S(1)}, u32[]{:S(2)}, u32[]{:S(2)}) collective-permute-start(f32[192,256]{1,0:T(8,128)S(1)} %get-tuple-element.35), channel_id=1, source_target_pairs={{2,6},{4,0},{10,14},{12,8},{18,22},{20,16},{26,30},{28,24}} | collective-permute-start | bytes 589832 | tf_op jit(solution)/shard_map/ppermute | solution.py:252
  37.0 4.6 %collective-permute-start.10 = (f32[192,256]{1,0:T(8,128)S(1)}, f32[192,256]{1,0:T(8,128)S(1)}, u32[]{:S(2)}, u32[]{:S(2)}) collective-permute-start(f32[192,256]{1,0:T(8,128)S(1)} %get-tuple-element.36), channel_id=1, source_target_pairs={{2,4},{4,2},{10,12},{12,10},{18,20},{20,18},{26,28},{28,26}} | collective-permute-start | bytes 589832 | tf_op jit(solution)/shard_map/ppermute | solution.py:252
  37.7 17.1 %collective-permute-start.11 = (f32[192,256]{1,0:T(8,128)S(1)}, f32[192,256]{1,0:T(8,128)S(1)}, u32[]{:S(2)}, u32[]{:S(2)}) collective-permute-start(f32[192,256]{1,0:T(8,128)S(1)} %get-tuple-element.33.refs_0_), channel_id=1, source_target_pairs={{0,1},{2,3},{4,5},{6,7},{8,9},{10,11},{12,13},{14,15},{16,17},{18,... | collective-permute-start | bytes 589832 | tf_op jit(solution)/shard_map/ppermute | solution.py:254
  39.0 17.4 %collective-permute-start.12 = (f32[192,256]{1,0:T(8,128)S(1)}, f32[192,256]{1,0:T(8,128)S(1)}, u32[]{:S(2)}, u32[]{:S(2)}) collective-permute-start(f32[192,256]{1,0:T(8,128)S(1)} %collective-permute-done.8.refs_1_), channel_id=1, source_target_pairs={{0,1},{2,3},{4,5},{6,7},{8,9},{10,11},{12,13},{14,15},{16,17},{18,... | collective-permute-start | bytes 589832 | tf_op jit(solution)/shard_map/ppermute | solution.py:254
  40.3 17.4 %collective-permute-start.13 = (f32[192,256]{1,0:T(8,128)S(1)}, f32[192,256]{1,0:T(8,128)S(1)}, u32[]{:S(2)}, u32[]{:S(2)}) collective-permute-start(f32[192,256]{1,0:T(8,128)S(1)} %collective-permute-done.9.refs_2_), channel_id=1, source_target_pairs={{0,1},{2,3},{4,5},{6,7},{8,9},{10,11},{12,13},{14,15},{16,17},{18,... | collective-permute-start | bytes 589832 | tf_op jit(solution)/shard_map/ppermute | solution.py:254
  41.6 18.4 %collective-permute-start.14 = (f32[192,256]{1,0:T(8,128)S(1)}, f32[192,256]{1,0:T(8,128)S(1)}, u32[]{:S(2)}, u32[]{:S(2)}) collective-permute-start(f32[192,256]{1,0:T(8,128)S(1)} %collective-permute-done.10.refs_3_), channel_id=1, source_target_pairs={{0,1},{2,3},{4,5},{6,7},{8,9},{10,11},{12,13},{14,15},{16,17},{18,... | collective-permute-start | bytes 589832 | tf_op jit(solution)/shard_map/ppermute | solution.py:254

commit v2 on v0

v2 whole, which is shorter than its diff:
```python
import functools

import jax
import jax.numpy as jnp
from jax import lax
from jax.experimental import pallas as pl
from jax.experimental.pallas import tpu as pltpu
from jax.sharding import PartitionSpec as P

F32 = jnp.float32
NN = (((1,), (0,)), ((), ()))
NT = (((1,), (1,)), ((), ()))
VMEM = pl.BlockSpec(memory_space=pltpu.VMEM)
SHADOW = 3_000_000_000
HBM = pl.BlockSpec(memory_space=pltpu.HBM)


def split(value):
    high = value.astype(jnp.bfloat16)
    return high, (value - high.astype(F32)).astype(jnp.bfloat16)


def product(left, right, dims=NN):
    dot = functools.partial(lax.dot_general, dimension_numbers=dims, preferred_element_type=F32)
    return dot(left[0], right[0]) + (dot(left[0], right[1]) + dot(left[1], right[0]))


def call(kernel, outs, scratch=(), spec=VMEM, out_spec=VMEM, flops=None):
    def run(*args):
        return pl.pallas_call(
            kernel,
            in_specs=[spec] * len(args),
            out_specs=[out_spec] * len(outs),
            out_shape=[jax.ShapeDtypeStruct(shape, F32) for shape in outs],
            scratch_shapes=list(scratch),
            cost_estimate=flops and pl.CostEstimate(flops=flops, bytes_accessed=0, transcendentals=0),
            compiler_params=pltpu.CompilerParams(vmem_limit_bytes=32 * 1024 * 1024),
        )(*args)

    return run


def where():
    place = lax.axis_index("ry")
    return lax.axis_index("rx"), place // 2, place % 2


def rows(start, size):
    return pl.ds(pl.multiple_of(start, 8), size)


def local_kernel(a_ref, f_ref, own_ref, first_ref, rest_ref, sems):
    n, b = a_ref.shape[:2]
    copies = []
    for i in range(n):
        to = first_ref if i == 0 else rest_ref.at[i - 1]
        copies.append(
            (
                pltpu.make_async_copy(a_ref.at[i], to.at[:, pl.ds(0, b)], sems.at[i, 0]),
                pltpu.make_async_copy(f_ref.at[i], to.at[:, pl.ds(b, f_ref.shape[2])], sems.at[i, 1]),
            )
        )
    for part in range(2):
        for i in range(n):
            copies[i][part].start()
    copies[0][0].wait()
    total = first_ref[:, :b]
    steps = []
    for i in range(1, n):
        copies[i][0].wait()
        steps.append(split(rest_ref[i - 1, :, :b]))
        total = product(steps[-1], split(total))
    own_ref[:, :b] = total
    copies[0][1].wait()
    total = first_ref[:, b:]
    for i in range(1, n):
        copies[i][1].wait()
        total = product(steps[i - 1], split(total)) + rest_ref[i - 1, :, b:]
    own_ref[:, b:] = total


def chip_kernel(heads, own_ref, other_ref, map_ref, *refs):
    outs, state_ref = refs[:-1], refs[-1]
    _, z, core = where()
    b = own_ref.shape[0]
    part = outs[0].shape[0] - b // 2

    def combine(earlier_ref, later_ref):
        later = split(later_ref[:, :b])
        map_ref[...] = product(later, split(earlier_ref[:, :b])).T
        state_ref[...] = (product(later, split(earlier_ref[:, b:])) + later_ref[:, b:]).T

    @pl.when(core == 0)
    def _():
        combine(own_ref, other_ref)

    @pl.when(core == 1)
    def _():
        combine(other_ref, own_ref)

    for d, out in enumerate(outs):
        for j, head in enumerate(heads):

            @pl.when(z ^ d == head)
            def _():
                out[: b // 2] = map_ref[rows(core * (b // 2), b // 2)]
                out[b // 2 :] = state_ref[rows((2 * j + core) * part, part)]


def line_kernel(heads, chips, *refs):
    map_ref, ins, others = refs[0], refs[1 : 1 + chips], refs[1 + chips : 2 * chips]
    preP_ref, preF_ref, p_ref, f_ref = refs[2 * chips :]
    _, z, core = where()
    b = map_ref.shape[0]
    half = b // 2

    @pl.when(functools.reduce(jnp.logical_or, [z == head for head in heads]))
    def _():
        for d in range(chips):
            preF_ref[z ^ d] = ins[d][half:]
            if d == 0:
                preP_ref[z] = map_ref[...]
            else:
                preP_ref[z ^ d, rows(core * half, half)] = ins[d][:half]
                preP_ref[z ^ d, rows(half - core * half, half)] = others[d - 1][:half]
        total_map, total_state = preP_ref[0], preF_ref[0]
        for c in range(1, chips):
            step, state = split(preP_ref[c]), preF_ref[c]
            preP_ref[c], preF_ref[c] = total_map, total_state
            total_map = product(split(total_map), step)
            total_state = product(split(total_state), step) + state
        p_ref[...] = total_map
        f_ref[...] = total_state


def total_kernel(with_map, *refs):
    *preP, preF_ref, p_ref, f_ref = refs[: 3 + with_map]
    outs = refs[3 + with_map :]
    step = split(p_ref[...])
    outs[0][...] = product(split(preF_ref[...]), step) + f_ref[...]
    if with_map:
        outs[1][...] = product(split(preP[0][...]), step)


def choose(refs, width, out_ref):
    g = where()[0]
    source = g // (2 * width) * (2 * width) + width - 1
    for j, ref in enumerate(refs):

        @pl.when(g ^ (width + j) == source)
        def _():
            out_ref[...] = ref[...]


def prefix_map_kernel(width, *refs):
    *maps, pre_ref, out_ref = refs
    g = where()[0]

    @pl.when(g // width % 2 == 0)
    def _():
        out_ref[...] = pre_ref[...]

    @pl.when(g // width % 2 == 1)
    def _():
        choose(maps, width, out_ref)

        @pl.when(g % width != 0)
        def _():
            out_ref[...] = product(split(out_ref[...]), split(pre_ref[...]))


def advance(width, states, pre, out_ref):
    g = where()[0]

    @pl.when(g // width % 2 == 1)
    def _():
        choose(states, width, out_ref)
        if pre:

            @pl.when(g % width != 0)
            def _():
                out_ref[...] = product(split(out_ref[...]), split(pre[0][...])) + pre[1][...]

    if pre:

        @pl.when(g // width % 2 == 0)
        def _():
            out_ref[...] = pre[1][...]


def prefix_state_kernel(width, count, *refs):
    advance(width, refs[:count], refs[count:-1], refs[-1])


def enter_kernel(width, count, with_pre, *refs):
    states, refs = refs[:count], refs[count:]
    pre, refs = refs[: 2 * with_pre], refs[2 * with_pre :]
    lineP_ref, lineF_ref, *outs, start_ref = refs
    g, z, _ = where()
    if count:
        advance(width, states, pre, start_ref)

    @pl.when(g == 0)
    def _():
        start_ref[...] = jnp.zeros_like(start_ref)

    start = split(start_ref[...])
    for c in range(len(outs)):
        state = start_ref[...]
        if c:
            state = product(start, split(lineP_ref[c])) + lineF_ref[c]
        for d in range(len(outs)):

            @pl.when(z ^ d == c)
            def _():
                outs[d][...] = state


def run_kernel(heads, count, *refs):
    parts, shared = refs[:count], refs[count : 2 * count]
    other_ref, next_ref, first_ref, rest_ref, x_ref, s_ref, in_ref, xs_ref, ss_ref, sems = refs[2 * count :]
    g, z, core = where()
    b = first_ref.shape[0]
    n = x_ref.shape[0]
    part = parts[0].shape[0]
    for d in range(count):
        for j, head in enumerate(heads):

            @pl.when(z ^ d == head)
            def _():
                in_ref[rows((2 * j + core) * part, part)] = parts[d][...]
                in_ref[rows((2 * j + 1 - core) * part, part)] = shared[d][...]

    entering = split(in_ref[...])
    step = split(first_ref[:, :b])

    @pl.when(core == 0)
    def _():
        xs_ref[0] = product(step, entering, NT) + first_ref[:, b:]

    @pl.when(core == 1)
    def _():
        state = product(split(other_ref[:, :b]), entering, NT) + other_ref[:, b:]
        xs_ref[0] = product(step, split(state)) + first_ref[:, b:]

    copies = [pltpu.make_async_copy(xs_ref.at[i], x_ref.at[i], sems.at[0, i]) for i in range(n)]
    copies += [pltpu.make_async_copy(ss_ref.at[i], s_ref.at[i], sems.at[1, i]) for i in range(n)]
    copies[0].start()
    now = xs_ref[0]
    for i in range(1, n):
        later = product(split(rest_ref[i - 1, :, :b]), split(now)) + rest_ref[i - 1, :, b:]
        xs_ref[i] = later
        copies[i].start()
        ss_ref[i - 1] = later - now
        copies[n + i - 1].start()
        now = later
    ss_ref[n - 1] = product(split(next_ref[:, :b]), split(now)) + next_ref[:, b:] - now

    @pl.when(g * lax.axis_size("ry") + 2 * z + core == lax.axis_size("rx") * lax.axis_size("ry") - 1)
    def _():
        ss_ref[n - 1] = -xs_ref[n - 1]

    copies[2 * n - 1].start()
    for copy in copies:
        copy.wait()


def filled(useful, chips):
    sources = [c for c in range(chips) if all(c != s for s, _ in useful)]
    targets = [c for c in range(chips) if all(c != t for _, t in useful)]
    pairs = []
    for s, t in [*useful, *zip(sources, targets, strict=True)]:
        pairs += [(2 * s + core, 2 * t + (core ^ (s == t))) for core in range(2)]
    return pairs


def on_device(propagator, forcing):
    intervals, b, r = forcing.shape
    lines, places = lax.axis_size("rx"), lax.axis_size("ry")
    chips, devices = places // 2, lines * places
    heads = sorted({max(chips // 2 - 1, 0), chips // 2})
    part = r // (2 * len(heads))

    def swap(value):
        return lax.ppermute(value, "ry", [(i, i ^ 1) for i in range(places)])

    def hop(value, d, start=0):
        pairs = []
        for g in range(lines):
            for i in range(places):
                at, to = (g ^ d, i) if i // 2 in heads and g >= start else (g, i ^ 1)
                pairs.append((g * places + i, at * places + to))
        return lax.ppermute(value, ("rx", "ry"), pairs)

    propagator, forcing = (pltpu.with_memory_space_constraint(a, pltpu.HBM) for a in (propagator, forcing))
    own, first, rest = call(
        local_kernel,
        [(b, b + r), (b, b + r), (max(intervals - 1, 1), b, b + r)],
        [pltpu.SemaphoreType.DMA((intervals, 2))],
        spec=HBM,
    )(propagator, forcing)
    other = swap(own)
    chip_map, *cuts = call(
        functools.partial(chip_kernel, heads),
        [(b, b)] + [(b // 2 + part, b)] * chips,
        [pltpu.VMEM((r, b), F32)],
    )(own, other)
    gathered = [
        lax.ppermute(cuts[d], "ry", filled([(h ^ d, h) for h in heads], chips)) for d in range(1, chips)
    ]
    swapped = [swap(value) for value in gathered]
    lineP, lineF, line_map, line_state = call(
        functools.partial(line_kernel, heads, chips),
        [(chips, b, b), (chips, part, b), (b, b), (part, b)],
    )(chip_map, cuts[0], *gathered, *swapped)

    def carried(value, width, pre):
        maps = [hop(value, d, 2 * width) for d in range(width, 2 * width)]
        if width == 1:
            return maps
        return call(functools.partial(prefix_map_kernel, width), [(b, b)])(*maps, *pre)

    total_map, total_state, pre_map, pre_state = line_map, line_state, [], None
    width, states = 1, []
    while width < lines:
        last = 2 * width >= lines
        if width > 1:
            total_state, *total_map = call(
                functools.partial(total_kernel, not last),
                [(part, b)] + [(b, b)] * (not last),
                flops=SHADOW,
            )(*pre_map * (not last), pre_state, line_map, line_state)
            total_map = total_map and total_map[0]
        states = [hop(total_state, d) for d in range(width, 2 * width)]
        if last:
            break
        pre_map = carried(total_map, width, pre_map)
        if width == 1:
            pre_state = states[0]
        else:
            (pre_state,) = call(functools.partial(prefix_state_kernel, width, width), [(part, b)])(
                *states, *pre_map, pre_state
            )
        width *= 2
    pre = [] if pre_state is None else [*pre_map, pre_state]
    first_late, _ = lax.optimization_barrier((first, line_state))
    following = lax.ppermute(first_late, ("rx", "ry"), [(i, (i - 1) % devices) for i in range(devices)])
    entering = call(
        functools.partial(enter_kernel, width, len(states), bool(pre)),
        [(part, b)] * chips,
        [pltpu.VMEM((part, b), F32)],
    )(*states, *pre, lineP, lineF)
    parts = [entering[0]] + [
        lax.ppermute(entering[d], "ry", filled([(h, h ^ d) for h in heads], chips)) for d in range(1, chips)
    ]
    return tuple(
        call(
            functools.partial(run_kernel, heads, chips),
            [(intervals, b, r)] * 2,
            [
                pltpu.VMEM((r, b), F32),
                pltpu.VMEM((intervals, b, r), F32),
                pltpu.VMEM((intervals, b, r), F32),
                pltpu.SemaphoreType.DMA((2, intervals)),
            ],
            out_spec=HBM,
        )(*parts, *[swap(value) for value in parts], other, following, first, rest)
    )


def solution(mesh):
    spec = P(("rx", "ry"), None, None)
    return jax.shard_map(
        on_device, mesh=mesh, in_specs=(spec, spec), out_specs=(spec, spec), check_vma=False
    )
```

time: 246 us -> 49.8 us (0.20)
  the two profiles are of different devices: /device:TPU:7 before, /device:TPU:1 now
where the time goes in v2:
time: 49.8 us; the launch traced here: 49.7 us
  starting transfers between devices  31.4 us (63%)
  waiting for transfers between devices  11.7 us (23%)
  Pallas kernels  5.87 us (12%)
  between operations  0.7 us (1%)
    ppermute x3, starting transfers between devices, on_device(): lax.ppermute(entering[d], 'ry', filled([(h, h ^ d) for h in heads], chips))  11.2 us
    ppermute x8, starting transfers between devices, swap(): return lax.ppermute(value, 'ry', [(i, i ^ 1) for i in range(places)])  7.85 us
    ppermute x4, starting transfers between devices, hop(): return lax.ppermute(value, ('rx', 'ry'), pairs)  6.47 us
    ppermute x3, waiting for transfers between devices, on_device(): lax.ppermute(cuts[d], 'ry', filled([(h ^ d, h) for h in heads], chips))  5.95 us
    pallas_call x6, Pallas kernels, run(): pl.pallas_call(kernel, in_specs=[spec] * len(args), out_specs=[out_spec]...  5.87 us
    ppermute x3, starting transfers between devices, on_device(): lax.ppermute(cuts[d], 'ry', filled([(h ^ d, h) for h in heads], chips))  5.74 us
    ppermute x8, waiting for transfers between devices, swap(): return lax.ppermute(value, 'ry', [(i, i ^ 1) for i in range(places)])  4.81 us
  transfers between devices with their start and end apart: 19, of which 9 were waited for; matrix products, arithmetic and copies ran while one was open for 0% of the time, Pallas kernels for 2%

profile of v2, /device:TPU:1, one launch (start us, length us, event | category | flops | bytes accessed | tf_op | source)
XLA Modules:
  0.0 49.7 jit_solution(5574974525561305362)
XLA Ops:
  0.6 1.8 %shard_map.41 = (f32[256,640]{1,0:T(8,128)S(1)}, f32[256,640]{1,0:T(8,128)S(1)}, f32[1,256,640]{2,1,0:T(8,128)S(1)}) custom-call(f32[2,256,256]{2,1,0:T(8,128)} %a_ref.1, f32[2,256,384]{2,1,0:T(8,128)} %f_ref.1), custom_call_target="tpu_custom_call" | custom-call | tf_op jit(solution)/shard_map/pallas_call | solution.py:30
  2.6 2.0 %collective-permute-done.other_ref.refs_8_ = f32[256,640]{1,0:T(8,128)S(1)} collective-permute-done((f32[256,640]{1,0:T(8,128)S(1)}, f32[256,640]{1,0:T(8,128)S(1)}, u32[]{:S(2)}, u32[]{:S(2)}) %collective-permute-start) | collective-permute-done | bytes 655392 | tf_op jit(solution)/shard_map/ppermute | solution.py:285
  4.6 0.7 %shard_map.42 = (f32[256,256]{1,0:T(8,128)S(1)}, f32[224,256]{1,0:T(8,128)S(1)}, f32[224,256]{1,0:T(8,128)S(1)}, f32[224,256]{1,0:T(8,128)S(1)}, f32[224,256]{1,0:T(8,128)S(1)}) custom-call(f32[256,640]{1,0:T(8,128)S(1)} %get-tuple-element.19.own_ref, f32[256,640]{1,0:T(8,128)S(1)} %collective-permute-done.other_ref.refs_8_), custom_call_target="tpu_custom_call" | custom-call | tf_op jit(solution)/shard_map/pallas_call | solution.py:30
  5.3 2.5 %collective-permute-start.1 = (f32[224,256]{1,0:T(8,128)S(1)}, f32[224,256]{1,0:T(8,128)S(1)}, u32[]{:S(2)}, u32[]{:S(2)}) collective-permute-start(f32[224,256]{1,0:T(8,128)S(1)} %get-tuple-element.22), channel_id=1, source_target_pairs={{0,2},{1,3},{6,4},{7,5},{2,0},{3,1},{4,6},{5,7},{8,10},{9,11},{14,... | collective-permute-start | bytes 688136 | tf_op jit(solution)/shard_map/ppermute | solution.py:309
  7.8 2.3 %collective-permute-start.2 = (f32[224,256]{1,0:T(8,128)S(1)}, f32[224,256]{1,0:T(8,128)S(1)}, u32[]{:S(2)}, u32[]{:S(2)}) collective-permute-start(f32[224,256]{1,0:T(8,128)S(1)} %get-tuple-element.23), channel_id=1, source_target_pairs={{6,2},{7,3},{0,4},{1,5},{2,0},{3,1},{4,6},{5,7},{14,10},{15,11},{8... | collective-permute-start | bytes 688136 | tf_op jit(solution)/shard_map/ppermute | solution.py:309
  10.1 0.9 %collective-permute-start.3 = (f32[224,256]{1,0:T(8,128)S(1)}, f32[224,256]{1,0:T(8,128)S(1)}, u32[]{:S(2)}, u32[]{:S(2)}) collective-permute-start(f32[224,256]{1,0:T(8,128)S(1)} %get-tuple-element.24), channel_id=1, source_target_pairs={{4,2},{5,3},{2,4},{3,5},{0,1},{1,0},{6,7},{7,6},{12,10},{13,11},{1... | collective-permute-start | bytes 688136 | tf_op jit(solution)/shard_map/ppermute | solution.py:309
  11.0 2.4 %collective-permute-done.1.refs_2_ = f32[224,256]{1,0:T(8,128)S(1)} collective-permute-done((f32[224,256]{1,0:T(8,128)S(1)}, f32[224,256]{1,0:T(8,128)S(1)}, u32[]{:S(2)}, u32[]{:S(2)}) %collective-permute-start.1) | collective-permute-done | bytes 229408 | tf_op jit(solution)/shard_map/ppermute | solution.py:309
  13.5 1.4 %collective-permute-start.4 = (f32[224,256]{1,0:T(8,128)S(1)}, f32[224,256]{1,0:T(8,128)S(1)}, u32[]{:S(2)}, u32[]{:S(2)}) collective-permute-start(f32[224,256]{1,0:T(8,128)S(1)} %collective-permute-done.1.refs_2_), channel_id=1, source_target_pairs={{0,1},{1,0},{2,3},{3,2},{4,5},{5,4},{6,7},{7,6},{8,9},{9,8},{10,11... | collective-permute-start | bytes 688136 | tf_op jit(solution)/shard_map/ppermute | solution.py:285
  14.8 3.5 %collective-permute-done.2.refs_3_ = f32[224,256]{1,0:T(8,128)S(1)} collective-permute-done((f32[224,256]{1,0:T(8,128)S(1)}, f32[224,256]{1,0:T(8,128)S(1)}, u32[]{:S(2)}, u32[]{:S(2)}) %collective-permute-start.2) | collective-permute-done | bytes 229408 | tf_op jit(solution)/shard_map/ppermute | solution.py:309
  18.4 0.9 %collective-permute-start.5 = (f32[224,256]{1,0:T(8,128)S(1)}, f32[224,256]{1,0:T(8,128)S(1)}, u32[]{:S(2)}, u32[]{:S(2)}) collective-permute-start(f32[224,256]{1,0:T(8,128)S(1)} %collective-permute-done.2.refs_3_), channel_id=1, source_target_pairs={{0,1},{1,0},{2,3},{3,2},{4,5},{5,4},{6,7},{7,6},{8,9},{9,8},{10,11... | collective-permute-start | bytes 688136 | tf_op jit(solution)/shard_map/ppermute | solution.py:285
  19.3 1.1 %collective-permute-done.5.refs_6_ = f32[224,256]{1,0:T(8,128)S(1)} collective-permute-done((f32[224,256]{1,0:T(8,128)S(1)}, f32[224,256]{1,0:T(8,128)S(1)}, u32[]{:S(2)}, u32[]{:S(2)}) %collective-permute-start.5) | collective-permute-done | bytes 229408 | tf_op jit(solution)/shard_map/ppermute | solution.py:285
  20.4 0.4 collective-permute-done.6.refs_7_
  20.8 0.3 collective-permute-start.7
  21.3 5.6 %collective-permute-start.10 = (f32[256,256]{1,0:T(8,128)S(1)}, f32[256,256]{1,0:T(8,128)S(1)}, u32[]{:S(2)}, u32[]{:S(2)}) collective-permute-start(f32[256,256]{1,0:T(8,128)S(1)} %get-tuple-element.26.refs_1_), channel_id=1, source_target_pairs={{0,1},{1,0},{2,3},{3,2},{4,5},{5,4},{6,7},{7,6},{8,9},{9,8},{10,11... | collective-permute-start | bytes 786440 | tf_op jit(solution)/shard_map/ppermute | solution.py:293
  27.1 0.5 collective-permute-start.8
  27.6 0.8 %collective-permute-done.9.refs_1_ = f32[96,256]{1,0:T(8,128)S(1)} collective-permute-done((f32[96,256]{1,0:T(8,128)S(1)}, f32[96,256]{1,0:T(8,128)S(1)}, u32[]{:S(2)}, u32[]{:S(2)}) %collective-permute-start.9) | collective-permute-done | bytes 98336 | tf_op jit(solution)/shard_map/ppermute | solution.py:293
  28.6 0.8 %shard_map.45 = (f32[96,256]{1,0:T(8,128)S(1)}, f32[96,256]{1,0:T(8,128)S(1)}, f32[96,256]{1,0:T(8,128)S(1)}, f32[96,256]{1,0:T(8,128)S(1)}) custom-call(f32[96,256]{1,0:T(8,128)S(1)} %collective-permute-done.8.refs_0_, f32[96,256]{1,0:T(8,128)S(1)} %collective-permute-done.9.refs_1_, f32[256,256]{1,0:T(8,128)S(1)} %collective-permute-done.10.refs_2_, ...), custom_call_target="tpu_custom_call" | custom-call | tf_op jit(solution)/shard_map/pallas_call | solution.py:30
  29.4 9.1 %collective-permute-start.11 = (f32[96,256]{1,0:T(8,128)S(1)}, f32[96,256]{1,0:T(8,128)S(1)}, u32[]{:S(2)}, u32[]{:S(2)}) collective-permute-start(f32[96,256]{1,0:T(8,128)S(1)} %get-tuple-element.30), channel_id=1, source_target_pairs={{2,0},{3,1},{4,6},{5,7},{0,2},{1,3},{6,4},{7,5},{10,8},{11,9},{12,... | collective-permute-start | bytes 294920 | tf_op jit(solution)/shard_map/ppermute | solution.py:354
  38.5 2.0 %collective-permute-start.13 = (f32[96,256]{1,0:T(8,128)S(1)}, f32[96,256]{1,0:T(8,128)S(1)}, u32[]{:S(2)}, u32[]{:S(2)}) collective-permute-start(f32[96,256]{1,0:T(8,128)S(1)} %get-tuple-element.32), channel_id=1, source_target_pairs={{2,4},{3,5},{4,2},{5,3},{0,1},{1,0},{6,7},{7,6},{10,12},{11,13},{1... | collective-permute-start | bytes 294920 | tf_op jit(solution)/shard_map/ppermute | solution.py:354
  40.5 3.6 %collective-permute-start.15 = (f32[96,256]{1,0:T(8,128)S(1)}, f32[96,256]{1,0:T(8,128)S(1)}, u32[]{:S(2)}, u32[]{:S(2)}) collective-permute-start(f32[96,256]{1,0:T(8,128)S(1)} %collective-permute-done.11.refs_1_), channel_id=1, source_target_pairs={{0,1},{1,0},{2,3},{3,2},{4,5},{5,4},{6,7},{7,6},{8,9},{9,8},{10,11... | collective-permute-start | bytes 294920 | tf_op jit(solution)/shard_map/ppermute | solution.py:285
  44.1 1.9 %collective-permute-start.16 = (f32[96,256]{1,0:T(8,128)S(1)}, f32[96,256]{1,0:T(8,128)S(1)}, u32[]{:S(2)}, u32[]{:S(2)}) collective-permute-start(f32[96,256]{1,0:T(8,128)S(1)} %collective-permute-done.12.refs_2_), channel_id=1, source_target_pairs={{0,1},{1,0},{2,3},{3,2},{4,5},{5,4},{6,7},{7,6},{8,9},{9,8},{10,11... | collective-permute-start | bytes 294920 | tf_op jit(solution)/shard_map/ppermute | solution.py:285
  46.0 0.9 %collective-permute-done.16.refs_6_ = f32[96,256]{1,0:T(8,128)S(1)} collective-permute-done((f32[96,256]{1,0:T(8,128)S(1)}, f32[96,256]{1,0:T(8,128)S(1)}, u32[]{:S(2)}, u32[]{:S(2)}) %collective-permute-start.16) | collective-permute-done | bytes 98336 | tf_op jit(solution)/shard_map/ppermute | solution.py:285
  46.9 0.4 collective-permute-done.17.refs_7_
  47.3 2.4 %shard_map.46 = (f32[2,256,384]{2,1,0:T(8,128)}, f32[2,256,384]{2,1,0:T(8,128)}) custom-call(f32[96,256]{1,0:T(8,128)S(1)} %get-tuple-element.29.refs_0_, f32[96,256]{1,0:T(8,128)S(1)} %collective-permute-done.11.refs_1_, f32[96,256]{1,0:T(8,128)S(1)} %collective-permute-done.12.refs_2_, f32[96,256]{1,0:T(8,128)S(1)} %collective-permute-done.13.refs_3_, ...), custom_call_target="tpu_custom_call" | custom-call | tf_op jit(solution)/shard_map/pallas_call | solution.py:30
  (20 shorter events, 0.8 us)
Async XLA Ops:
  2.5 2.2 %collective-permute-start = (f32[256,640]{1,0:T(8,128)S(1)}, f32[256,640]{1,0:T(8,128)S(1)}, u32[]{:S(2)}, u32[]{:S(2)}) collective-permute-start(f32[256,640]{1,0:T(8,128)S(1)} %get-tuple-element.19.own_ref), channel_id=1, source_target_pairs={{0,1},{1,0},{2,3},{3,2},{4,5},{5,4},{6,7},{7,6},{8,9},{9,8},{10,11... | collective-permute-start | bytes 1966088 | tf_op jit(solution)/shard_map/ppermute | solution.py:285
  5.3 8.2 %collective-permute-start.1 = (f32[224,256]{1,0:T(8,128)S(1)}, f32[224,256]{1,0:T(8,128)S(1)}, u32[]{:S(2)}, u32[]{:S(2)}) collective-permute-start(f32[224,256]{1,0:T(8,128)S(1)} %get-tuple-element.22), channel_id=1, source_target_pairs={{0,2},{1,3},{6,4},{7,5},{2,0},{3,1},{4,6},{5,7},{8,10},{9,11},{14,... | collective-permute-start | bytes 688136 | tf_op jit(solution)/shard_map/ppermute | solution.py:309
  7.8 10.6 %collective-permute-start.2 = (f32[224,256]{1,0:T(8,128)S(1)}, f32[224,256]{1,0:T(8,128)S(1)}, u32[]{:S(2)}, u32[]{:S(2)}) collective-permute-start(f32[224,256]{1,0:T(8,128)S(1)} %get-tuple-element.23), channel_id=1, source_target_pairs={{6,2},{7,3},{0,4},{1,5},{2,0},{3,1},{4,6},{5,7},{14,10},{15,11},{8... | collective-permute-start | bytes 688136 | tf_op jit(solution)/shard_map/ppermute | solution.py:309
  10.1 9.2 %collective-permute-start.3 = (f32[224,256]{1,0:T(8,128)S(1)}, f32[224,256]{1,0:T(8,128)S(1)}, u32[]{:S(2)}, u32[]{:S(2)}) collective-permute-start(f32[224,256]{1,0:T(8,128)S(1)} %get-tuple-element.24), channel_id=1, source_target_pairs={{4,2},{5,3},{2,4},{3,5},{0,1},{1,0},{6,7},{7,6},{12,10},{13,11},{1... | collective-permute-start | bytes 688136 | tf_op jit(solution)/shard_map/ppermute | solution.py:309
  13.5 5.8 %collective-permute-start.4 = (f32[224,256]{1,0:T(8,128)S(1)}, f32[224,256]{1,0:T(8,128)S(1)}, u32[]{:S(2)}, u32[]{:S(2)}) collective-permute-start(f32[224,256]{1,0:T(8,128)S(1)} %collective-permute-done.1.refs_2_), channel_id=1, source_target_pairs={{0,1},{1,0},{2,3},{3,2},{4,5},{5,4},{6,7},{7,6},{8,9},{9,8},{10,11... | collective-permute-start | bytes 688136 | tf_op jit(solution)/shard_map/ppermute | solution.py:285
  18.4 2.0 %collective-permute-start.5 = (f32[224,256]{1,0:T(8,128)S(1)}, f32[224,256]{1,0:T(8,128)S(1)}, u32[]{:S(2)}, u32[]{:S(2)}) collective-permute-start(f32[224,256]{1,0:T(8,128)S(1)} %collective-permute-done.2.refs_3_), channel_id=1, source_target_pairs={{0,1},{1,0},{2,3},{3,2},{4,5},{5,4},{6,7},{7,6},{8,9},{9,8},{10,11... | collective-permute-start | bytes 688136 | tf_op jit(solution)/shard_map/ppermute | solution.py:285
  19.3 1.5 %collective-permute-start.6 = (f32[224,256]{1,0:T(8,128)S(1)}, f32[224,256]{1,0:T(8,128)S(1)}, u32[]{:S(2)}, u32[]{:S(2)}) collective-permute-start(f32[224,256]{1,0:T(8,128)S(1)} %collective-permute-done.3.refs_4_), channel_id=1, source_target_pairs={{0,1},{1,0},{2,3},{3,2},{4,5},{5,4},{6,7},{7,6},{8,9},{9,8},{10,11... | collective-permute-start | bytes 688136 | tf_op jit(solution)/shard_map/ppermute | solution.py:285
  20.8 6.1 %collective-permute-start.7 = (f32[96,256]{1,0:T(8,128)S(1)}, f32[96,256]{1,0:T(8,128)S(1)}, u32[]{:S(2)}, u32[]{:S(2)}) collective-permute-start(f32[96,256]{1,0:T(8,128)S(1)} %get-tuple-element.25.refs_2_), channel_id=1, source_target_pairs={{0,1},{1,0},{2,10},{3,11},{4,12},{5,13},{6,7},{7,6},{8,9},{9,8},{1... | collective-permute-start | bytes 294920 | tf_op jit(solution)/shard_map/ppermute | solution.py:293
  21.1 26.2 %collective-permute-start.18 = (f32[256,640]{1,0:T(8,128)S(1)}, f32[256,640]{1,0:T(8,128)S(1)}, u32[]{:S(2)}, u32[]{:S(2)}) collective-permute-start(f32[256,640]{1,0:T(8,128)S(1)} %get-tuple-element.34.refs_10_), channel_id=1, source_target_pairs={{0,31},{1,0},{2,1},{3,2},{4,3},{5,4},{6,5},{7,6},{8,7},{9,8},{10,9... | collective-permute-start | bytes 1966088 | tf_op jit(solution)/shard_map/ppermute | solution.py:347
  21.3 7.3 %collective-permute-start.10 = (f32[256,256]{1,0:T(8,128)S(1)}, f32[256,256]{1,0:T(8,128)S(1)}, u32[]{:S(2)}, u32[]{:S(2)}) collective-permute-start(f32[256,256]{1,0:T(8,128)S(1)} %get-tuple-element.26.refs_1_), channel_id=1, source_target_pairs={{0,1},{1,0},{2,3},{3,2},{4,5},{5,4},{6,7},{7,6},{8,9},{9,8},{10,11... | collective-permute-start | bytes 786440 | tf_op jit(solution)/shard_map/ppermute | solution.py:293
  27.1 1.4 %collective-permute-start.9 = (f32[96,256]{1,0:T(8,128)S(1)}, f32[96,256]{1,0:T(8,128)S(1)}, u32[]{:S(2)}, u32[]{:S(2)}) collective-permute-start(f32[96,256]{1,0:T(8,128)S(1)} %shard_map.44), channel_id=1, source_target_pairs={{0,1},{1,0},{2,26},{3,27},{4,28},{5,29},{6,7},{7,6},{8,9},{9,8},{1... | collective-permute-start | bytes 294920 | tf_op jit(solution)/shard_map/ppermute | solution.py:293
  27.1 1.4 %collective-permute-start.8 = (f32[96,256]{1,0:T(8,128)S(1)}, f32[96,256]{1,0:T(8,128)S(1)}, u32[]{:S(2)}, u32[]{:S(2)}) collective-permute-start(f32[96,256]{1,0:T(8,128)S(1)} %shard_map.44), channel_id=1, source_target_pairs={{0,1},{1,0},{2,18},{3,19},{4,20},{5,21},{6,7},{7,6},{8,9},{9,8},{1... | collective-permute-start | bytes 294920 | tf_op jit(solution)/shard_map/ppermute | solution.py:293
  29.4 11.2 %collective-permute-start.11 = (f32[96,256]{1,0:T(8,128)S(1)}, f32[96,256]{1,0:T(8,128)S(1)}, u32[]{:S(2)}, u32[]{:S(2)}) collective-permute-start(f32[96,256]{1,0:T(8,128)S(1)} %get-tuple-element.30), channel_id=1, source_target_pairs={{2,0},{3,1},{4,6},{5,7},{0,2},{1,3},{6,4},{7,5},{10,8},{11,9},{12,... | collective-permute-start | bytes 294920 | tf_op jit(solution)/shard_map/ppermute | solution.py:354
  38.5 5.6 %collective-permute-start.12 = (f32[96,256]{1,0:T(8,128)S(1)}, f32[96,256]{1,0:T(8,128)S(1)}, u32[]{:S(2)}, u32[]{:S(2)}) collective-permute-start(f32[96,256]{1,0:T(8,128)S(1)} %get-tuple-element.31), channel_id=1, source_target_pairs={{2,6},{3,7},{4,0},{5,1},{0,2},{1,3},{6,4},{7,5},{10,14},{11,15},{1... | collective-permute-start | bytes 294920 | tf_op jit(solution)/shard_map/ppermute | solution.py:354
  38.5 7.4 %collective-permute-start.13 = (f32[96,256]{1,0:T(8,128)S(1)}, f32[96,256]{1,0:T(8,128)S(1)}, u32[]{:S(2)}, u32[]{:S(2)}) collective-permute-start(f32[96,256]{1,0:T(8,128)S(1)} %get-tuple-element.32), channel_id=1, source_target_pairs={{2,4},{3,5},{4,2},{5,3},{0,1},{1,0},{6,7},{7,6},{10,12},{11,13},{1... | collective-permute-start | bytes 294920 | tf_op jit(solution)/shard_map/ppermute | solution.py:354
  40.5 5.5 %collective-permute-start.14 = (f32[96,256]{1,0:T(8,128)S(1)}, f32[96,256]{1,0:T(8,128)S(1)}, u32[]{:S(2)}, u32[]{:S(2)}) collective-permute-start(f32[96,256]{1,0:T(8,128)S(1)} %get-tuple-element.29.refs_0_), channel_id=1, source_target_pairs={{0,1},{1,0},{2,3},{3,2},{4,5},{5,4},{6,7},{7,6},{8,9},{9,8},{10,11... | collective-permute-start | bytes 294920 | tf_op jit(solution)/shard_map/ppermute | solution.py:285
  40.5 5.5 %collective-permute-start.15 = (f32[96,256]{1,0:T(8,128)S(1)}, f32[96,256]{1,0:T(8,128)S(1)}, u32[]{:S(2)}, u32[]{:S(2)}) collective-permute-start(f32[96,256]{1,0:T(8,128)S(1)} %collective-permute-done.11.refs_1_), channel_id=1, source_target_pairs={{0,1},{1,0},{2,3},{3,2},{4,5},{5,4},{6,7},{7,6},{8,9},{9,8},{10,11... | collective-permute-start | bytes 294920 | tf_op jit(solution)/shard_map/ppermute | solution.py:285
  44.1 2.8 %collective-permute-start.16 = (f32[96,256]{1,0:T(8,128)S(1)}, f32[96,256]{1,0:T(8,128)S(1)}, u32[]{:S(2)}, u32[]{:S(2)}) collective-permute-start(f32[96,256]{1,0:T(8,128)S(1)} %collective-permute-done.12.refs_2_), channel_id=1, source_target_pairs={{0,1},{1,0},{2,3},{3,2},{4,5},{5,4},{6,7},{7,6},{8,9},{9,8},{10,11... | collective-permute-start | bytes 294920 | tf_op jit(solution)/shard_map/ppermute | solution.py:285
  46.0 1.3 %collective-permute-start.17 = (f32[96,256]{1,0:T(8,128)S(1)}, f32[96,256]{1,0:T(8,128)S(1)}, u32[]{:S(2)}, u32[]{:S(2)}) collective-permute-start(f32[96,256]{1,0:T(8,128)S(1)} %collective-permute-done.13.refs_3_), channel_id=1, source_target_pairs={{0,1},{1,0},{2,3},{3,2},{4,5},{5,4},{6,7},{7,6},{8,9},{9,8},{10,11... | collective-permute-start | bytes 294920 | tf_op jit(solution)/shard_map/ppermute | solution.py:285

commit v3 on v2

v3 whole, which is shorter than its diff:
```python
import functools

import jax
import jax.numpy as jnp
from jax import lax
from jax.experimental import pallas as pl
from jax.experimental.pallas import tpu as pltpu
from jax.sharding import PartitionSpec as P

F32 = jnp.float32
BF16 = jnp.bfloat16
NN = (((1,), (0,)), ((), ()))
VMEM = pl.BlockSpec(memory_space=pltpu.VMEM)
HBM = pl.BlockSpec(memory_space=pltpu.HBM)
SHADOW = 3_000_000_000


def split(value):
    high = value.astype(BF16)
    return high, (value - high.astype(F32)).astype(BF16)


def product(left, right):
    dot = functools.partial(lax.dot_general, dimension_numbers=NN, preferred_element_type=F32)
    return dot(left[0], right[0]) + (dot(left[0], right[1]) + dot(left[1], right[0]))


def call(kernel, outs, scratch=(), spec=VMEM, out_spec=VMEM, cost=0):
    shapes = [out if isinstance(out, jax.ShapeDtypeStruct) else jax.ShapeDtypeStruct(out, F32) for out in outs]

    def run(*args):
        specs = spec if isinstance(spec, list) else [spec] * len(args)
        return pl.pallas_call(
            kernel,
            in_specs=specs,
            out_specs=[out_spec] * len(outs),
            out_shape=shapes,
            scratch_shapes=list(scratch),
            cost_estimate=pl.CostEstimate(flops=cost, bytes_accessed=0, transcendentals=0) if cost else None,
            compiler_params=pltpu.CompilerParams(vmem_limit_bytes=32 * 1024 * 1024),
        )(*args)

    return run


def halved(*shape):
    return jax.ShapeDtypeStruct(shape, BF16)


def put(ref, value, *at):
    ref[*at, 0], ref[*at, 1] = split(value)


def get(ref, *at):
    return ref[*at, 0], ref[*at, 1]


def where():
    place = lax.axis_index("ry")
    return lax.axis_index("rx"), place // 2, place % 2


def rows(start, size):
    return pl.ds(pl.multiple_of(start, 8), size)


def local_kernel(a_ref, f_ref, own_ref, first_ref, rest_ref, sems):
    n, b = a_ref.shape[:2]
    copies = []
    for i in range(n):
        to = first_ref if i == 0 else rest_ref.at[i - 1]
        copies.append(
            (
                pltpu.make_async_copy(a_ref.at[i], to.at[:, pl.ds(0, b)], sems.at[i, 0]),
                pltpu.make_async_copy(f_ref.at[i], to.at[:, pl.ds(b, f_ref.shape[2])], sems.at[i, 1]),
            )
        )
    for part in range(2):
        for i in range(n):
            copies[i][part].start()
    copies[0][0].wait()
    total = first_ref[:, :b]
    steps = []
    for i in range(1, n):
        copies[i][0].wait()
        steps.append(split(rest_ref[i - 1, :, :b]))
        total = product(steps[-1], split(total))
    own_ref[:, :b] = total
    copies[0][1].wait()
    total = first_ref[:, b:]
    for i in range(1, n):
        copies[i][1].wait()
        total = product(steps[i - 1], split(total)) + rest_ref[i - 1, :, b:]
    own_ref[:, b:] = total


def chip_kernel(heads, own_ref, other_ref, map_ref, *refs):
    outs, state_ref = refs[:-1], refs[-1]
    _, z, core = where()
    b = own_ref.shape[0]
    part = outs[0].shape[0] - b // 2

    def combine(earlier_ref, later_ref):
        later = split(later_ref[:, :b])
        map_ref[...] = product(later, split(earlier_ref[:, :b])).T
        state_ref[...] = (product(later, split(earlier_ref[:, b:])) + later_ref[:, b:]).T

    @pl.when(core == 0)
    def _():
        combine(own_ref, other_ref)

    @pl.when(core == 1)
    def _():
        combine(other_ref, own_ref)

    for d, out in enumerate(outs):
        for j, head in enumerate(heads):

            @pl.when(z ^ d == head)
            def _():
                out[: b // 2] = map_ref[rows(core * (b // 2), b // 2)]
                out[b // 2 :] = state_ref[rows((2 * j + core) * part, part)]


def on_head(heads, body):
    pl.when(functools.reduce(jnp.logical_or, [where()[1] == head for head in heads]))(body)


def line_state_kernel(heads, chips, *refs):
    map_ref, ins, others = refs[0], refs[1 : 1 + chips], refs[1 + chips : 2 * chips]
    steps_ref, pre_ref, total_ref, all_ref = refs[2 * chips :]
    _, z, core = where()
    half = map_ref.shape[0] // 2

    def body():
        all_ref[z] = map_ref[...]
        for d in range(chips):
            pre_ref[z ^ d] = ins[d][half:]
            if d:
                all_ref[z ^ d, rows(core * half, half)] = ins[d][:half]
                all_ref[z ^ d, rows(half - core * half, half)] = others[d - 1][:half]
        total = pre_ref[0]
        for c in range(1, chips):
            here = pre_ref[c]
            pre_ref[c] = total
            put(steps_ref, all_ref[c], c)
            total = product(split(total), get(steps_ref, c)) + here
        total_ref[...] = total
        put(steps_ref, all_ref[0], 0)

    on_head(heads, body)


def line_map_kernel(heads, chips, steps_ref, pre_ref, total_ref):
    def body():
        pre_ref[1] = steps_ref[0]
        for c in range(1, chips):
            total = product(get(pre_ref, c), get(steps_ref, c))
            put(pre_ref, total, (c + 1) % chips)
        total_ref[...] = total

    if chips > 1:
        on_head(heads, body)
    else:
        pre_ref[...] = steps_ref[...]
        total_ref[...] = steps_ref[0, 0].astype(F32) + steps_ref[0, 1].astype(F32)


def total_kernel(with_map, *refs):
    *preP, preF_ref, line_ref, f_ref = refs[: 3 + with_map]
    outs = refs[3 + with_map :]
    step = get(line_ref, 0)
    outs[0][...] = product(split(preF_ref[...]), step) + f_ref[...]
    if with_map:
        outs[1][...] = product(split(preP[0][...]), step)


def choose(refs, width, out_ref):
    for j, ref in enumerate(refs):

        @pl.when(where()[0] % width == j)
        def _():
            out_ref[...] = ref[...]


def prefix_map_kernel(width, *refs):
    *maps, pre_ref, out_ref = refs
    g = where()[0]

    @pl.when(g // width % 2 == 0)
    def _():
        out_ref[...] = pre_ref[...]

    @pl.when(g // width % 2 == 1)
    def _():
        choose(maps, width, out_ref)

        @pl.when(g % width != 0)
        def _():
            out_ref[...] = product(split(out_ref[...]), split(pre_ref[...]))


def advance(width, states, pre, out_ref):
    g = where()[0]

    @pl.when(g // width % 2 == 1)
    def _():
        choose(states, width, out_ref)
        if pre:

            @pl.when(g % width != 0)
            def _():
                out_ref[...] = product(split(out_ref[...]), split(pre[0][...])) + pre[1][...]

    if pre:

        @pl.when(g // width % 2 == 0)
        def _():
            out_ref[...] = pre[1][...]


def prefix_state_kernel(width, count, *refs):
    advance(width, refs[:count], refs[count:-1], refs[-1])


def start_kernel(width, count, with_pre, ds, *refs):
    states, refs = refs[:count], refs[count:]
    pre, refs = refs[: 2 * with_pre], refs[2 * with_pre :]
    lineP_ref, lineF_ref, start_ref, *outs = refs
    if count:
        advance(width, states, pre, start_ref)

    @pl.when(where()[0] == 0)
    def _():
        start_ref[...] = jnp.zeros_like(start_ref)

    enter_kernel(ds, start_ref, lineP_ref, lineF_ref, *outs)


def enter_kernel(ds, start_ref, lineP_ref, lineF_ref, *outs):
    start = split(start_ref[...])
    for d, out in zip(ds, outs, strict=True):
        c = where()[1] ^ d

        @pl.when(c == 0)
        def _():
            out[...] = start_ref[...]

        @pl.when(c != 0)
        def _():
            out[...] = product(start, get(lineP_ref, c)) + lineF_ref[c]


def prepare_kernel(other_ref, first_ref, rest_ref, m_ref, c_ref, now_ref):
    core = where()[2]
    n, b = c_ref.shape[:2]

    @pl.when(core == 0)
    def _():
        now_ref[...] = first_ref[...]

    @pl.when(core == 1)
    def _():
        step = split(first_ref[:, :b])
        now_ref[:, :b] = product(step, split(other_ref[:, :b]))
        now_ref[:, b:] = product(step, split(other_ref[:, b:])) + first_ref[:, b:]

    for i in range(n):
        now = split(now_ref[...])
        m_ref[i, 0], m_ref[i, 1] = now[0][:, :b], now[1][:, :b]
        c_ref[i] = now_ref[:, b:]
        if i < n - 1:
            later = product(split(rest_ref[i, :, :b]), now)
            now_ref[:, :b] = later[:, :b]
            now_ref[:, b:] = later[:, b:] + rest_ref[i, :, b:]


def follow_kernel(m_ref, c_ref, next_ref, out_ref, add_ref):
    n, b = c_ref.shape[:2]
    step = split(next_ref[:, :b])
    put(out_ref, product(step, get(m_ref, n - 1)))
    add_ref[...] = product(step, split(c_ref[n - 1])) + next_ref[:, b:]


def run_kernel(heads, count, *refs):
    parts, shared = refs[:count], refs[count : 2 * count]
    m_ref, c_ref, next_ref, add_ref, x_ref, s_ref, in_ref, xs_ref, ss_ref, sems = refs[2 * count :]
    g, z, core = where()
    n = x_ref.shape[0]
    part = parts[0].shape[0]
    for d in range(count):
        for j, head in enumerate(heads):

            @pl.when(z ^ d == head)
            def _():
                in_ref[rows((2 * j + core) * part, part)] = parts[d][...]
                in_ref[rows((2 * j + 1 - core) * part, part)] = shared[d][...]

    entering = split(in_ref[...].T)
    copies = [pltpu.make_async_copy(xs_ref.at[i], x_ref.at[i], sems.at[0, i]) for i in range(n)]
    copies += [pltpu.make_async_copy(ss_ref.at[i], s_ref.at[i], sems.at[1, i]) for i in range(n)]
    for i in range(n):
        xs_ref[i] = product(get(m_ref, i), entering) + c_ref[i]
        copies[i].start()
        if i:
            ss_ref[i - 1] = xs_ref[i] - xs_ref[i - 1]
            copies[n + i - 1].start()
    ss_ref[n - 1] = product(get(next_ref), entering) + add_ref[...] - xs_ref[n - 1]

    @pl.when(g * lax.axis_size("ry") + 2 * z + core == lax.axis_size("rx") * lax.axis_size("ry") - 1)
    def _():
        ss_ref[n - 1] = -xs_ref[n - 1]

    copies[2 * n - 1].start()
    for copy in copies:
        copy.wait()


def filled(useful, chips):
    sources = [c for c in range(chips) if all(c != s for s, _ in useful)]
    targets = [c for c in range(chips) if all(c != t for _, t in useful)]
    pairs = []
    for s, t in [*useful, *zip(sources, targets, strict=True)]:
        pairs += [(2 * s + core, 2 * t + (core ^ (s == t))) for core in range(2)]
    return pairs


def on_device(propagator, forcing):
    intervals, b, r = forcing.shape
    lines, places = lax.axis_size("rx"), lax.axis_size("ry")
    chips, devices = places // 2, lines * places
    heads = sorted({max(chips // 2 - 1, 0), chips // 2})
    part = r // (2 * len(heads))

    def swap(value):
        return lax.ppermute(value, "ry", [(i, i ^ 1) for i in range(places)])

    def to_heads(value, d):
        return lax.ppermute(value, "ry", filled([(h ^ d, h) for h in heads], chips))

    def from_heads(value, d):
        return lax.ppermute(value, "ry", filled([(h, h ^ d) for h in heads], chips))

    def hops(value, width, start=0):
        out = []
        for j in range(width):
            to = {}
            for block in range(start, lines, 2 * width):
                source, target = block + width - 1, block + width + j
                back = block + j
                to[source], to[target], to[back] = target, back, source
                if back == source:
                    to[source] = target
            pairs = []
            for g in range(lines):
                for i in range(places):
                    at = to.get(g) if i // 2 in heads else None
                    pairs.append((g * places + i, g * places + (i ^ 1) if at is None else at * places + i))
            out.append(lax.ppermute(value, ("rx", "ry"), pairs))
        return out

    propagator, forcing = (pltpu.with_memory_space_constraint(a, pltpu.HBM) for a in (propagator, forcing))
    own, first, rest = call(
        local_kernel,
        [(b, b + r), (b, b + r), (max(intervals - 1, 1), b, b + r)],
        [pltpu.SemaphoreType.DMA((intervals, 2))],
        spec=HBM,
    )(propagator, forcing)
    other = swap(own)
    chip_map, *cuts = call(
        functools.partial(chip_kernel, heads),
        [(b, b)] + [(b // 2 + part, b)] * chips,
        [pltpu.VMEM((r, b), F32)],
    )(own, other)
    gathered = [to_heads(cuts[d], d) for d in range(1, chips)]
    early, _ = lax.optimization_barrier((first, cuts))
    matrices, constants = call(
        prepare_kernel,
        [halved(intervals, 2, b, b), (intervals, b, r)],
        [pltpu.VMEM((b, b + r), F32)],
        cost=SHADOW,
    )(other, early, rest)
    for d in range(chips - 1):
        gathered[d], _ = lax.optimization_barrier((gathered[d], constants))
    swapped = [swap(value) for value in gathered]
    steps, lineF, line_state = call(
        functools.partial(line_state_kernel, heads, chips),
        [halved(chips, 2, b, b), (chips, part, b), (part, b)],
        [pltpu.VMEM((chips, b, b), F32)],
    )(chip_map, cuts[0], *gathered, *swapped)
    lineP, line_map = call(
        functools.partial(line_map_kernel, heads, chips), [halved(chips, 2, b, b), (b, b)], cost=SHADOW
    )(steps)

    def carried(value, width, pre):
        maps = hops(value, width, 2 * width)
        if width == 1:
            return maps
        return call(functools.partial(prefix_map_kernel, width), [(b, b)])(*maps, *pre)

    total_map, total_state, pre_map, pre_state = line_map, line_state, [], None
    width, states = 1, []
    while width < lines:
        last = 2 * width >= lines
        if width > 1:
            total_state, *more = call(
                functools.partial(total_kernel, not last), [(part, b)] + [(b, b)] * (not last), cost=SHADOW
            )(*pre_map * (not last), pre_state, lineP, line_state)
            total_map = more and more[0]
        states = hops(total_state, width)
        if last:
            break
        pre_map = carried(total_map, width, pre_map)
        if width == 1:
            pre_state = states[0]
        else:
            (pre_state,) = call(functools.partial(prefix_state_kernel, width, width), [(part, b)])(
                *states, *pre_map, pre_state
            )
        width *= 2
    pre = [] if pre_state is None else [*pre_map, pre_state]
    first_late, _ = lax.optimization_barrier((first, line_state))
    following = lax.ppermute(first_late, ("rx", "ry"), [(i, (i - 1) % devices) for i in range(devices)])
    near, far = range(max(chips // 2, 1)), range(max(chips // 2, 1), chips)
    start, *later = call(
        functools.partial(start_kernel, width, len(states), bool(pre), far), [(part, b)] * (1 + len(far))
    )(*states, *pre, lineP, lineF)
    entering = call(functools.partial(enter_kernel, near), [(part, b)] * len(near), cost=SHADOW)(start, lineP, lineF)
    entering = [*entering, *later]
    parts = [entering[0]] + [from_heads(entering[d], d) for d in range(1, chips)]
    following, _ = lax.optimization_barrier((following, start))
    next_matrix, next_constant = call(follow_kernel, [halved(2, b, b), (b, r)], cost=SHADOW)(
        matrices, constants, following
    )
    for d in range(1, chips):
        parts[d], _ = lax.optimization_barrier((parts[d], next_constant))
    return tuple(
        call(
            functools.partial(run_kernel, heads, chips),
            [(intervals, b, r)] * 2,
            [
                pltpu.VMEM((r, b), F32),
                pltpu.VMEM((intervals, b, r), F32),
                pltpu.VMEM((intervals, b, r), F32),
                pltpu.SemaphoreType.DMA((2, intervals)),
            ],
            out_spec=HBM,
        )(*parts, *[swap(value) for value in parts], matrices, constants, next_matrix, next_constant)
    )


def solution(mesh):
    spec = P(("rx", "ry"), None, None)
    return jax.shard_map(
        on_device, mesh=mesh, in_specs=(spec, spec), out_specs=(spec, spec), check_vma=False
    )
```

time: 49.8 us -> 46.2 us (0.928)
  the two profiles are of different devices: /device:TPU:1 before, /device:TPU:0 now
where the time goes in v3:
time: 46.2 us; the launch traced here: 46 us
  starting transfers between devices  22.3 us (48%)
  waiting for transfers between devices  16.8 us (36%)
  Pallas kernels  6.2 us (13%)
  between operations  0.72 us (2%)
    ppermute x3, starting transfers between devices, from_heads(): return lax.ppermute(value, 'ry', filled([(h, h ^ d) for h in heads], chips))  8.67 us
    ppermute x3, waiting for transfers between devices, to_heads(): return lax.ppermute(value, 'ry', filled([(h ^ d, h) for h in heads], chips))  7.68 us
    pallas_call x10, Pallas kernels, run(): pl.pallas_call(kernel, in_specs=specs, out_specs=[out_spec] * len(outs),...  6.2 us
    ppermute x3, starting transfers between devices, to_heads(): return lax.ppermute(value, 'ry', filled([(h ^ d, h) for h in heads], chips))  5.6 us
    ppermute x1, starting transfers between devices, on_device(): lax.ppermute(first_late, ('rx', 'ry'), [(i, (i - 1) % devices) for i in r...  5.44 us
    ppermute x8, waiting for transfers between devices, swap(): return lax.ppermute(value, 'ry', [(i, i ^ 1) for i in range(places)])  4.32 us
    ppermute x3, waiting for transfers between devices, from_heads(): return lax.ppermute(value, 'ry', filled([(h, h ^ d) for h in heads], chips))  3.81 us
    ppermute x8, starting transfers between devices, swap(): return lax.ppermute(value, 'ry', [(i, i ^ 1) for i in range(places)])  1.55 us
  transfers between devices with their start and end apart: 19, of which 12 were waited for; matrix products, arithmetic and copies ran while one was open for 0% of the time, Pallas kernels for 4%

profile of v3, /device:TPU:0, one launch (start us, length us, event | category | flops | bytes accessed | tf_op | source)
XLA Modules:
  0.0 46.0 jit_solution(9781636671064140012)
XLA Ops:
  0.6 1.8 %shard_map.41 = (f32[256,640]{1,0:T(8,128)S(1)}, f32[256,640]{1,0:T(8,128)S(1)}, f32[1,256,640]{2,1,0:T(8,128)S(1)}) custom-call(f32[2,256,256]{2,1,0:T(8,128)} %a_ref.1, f32[2,256,384]{2,1,0:T(8,128)} %f_ref.1), custom_call_target="tpu_custom_call" | custom-call | tf_op jit(solution)/shard_map/pallas_call | solution.py:33
  2.5 0.5 %collective-permute-start = (f32[256,640]{1,0:T(8,128)S(1)}, f32[256,640]{1,0:T(8,128)S(1)}, u32[]{:S(2)}, u32[]{:S(2)}) collective-permute-start(f32[256,640]{1,0:T(8,128)S(1)} %get-tuple-element.33.own_ref), channel_id=1, source_target_pairs={{0,1},{1,0},{2,3},{3,2},{4,5},{5,4},{6,7},{7,6},{8,9},{9,8},{10,11... | collective-permute-start | bytes 1966088 | tf_op jit(solution)/shard_map/ppermute | solution.py:336
  3.0 1.7 %collective-permute-done.other_ref = f32[256,640]{1,0:T(8,128)S(1)} collective-permute-done((f32[256,640]{1,0:T(8,128)S(1)}, f32[256,640]{1,0:T(8,128)S(1)}, u32[]{:S(2)}, u32[]{:S(2)}) %collective-permute-start) | collective-permute-done | bytes 655392 | tf_op jit(solution)/shard_map/ppermute | solution.py:336
  4.7 0.7 %shard_map.42 = (f32[256,256]{1,0:T(8,128)S(1)}, f32[224,256]{1,0:T(8,128)S(1)}, f32[224,256]{1,0:T(8,128)S(1)}, f32[224,256]{1,0:T(8,128)S(1)}, f32[224,256]{1,0:T(8,128)S(1)}) custom-call(f32[256,640]{1,0:T(8,128)S(1)} %get-tuple-element.33.own_ref, f32[256,640]{1,0:T(8,128)S(1)} %collective-permute-done.other_ref), custom_call_target="tpu_custom_call" | custom-call | tf_op jit(solution)/shard_map/pallas_call | solution.py:33
  5.4 3.0 %collective-permute-start.1 = (f32[224,256]{1,0:T(8,128)S(1)}, f32[224,256]{1,0:T(8,128)S(1)}, u32[]{:S(2)}, u32[]{:S(2)}) collective-permute-start(f32[224,256]{1,0:T(8,128)S(1)} %get-tuple-element.36), channel_id=1, source_target_pairs={{0,2},{1,3},{6,4},{7,5},{2,0},{3,1},{4,6},{5,7},{8,10},{9,11},{14,... | collective-permute-start | bytes 688136 | tf_op jit(solution)/shard_map/ppermute | solution.py:339
  8.4 2.6 %collective-permute-start.2 = (f32[224,256]{1,0:T(8,128)S(1)}, f32[224,256]{1,0:T(8,128)S(1)}, u32[]{:S(2)}, u32[]{:S(2)}) collective-permute-start(f32[224,256]{1,0:T(8,128)S(1)} %get-tuple-element.38), channel_id=1, source_target_pairs={{6,2},{7,3},{0,4},{1,5},{2,0},{3,1},{4,6},{5,7},{14,10},{15,11},{8... | collective-permute-start | bytes 688136 | tf_op jit(solution)/shard_map/ppermute | solution.py:339
  11.0 0.5 %shard_map.43 = (bf16[2,2,256,256]{3,2,1,0:T(8,128)(2,1)S(1)}, f32[2,256,384]{2,1,0:T(8,128)S(1)}) custom-call(f32[256,640]{1,0:T(8,128)S(1)} %collective-permute-done.other_ref, f32[256,640]{1,0:T(8,128)S(1)} %get-tuple-element.55.first_ref, f32[1,256,640]{2,1,0:T(8,128)S(1)} %get-tuple-element.41.rest_ref), custom_call_target="tpu_custom_call" | custom-call | flops 3000000000 | tf_op jit(solution)/shard_map/pallas_call | solution.py:33
  11.5 3.3 %collective-permute-done.1.refs_2_ = f32[224,256]{1,0:T(8,128)S(1)} collective-permute-done((f32[224,256]{1,0:T(8,128)S(1)}, f32[224,256]{1,0:T(8,128)S(1)}, u32[]{:S(2)}, u32[]{:S(2)}) %collective-permute-start.1) | collective-permute-done | bytes 229408 | tf_op jit(solution)/shard_map/ppermute | solution.py:339
  14.8 4.4 %collective-permute-done.2.refs_3_ = f32[224,256]{1,0:T(8,128)S(1)} collective-permute-done((f32[224,256]{1,0:T(8,128)S(1)}, f32[224,256]{1,0:T(8,128)S(1)}, u32[]{:S(2)}, u32[]{:S(2)}) %collective-permute-start.2) | collective-permute-done | bytes 229408 | tf_op jit(solution)/shard_map/ppermute | solution.py:339
  19.2 0.5 %collective-permute-start.6 = (f32[224,256]{1,0:T(8,128)S(1)}, f32[224,256]{1,0:T(8,128)S(1)}, u32[]{:S(2)}, u32[]{:S(2)}) collective-permute-start(f32[224,256]{1,0:T(8,128)S(1)} %collective-permute-done.3.refs_4_), channel_id=1, source_target_pairs={{0,1},{1,0},{2,3},{3,2},{4,5},{5,4},{6,7},{7,6},{8,9},{9,8},{10,11... | collective-permute-start | bytes 688136 | tf_op jit(solution)/shard_map/ppermute | solution.py:336
  19.7 1.0 %collective-permute-done.5.refs_6_ = f32[224,256]{1,0:T(8,128)S(1)} collective-permute-done((f32[224,256]{1,0:T(8,128)S(1)}, f32[224,256]{1,0:T(8,128)S(1)}, u32[]{:S(2)}, u32[]{:S(2)}) %collective-permute-start.5) | collective-permute-done | bytes 229408 | tf_op jit(solution)/shard_map/ppermute | solution.py:336
  21.5 5.4 %collective-permute-start.12 = (f32[256,640]{1,0:T(8,128)S(1)}, f32[256,640]{1,0:T(8,128)S(1)}, u32[]{:S(2)}, u32[]{:S(2)}) collective-permute-start(f32[256,640]{1,0:T(8,128)S(1)} %get-tuple-element.55.first_ref), channel_id=1, source_target_pairs={{0,31},{1,0},{2,1},{3,2},{4,3},{5,4},{6,5},{7,6},{8,7},{9,8},{10,9... | collective-permute-start | bytes 1966088 | tf_op jit(solution)/shard_map/ppermute | solution.py:423
  27.3 0.5 %collective-permute-start.8 = (f32[96,256]{1,0:T(8,128)S(1)}, f32[96,256]{1,0:T(8,128)S(1)}, u32[]{:S(2)}, u32[]{:S(2)}) collective-permute-start(f32[96,256]{1,0:T(8,128)S(1)} %shard_map.46), channel_id=1, source_target_pairs={{0,1},{1,0},{2,10},{3,11},{4,12},{5,13},{6,7},{7,6},{8,9},{9,8},{1... | collective-permute-start | bytes 294920 | tf_op jit(solution)/shard_map/ppermute | solution.py:359
  27.8 0.8 %collective-permute-done.9.refs_1_ = f32[96,256]{1,0:T(8,128)S(1)} collective-permute-done((f32[96,256]{1,0:T(8,128)S(1)}, f32[96,256]{1,0:T(8,128)S(1)}, u32[]{:S(2)}, u32[]{:S(2)}) %collective-permute-start.9) | collective-permute-done | bytes 98336 | tf_op jit(solution)/shard_map/ppermute | solution.py:359
  28.7 0.4 shard_map.47
  29.2 7.1 %collective-permute-start.13 = (f32[96,256]{1,0:T(8,128)S(1)}, f32[96,256]{1,0:T(8,128)S(1)}, u32[]{:S(2)}, u32[]{:S(2)}) collective-permute-start(f32[96,256]{1,0:T(8,128)S(1)} %get-tuple-element.59), channel_id=1, source_target_pairs={{2,6},{3,7},{4,0},{5,1},{0,2},{1,3},{6,4},{7,5},{10,14},{11,15},{1... | collective-permute-start | bytes 294920 | tf_op jit(solution)/shard_map/ppermute | solution.py:342
  36.6 1.5 %collective-permute-start.11 = (f32[96,256]{1,0:T(8,128)S(1)}, f32[96,256]{1,0:T(8,128)S(1)}, u32[]{:S(2)}, u32[]{:S(2)}) collective-permute-start(f32[96,256]{1,0:T(8,128)S(1)} %get-tuple-element.53), channel_id=1, source_target_pairs={{2,0},{3,1},{4,6},{5,7},{0,2},{1,3},{6,4},{7,5},{10,8},{11,9},{12,... | collective-permute-start | bytes 294920 | tf_op jit(solution)/shard_map/ppermute | solution.py:342
  38.1 0.5 %shard_map.49 = (bf16[2,256,256]{2,1,0:T(8,128)(2,1)S(1)}, f32[256,384]{1,0:T(8,128)S(1)}) custom-call(bf16[2,2,256,256]{3,2,1,0:T(8,128)(2,1)S(1)} %get-tuple-element.54.m_ref.refs_8_, f32[2,256,384]{2,1,0:T(8,128)S(1)} %get-tuple-element.42.c_ref.refs_9_, f32[256,640]{1,0:T(8,128)S(1)} %collective-permute-done.12.next_ref), custom_call_target="tpu_custom_call" | custom-call | flops 3000000000 | tf_op jit(solution)/shard_map/pallas_call | solution.py:33
  38.6 1.8 %collective-permute-done.13.refs_2_ = f32[96,256]{1,0:T(8,128)S(1)} collective-permute-done((f32[96,256]{1,0:T(8,128)S(1)}, f32[96,256]{1,0:T(8,128)S(1)}, u32[]{:S(2)}, u32[]{:S(2)}) %collective-permute-start.13) | collective-permute-done | bytes 98336 | tf_op jit(solution)/shard_map/ppermute | solution.py:342
  40.4 2.0 %collective-permute-done.11.refs_1_ = f32[96,256]{1,0:T(8,128)S(1)} collective-permute-done((f32[96,256]{1,0:T(8,128)S(1)}, f32[96,256]{1,0:T(8,128)S(1)}, u32[]{:S(2)}, u32[]{:S(2)}) %collective-permute-start.11) | collective-permute-done | bytes 98336 | tf_op jit(solution)/shard_map/ppermute | solution.py:342
  42.4 0.5 %collective-permute-start.17 = (f32[96,256]{1,0:T(8,128)S(1)}, f32[96,256]{1,0:T(8,128)S(1)}, u32[]{:S(2)}, u32[]{:S(2)}) collective-permute-start(f32[96,256]{1,0:T(8,128)S(1)} %collective-permute-done.13.refs_2_), channel_id=1, source_target_pairs={{0,1},{1,0},{2,3},{3,2},{4,5},{5,4},{6,7},{7,6},{8,9},{9,8},{10,11... | collective-permute-start | bytes 294920 | tf_op jit(solution)/shard_map/ppermute | solution.py:336
  42.9 0.8 %collective-permute-done.16.refs_5_ = f32[96,256]{1,0:T(8,128)S(1)} collective-permute-done((f32[96,256]{1,0:T(8,128)S(1)}, f32[96,256]{1,0:T(8,128)S(1)}, u32[]{:S(2)}, u32[]{:S(2)}) %collective-permute-start.16) | collective-permute-done | bytes 98336 | tf_op jit(solution)/shard_map/ppermute | solution.py:336
  43.9 0.4 collective-permute-done.18.refs_7_
  44.2 1.8 %shard_map.50 = (f32[2,256,384]{2,1,0:T(8,128)}, f32[2,256,384]{2,1,0:T(8,128)}) custom-call(f32[96,256]{1,0:T(8,128)S(1)} %get-tuple-element.52.refs_0_, f32[96,256]{1,0:T(8,128)S(1)} %collective-permute-done.11.refs_1_, f32[96,256]{1,0:T(8,128)S(1)} %collective-permute-done.13.refs_2_, f32[96,256]{1,0:T(8,128)S(1)} %collective-permute-done.14.refs_3_, ...), custom_call_target="tpu_custom_call" | custom-call | tf_op jit(solution)/shard_map/pallas_call | solution.py:33
  (24 shorter events, 1.7 us)
Async XLA Ops:
  2.5 2.2 %collective-permute-start = (f32[256,640]{1,0:T(8,128)S(1)}, f32[256,640]{1,0:T(8,128)S(1)}, u32[]{:S(2)}, u32[]{:S(2)}) collective-permute-start(f32[256,640]{1,0:T(8,128)S(1)} %get-tuple-element.33.own_ref), channel_id=1, source_target_pairs={{0,1},{1,0},{2,3},{3,2},{4,5},{5,4},{6,7},{7,6},{8,9},{9,8},{10,11... | collective-permute-start | bytes 1966088 | tf_op jit(solution)/shard_map/ppermute | solution.py:336
  5.4 9.4 %collective-permute-start.1 = (f32[224,256]{1,0:T(8,128)S(1)}, f32[224,256]{1,0:T(8,128)S(1)}, u32[]{:S(2)}, u32[]{:S(2)}) collective-permute-start(f32[224,256]{1,0:T(8,128)S(1)} %get-tuple-element.36), channel_id=1, source_target_pairs={{0,2},{1,3},{6,4},{7,5},{2,0},{3,1},{4,6},{5,7},{8,10},{9,11},{14,... | collective-permute-start | bytes 688136 | tf_op jit(solution)/shard_map/ppermute | solution.py:339
  8.4 10.8 %collective-permute-start.2 = (f32[224,256]{1,0:T(8,128)S(1)}, f32[224,256]{1,0:T(8,128)S(1)}, u32[]{:S(2)}, u32[]{:S(2)}) collective-permute-start(f32[224,256]{1,0:T(8,128)S(1)} %get-tuple-element.38), channel_id=1, source_target_pairs={{6,2},{7,3},{0,4},{1,5},{2,0},{3,1},{4,6},{5,7},{14,10},{15,11},{8... | collective-permute-start | bytes 688136 | tf_op jit(solution)/shard_map/ppermute | solution.py:339
  11.0 8.2 %collective-permute-start.3 = (f32[224,256]{1,0:T(8,128)S(1)}, f32[224,256]{1,0:T(8,128)S(1)}, u32[]{:S(2)}, u32[]{:S(2)}) collective-permute-start(f32[224,256]{1,0:T(8,128)S(1)} %get-tuple-element.39), channel_id=1, source_target_pairs={{4,2},{5,3},{2,4},{3,5},{0,1},{1,0},{6,7},{7,6},{12,10},{13,11},{1... | collective-permute-start | bytes 688136 | tf_op jit(solution)/shard_map/ppermute | solution.py:339
  14.8 4.9 %collective-permute-start.4 = (f32[224,256]{1,0:T(8,128)S(1)}, f32[224,256]{1,0:T(8,128)S(1)}, u32[]{:S(2)}, u32[]{:S(2)}) collective-permute-start(f32[224,256]{1,0:T(8,128)S(1)} %collective-permute-done.1.refs_2_), channel_id=1, source_target_pairs={{0,1},{1,0},{2,3},{3,2},{4,5},{5,4},{6,7},{7,6},{8,9},{9,8},{10,11... | collective-permute-start | bytes 688136 | tf_op jit(solution)/shard_map/ppermute | solution.py:336
  19.2 1.5 %collective-permute-start.5 = (f32[224,256]{1,0:T(8,128)S(1)}, f32[224,256]{1,0:T(8,128)S(1)}, u32[]{:S(2)}, u32[]{:S(2)}) collective-permute-start(f32[224,256]{1,0:T(8,128)S(1)} %collective-permute-done.2.refs_3_), channel_id=1, source_target_pairs={{0,1},{1,0},{2,3},{3,2},{4,5},{5,4},{6,7},{7,6},{8,9},{9,8},{10,11... | collective-permute-start | bytes 688136 | tf_op jit(solution)/shard_map/ppermute | solution.py:336
  19.2 1.8 %collective-permute-start.6 = (f32[224,256]{1,0:T(8,128)S(1)}, f32[224,256]{1,0:T(8,128)S(1)}, u32[]{:S(2)}, u32[]{:S(2)}) collective-permute-start(f32[224,256]{1,0:T(8,128)S(1)} %collective-permute-done.3.refs_4_), channel_id=1, source_target_pairs={{0,1},{1,0},{2,3},{3,2},{4,5},{5,4},{6,7},{7,6},{8,9},{9,8},{10,11... | collective-permute-start | bytes 688136 | tf_op jit(solution)/shard_map/ppermute | solution.py:336
  21.0 6.0 %collective-permute-start.7 = (f32[96,256]{1,0:T(8,128)S(1)}, f32[96,256]{1,0:T(8,128)S(1)}, u32[]{:S(2)}, u32[]{:S(2)}) collective-permute-start(f32[96,256]{1,0:T(8,128)S(1)} %get-tuple-element.46.refs_2_), channel_id=1, source_target_pairs={{0,1},{1,0},{2,10},{3,11},{4,12},{5,13},{6,7},{7,6},{8,9},{9,8},{1... | collective-permute-start | bytes 294920 | tf_op jit(solution)/shard_map/ppermute | solution.py:359
  21.2 7.5 %collective-permute-start.10 = (f32[256,256]{1,0:T(8,128)S(1)}, f32[256,256]{1,0:T(8,128)S(1)}, u32[]{:S(2)}, u32[]{:S(2)}) collective-permute-start(f32[256,256]{1,0:T(8,128)S(1)} %get-tuple-element.49), channel_id=1, source_target_pairs={{0,1},{1,0},{2,3},{3,2},{4,5},{5,4},{6,7},{7,6},{8,9},{9,8},{10,11... | collective-permute-start | bytes 786440 | tf_op jit(solution)/shard_map/ppermute | solution.py:359
  21.5 16.6 %collective-permute-start.12 = (f32[256,640]{1,0:T(8,128)S(1)}, f32[256,640]{1,0:T(8,128)S(1)}, u32[]{:S(2)}, u32[]{:S(2)}) collective-permute-start(f32[256,640]{1,0:T(8,128)S(1)} %get-tuple-element.55.first_ref), channel_id=1, source_target_pairs={{0,31},{1,0},{2,1},{3,2},{4,3},{5,4},{6,5},{7,6},{8,7},{9,8},{10,9... | collective-permute-start | bytes 1966088 | tf_op jit(solution)/shard_map/ppermute | solution.py:423
  27.2 1.4 %collective-permute-start.9 = (f32[96,256]{1,0:T(8,128)S(1)}, f32[96,256]{1,0:T(8,128)S(1)}, u32[]{:S(2)}, u32[]{:S(2)}) collective-permute-start(f32[96,256]{1,0:T(8,128)S(1)} %shard_map.46), channel_id=1, source_target_pairs={{0,1},{1,0},{2,3},{3,2},{4,5},{5,4},{6,7},{7,6},{8,9},{9,8},{10,26... | collective-permute-start | bytes 294920 | tf_op jit(solution)/shard_map/ppermute | solution.py:359
  27.3 1.4 %collective-permute-start.8 = (f32[96,256]{1,0:T(8,128)S(1)}, f32[96,256]{1,0:T(8,128)S(1)}, u32[]{:S(2)}, u32[]{:S(2)}) collective-permute-start(f32[96,256]{1,0:T(8,128)S(1)} %shard_map.46), channel_id=1, source_target_pairs={{0,1},{1,0},{2,10},{3,11},{4,12},{5,13},{6,7},{7,6},{8,9},{9,8},{1... | collective-permute-start | bytes 294920 | tf_op jit(solution)/shard_map/ppermute | solution.py:359
  29.2 11.2 %collective-permute-start.13 = (f32[96,256]{1,0:T(8,128)S(1)}, f32[96,256]{1,0:T(8,128)S(1)}, u32[]{:S(2)}, u32[]{:S(2)}) collective-permute-start(f32[96,256]{1,0:T(8,128)S(1)} %get-tuple-element.59), channel_id=1, source_target_pairs={{2,6},{3,7},{4,0},{5,1},{0,2},{1,3},{6,4},{7,5},{10,14},{11,15},{1... | collective-permute-start | bytes 294920 | tf_op jit(solution)/shard_map/ppermute | solution.py:342
  36.3 2.3 %collective-permute-start.14 = (f32[96,256]{1,0:T(8,128)S(1)}, f32[96,256]{1,0:T(8,128)S(1)}, u32[]{:S(2)}, u32[]{:S(2)}) collective-permute-start(f32[96,256]{1,0:T(8,128)S(1)} %get-tuple-element.61), channel_id=1, source_target_pairs={{2,4},{3,5},{4,2},{5,3},{0,1},{1,0},{6,7},{7,6},{10,12},{11,13},{1... | collective-permute-start | bytes 294920 | tf_op jit(solution)/shard_map/ppermute | solution.py:342
  36.6 5.8 %collective-permute-start.11 = (f32[96,256]{1,0:T(8,128)S(1)}, f32[96,256]{1,0:T(8,128)S(1)}, u32[]{:S(2)}, u32[]{:S(2)}) collective-permute-start(f32[96,256]{1,0:T(8,128)S(1)} %get-tuple-element.53), channel_id=1, source_target_pairs={{2,0},{3,1},{4,6},{5,7},{0,2},{1,3},{6,4},{7,5},{10,8},{11,9},{12,... | collective-permute-start | bytes 294920 | tf_op jit(solution)/shard_map/ppermute | solution.py:342
  38.1 4.8 %collective-permute-start.15 = (f32[96,256]{1,0:T(8,128)S(1)}, f32[96,256]{1,0:T(8,128)S(1)}, u32[]{:S(2)}, u32[]{:S(2)}) collective-permute-start(f32[96,256]{1,0:T(8,128)S(1)} %get-tuple-element.52.refs_0_), channel_id=1, source_target_pairs={{0,1},{1,0},{2,3},{3,2},{4,5},{5,4},{6,7},{7,6},{8,9},{9,8},{10,11... | collective-permute-start | bytes 294920 | tf_op jit(solution)/shard_map/ppermute | solution.py:336
  42.4 1.3 %collective-permute-start.16 = (f32[96,256]{1,0:T(8,128)S(1)}, f32[96,256]{1,0:T(8,128)S(1)}, u32[]{:S(2)}, u32[]{:S(2)}) collective-permute-start(f32[96,256]{1,0:T(8,128)S(1)} %collective-permute-done.11.refs_1_), channel_id=1, source_target_pairs={{0,1},{1,0},{2,3},{3,2},{4,5},{5,4},{6,7},{7,6},{8,9},{9,8},{10,11... | collective-permute-start | bytes 294920 | tf_op jit(solution)/shard_map/ppermute | solution.py:336
  42.4 1.5 %collective-permute-start.17 = (f32[96,256]{1,0:T(8,128)S(1)}, f32[96,256]{1,0:T(8,128)S(1)}, u32[]{:S(2)}, u32[]{:S(2)}) collective-permute-start(f32[96,256]{1,0:T(8,128)S(1)} %collective-permute-done.13.refs_2_), channel_id=1, source_target_pairs={{0,1},{1,0},{2,3},{3,2},{4,5},{5,4},{6,7},{7,6},{8,9},{9,8},{10,11... | collective-permute-start | bytes 294920 | tf_op jit(solution)/shard_map/ppermute | solution.py:336
  42.9 1.3 %collective-permute-start.18 = (f32[96,256]{1,0:T(8,128)S(1)}, f32[96,256]{1,0:T(8,128)S(1)}, u32[]{:S(2)}, u32[]{:S(2)}) collective-permute-start(f32[96,256]{1,0:T(8,128)S(1)} %collective-permute-done.14.refs_3_), channel_id=1, source_target_pairs={{0,1},{1,0},{2,3},{3,2},{4,5},{5,4},{6,7},{7,6},{8,9},{9,8},{10,11... | collective-permute-start | bytes 294920 | tf_op jit(solution)/shard_map/ppermute | solution.py:336

commit v4 on v3

--- a/solution.py
+++ b/solution.py
@@ -10,6 +10,7 @@
 F32 = jnp.float32
 BF16 = jnp.bfloat16
 NN = (((1,), (0,)), ((), ()))
+NT = (((1,), (1,)), ((), ()))
 VMEM = pl.BlockSpec(memory_space=pltpu.VMEM)
 HBM = pl.BlockSpec(memory_space=pltpu.HBM)
 SHADOW = 3_000_000_000
@@ -20,8 +21,8 @@
     return high, (value - high.astype(F32)).astype(BF16)
 
 
-def product(left, right):
-    dot = functools.partial(lax.dot_general, dimension_numbers=NN, preferred_element_type=F32)
+def product(left, right, dims=NN):
+    dot = functools.partial(lax.dot_general, dimension_numbers=dims, preferred_element_type=F32)
     return dot(left[0], right[0]) + (dot(left[0], right[1]) + dot(left[1], right[0]))
 
 
@@ -94,11 +95,9 @@
     own_ref[:, b:] = total
 
 
-def chip_kernel(heads, own_ref, other_ref, map_ref, *refs):
-    outs, state_ref = refs[:-1], refs[-1]
-    _, z, core = where()
+def chip_kernel(heads, ds, own_ref, other_ref, map_ref, state_ref, *outs):
+    core = where()[2]
     b = own_ref.shape[0]
-    part = outs[0].shape[0] - b // 2
 
     def combine(earlier_ref, later_ref):
         later = split(later_ref[:, :b])
@@ -113,13 +112,20 @@
     def _():
         combine(other_ref, own_ref)
 
-    for d, out in enumerate(outs):
+    cut_kernel(heads, ds, map_ref, state_ref, *outs)
+
+
+def cut_kernel(heads, ds, map_ref, state_ref, *outs):
+    _, z, core = where()
+    half = map_ref.shape[0] // 2
+    part = outs[0].shape[0] - half
+    for d, out in zip(ds, outs, strict=True):
         for j, head in enumerate(heads):
 
             @pl.when(z ^ d == head)
             def _():
-                out[: b // 2] = map_ref[rows(core * (b // 2), b // 2)]
-                out[b // 2 :] = state_ref[rows((2 * j + core) * part, part)]
+                out[:half] = map_ref[rows(core * half, half)]
+                out[half:] = state_ref[rows((2 * j + core) * part, part)]
 
 
 def on_head(heads, body):
@@ -151,28 +157,35 @@
     on_head(heads, body)
 
 
-def line_map_kernel(heads, chips, steps_ref, pre_ref, total_ref):
+def line_map_kernel(heads, chips, steps_ref, state_ref, pre_ref, total_ref):
+    b = steps_ref.shape[2]
+
     def body():
-        pre_ref[1] = steps_ref[0]
+        if chips == 1:
+            pre_ref[0] = steps_ref[0]
+            total_ref[:b] = steps_ref[0, 0].astype(F32) + steps_ref[0, 1].astype(F32)
+        else:
+            pre_ref[1] = steps_ref[0]
         for c in range(1, chips):
             total = product(get(pre_ref, c), get(steps_ref, c))
             put(pre_ref, total, (c + 1) % chips)
-        total_ref[...] = total
-
-    if chips > 1:
-        on_head(heads, body)
-    else:
-        pre_ref[...] = steps_ref[...]
-        total_ref[...] = steps_ref[0, 0].astype(F32) + steps_ref[0, 1].astype(F32)
-
-
-def total_kernel(with_map, *refs):
-    *preP, preF_ref, line_ref, f_ref = refs[: 3 + with_map]
-    outs = refs[3 + with_map :]
+            if c == chips - 1:
+                total_ref[:b] = total
+        total_ref[b:] = state_ref[...]
+
+    on_head(heads, body)
+
+
+def total_kernel(whole, *refs):
+    pre0_ref, *pre, line_ref, f_ref = refs[: 3 + whole]
+    outs = refs[3 + whole :]
+    b = line_ref.shape[2]
     step = get(line_ref, 0)
-    outs[0][...] = product(split(preF_ref[...]), step) + f_ref[...]
-    if with_map:
-        outs[1][...] = product(split(preP[0][...]), step)
+    outs[0][...] = product(split(pre0_ref[...]), step) + f_ref[...]
+    if whole:
+        total = product(split(pre[0][...]), step)
+        outs[1][:b] = total[:b]
+        outs[1][b:] = total[b:] + f_ref[...]
 
 
 def choose(refs, width, out_ref):
@@ -183,9 +196,31 @@
             out_ref[...] = ref[...]
 
 
-def prefix_map_kernel(width, *refs):
-    *maps, pre_ref, out_ref = refs
+def advance(width, states, pre0, pre, out_ref):
     g = where()[0]
+
+    @pl.when(g // width % 2 == 1)
+    def _():
+        choose(states, width, out_ref)
+        if pre:
+            b = out_ref.shape[1]
+
+            @pl.when(g % width != 0)
+            def _():
+                out_ref[...] = product(split(out_ref[...]), split(pre[0][:b])) + pre[0][b:]
+
+    if pre0:
+
+        @pl.when(g // width % 2 == 0)
+        def _():
+            out_ref[...] = pre0[0][...]
+
+
+def prefix_kernel(width, *refs):
+    states, maps, (pre0_ref, pre_ref, out0_ref, out_ref) = refs[:width], refs[width : 2 * width], refs[2 * width :]
+    g = where()[0]
+    b = pre_ref.shape[1]
+    advance(width, states, [pre0_ref], [pre_ref], out0_ref)
 
     @pl.when(g // width % 2 == 0)
     def _():
@@ -197,30 +232,8 @@
 
         @pl.when(g % width != 0)
         def _():
-            out_ref[...] = product(split(out_ref[...]), split(pre_ref[...]))
-
-
-def advance(width, states, pre, out_ref):
-    g = where()[0]
-
-    @pl.when(g // width % 2 == 1)
-    def _():
-        choose(states, width, out_ref)
-        if pre:
-
-            @pl.when(g % width != 0)
-            def _():
-                out_ref[...] = product(split(out_ref[...]), split(pre[0][...])) + pre[1][...]
-
-    if pre:
-
-        @pl.when(g // width % 2 == 0)
-        def _():
-            out_ref[...] = pre[1][...]
-
-
-def prefix_state_kernel(width, count, *refs):
-    advance(width, refs[:count], refs[count:-1], refs[-1])
+            out_ref[...] = product(split(out_ref[...]), split(pre_ref[:b]))
+            out_ref[b:] += pre_ref[b:]
 
 
 def start_kernel(width, count, with_pre, ds, *refs):
@@ -228,7 +241,7 @@
     pre, refs = refs[: 2 * with_pre], refs[2 * with_pre :]
     lineP_ref, lineF_ref, start_ref, *outs = refs
     if count:
-        advance(width, states, pre, start_ref)
+        advance(width, states, pre[:1], pre[1:], start_ref)
 
     @pl.when(where()[0] == 0)
     def _():
@@ -296,16 +309,16 @@
                 in_ref[rows((2 * j + core) * part, part)] = parts[d][...]
                 in_ref[rows((2 * j + 1 - core) * part, part)] = shared[d][...]
 
-    entering = split(in_ref[...].T)
+    entering = split(in_ref[...])
     copies = [pltpu.make_async_copy(xs_ref.at[i], x_ref.at[i], sems.at[0, i]) for i in range(n)]
     copies += [pltpu.make_async_copy(ss_ref.at[i], s_ref.at[i], sems.at[1, i]) for i in range(n)]
     for i in range(n):
-        xs_ref[i] = product(get(m_ref, i), entering) + c_ref[i]
+        xs_ref[i] = product(get(m_ref, i), entering, NT) + c_ref[i]
         copies[i].start()
         if i:
             ss_ref[i - 1] = xs_ref[i] - xs_ref[i - 1]
             copies[n + i - 1].start()
-    ss_ref[n - 1] = product(get(next_ref), entering) + add_ref[...] - xs_ref[n - 1]
+    ss_ref[n - 1] = product(get(next_ref), entering, NT) + add_ref[...] - xs_ref[n - 1]
 
     @pl.when(g * lax.axis_size("ry") + 2 * z + core == lax.axis_size("rx") * lax.axis_size("ry") - 1)
     def _():
@@ -341,16 +354,16 @@
     def from_heads(value, d):
         return lax.ppermute(value, "ry", filled([(h, h ^ d) for h in heads], chips))
 
-    def hops(value, width, start=0):
+    def hops(value, width, first=True):
         out = []
         for j in range(width):
             to = {}
-            for block in range(start, lines, 2 * width):
+            for block in range(0 if first else 2 * width, 2 * width if first else lines, 2 * width):
                 source, target = block + width - 1, block + width + j
-                back = block + j
-                to[source], to[target], to[back] = target, back, source
-                if back == source:
-                    to[source] = target
+                back = block + j if j < width - 1 else target
+                to[source], to[target] = target, source
+                if back != target:
+                    to[target], to[back] = back, source
             pairs = []
             for g in range(lines):
                 for i in range(places):
@@ -367,13 +380,17 @@
         spec=HBM,
     )(propagator, forcing)
     other = swap(own)
-    chip_map, *cuts = call(
-        functools.partial(chip_kernel, heads),
-        [(b, b)] + [(b // 2 + part, b)] * chips,
-        [pltpu.VMEM((r, b), F32)],
+    soon = [d for d in range(chips) if chips // 2 <= d < max(chips - 1, 1)]
+    later = [d for d in range(chips) if d not in soon]
+    chip_map, chip_state, *cuts = call(
+        functools.partial(chip_kernel, heads, soon), [(b, b), (r, b)] + [(b // 2 + part, b)] * len(soon)
     )(own, other)
+    more = call(functools.partial(cut_kernel, heads, later), [(b // 2 + part, b)] * len(later), cost=SHADOW)(
+        chip_map, chip_state
+    )
+    cuts = dict(zip([*soon, *later], [*cuts, *more], strict=True))
     gathered = [to_heads(cuts[d], d) for d in range(1, chips)]
-    early, _ = lax.optimization_barrier((first, cuts))
+    early, _ = lax.optimization_barrier((first, cuts[0]))
     matrices, constants = call(
         prepare_kernel,
         [halved(intervals, 2, b, b), (intervals, b, r)],
@@ -383,44 +400,35 @@
     for d in range(chips - 1):
         gathered[d], _ = lax.optimization_barrier((gathered[d], constants))
     swapped = [swap(value) for value in gathered]
+    first_late, _ = lax.optimization_barrier((first, gathered))
+    following = lax.ppermute(first_late, ("rx", "ry"), [(i, (i - 1) % devices) for i in range(devices)])
     steps, lineF, line_state = call(
         functools.partial(line_state_kernel, heads, chips),
         [halved(chips, 2, b, b), (chips, part, b), (part, b)],
         [pltpu.VMEM((chips, b, b), F32)],
     )(chip_map, cuts[0], *gathered, *swapped)
     lineP, line_map = call(
-        functools.partial(line_map_kernel, heads, chips), [halved(chips, 2, b, b), (b, b)], cost=SHADOW
-    )(steps)
-
-    def carried(value, width, pre):
-        maps = hops(value, width, 2 * width)
-        if width == 1:
-            return maps
-        return call(functools.partial(prefix_map_kernel, width), [(b, b)])(*maps, *pre)
-
-    total_map, total_state, pre_map, pre_state = line_map, line_state, [], None
+        functools.partial(line_map_kernel, heads, chips), [halved(chips, 2, b, b), (b + part, b)], cost=SHADOW
+    )(steps, line_state)
+
+    total_map, total_state, pre = line_map, line_state, []
     width, states = 1, []
     while width < lines:
         last = 2 * width >= lines
         if width > 1:
             total_state, *more = call(
-                functools.partial(total_kernel, not last), [(part, b)] + [(b, b)] * (not last), cost=SHADOW
-            )(*pre_map * (not last), pre_state, lineP, line_state)
+                functools.partial(total_kernel, not last), [(part, b)] + [(b + part, b)] * (not last), cost=SHADOW
+            )(*pre[: 2 - last], lineP, line_state)
             total_map = more and more[0]
         states = hops(total_state, width)
         if last:
             break
-        pre_map = carried(total_map, width, pre_map)
+        maps = hops(total_map, width, first=False)
         if width == 1:
-            pre_state = states[0]
+            pre = [*states, *maps]
         else:
-            (pre_state,) = call(functools.partial(prefix_state_kernel, width, width), [(part, b)])(
-                *states, *pre_map, pre_state
-            )
+            pre = call(functools.partial(prefix_kernel, width), [(part, b), (b + part, b)])(*states, *maps, *pre)
         width *= 2
-    pre = [] if pre_state is None else [*pre_map, pre_state]
-    first_late, _ = lax.optimization_barrier((first, line_state))
-    following = lax.ppermute(first_late, ("rx", "ry"), [(i, (i - 1) % devices) for i in range(devices)])
     near, far = range(max(chips // 2, 1)), range(max(chips // 2, 1), chips)
     start, *later = call(
         functools.partial(start_kernel, width, len(states), bool(pre), far), [(part, b)] * (1 + len(far))
@@ -434,6 +442,10 @@
     )
     for d in range(1, chips):
         parts[d], _ = lax.optimization_barrier((parts[d], next_constant))
+    shared = {d: swap(parts[d]) for d in range(chips) if d != 1}
+    if chips > 1:
+        parts[1], shared = lax.optimization_barrier((parts[1], shared))
+        shared[1] = swap(parts[1])
     return tuple(
         call(
             functools.partial(run_kernel, heads, chips),
@@ -445,7 +457,7 @@
                 pltpu.SemaphoreType.DMA((2, intervals)),
             ],
             out_spec=HBM,
-        )(*parts, *[swap(value) for value in parts], matrices, constants, next_matrix, next_constant)
+        )(*parts, *[shared[d] for d in range(chips)], matrices, constants, next_matrix, next_constant)
     )
 
 

time: 46.2 us -> 44.8 us (0.970)
  the two profiles are of different devices: /device:TPU:0 before, /device:TPU:7 now
where the time goes in v4:
time: 44.8 us; the launch traced here: 44.7 us
  starting transfers between devices  24.6 us (55%)
  waiting for transfers between devices  12.6 us (28%)
  Pallas kernels  6.73 us (15%)
  between operations  0.74 us (2%)
    ppermute x3, starting transfers between devices, from_heads(): return lax.ppermute(value, 'ry', filled([(h, h ^ d) for h in heads], chips))  10.3 us
    ppermute x8, starting transfers between devices, swap(): return lax.ppermute(value, 'ry', [(i, i ^ 1) for i in range(places)])  7.75 us
    pallas_call x11, Pallas kernels, run(): pl.pallas_call(kernel, in_specs=specs, out_specs=[out_spec] * len(outs),...  6.73 us
    ppermute x3, waiting for transfers between devices, to_heads(): return lax.ppermute(value, 'ry', filled([(h ^ d, h) for h in heads], chips))  5.7 us
    ppermute x8, waiting for transfers between devices, swap(): return lax.ppermute(value, 'ry', [(i, i ^ 1) for i in range(places)])  3.8 us
    ppermute x3, starting transfers between devices, to_heads(): return lax.ppermute(value, 'ry', filled([(h ^ d, h) for h in heads], chips))  3.14 us
    ppermute x4, starting transfers between devices, hops(): out.append(lax.ppermute(value, ('rx', 'ry'), pairs))  2.85 us
    ppermute x4, waiting for transfers between devices, hops(): out.append(lax.ppermute(value, ('rx', 'ry'), pairs))  1.99 us
  transfers between devices with their start and end apart: 19, of which 11 were waited for; matrix products, arithmetic and copies ran while one was open for 0% of the time, Pallas kernels for 6%

profile of v4, /device:TPU:7, one launch (start us, length us, event | category | flops | bytes accessed | tf_op | source)
XLA Modules:
  0.0 44.7 jit_solution(13706448173951980470)
XLA Ops:
  0.6 1.8 %shard_map.41 = (f32[256,640]{1,0:T(8,128)S(1)}, f32[256,640]{1,0:T(8,128)S(1)}, f32[1,256,640]{2,1,0:T(8,128)S(1)}) custom-call(f32[2,256,256]{2,1,0:T(8,128)} %a_ref.1, f32[2,256,384]{2,1,0:T(8,128)} %f_ref.1), custom_call_target="tpu_custom_call" | custom-call | tf_op jit(solution)/shard_map/pallas_call | solution.py:34
  2.5 0.7 %collective-permute-start = (f32[256,640]{1,0:T(8,128)S(1)}, f32[256,640]{1,0:T(8,128)S(1)}, u32[]{:S(2)}, u32[]{:S(2)}) collective-permute-start(f32[256,640]{1,0:T(8,128)S(1)} %get-tuple-element.38.own_ref), channel_id=1, source_target_pairs={{0,1},{1,0},{2,3},{3,2},{4,5},{5,4},{6,7},{7,6},{8,9},{9,8},{10,11... | collective-permute-start | bytes 1966088 | tf_op jit(solution)/shard_map/ppermute | solution.py:349
  3.2 1.7 %collective-permute-done.other_ref = f32[256,640]{1,0:T(8,128)S(1)} collective-permute-done((f32[256,640]{1,0:T(8,128)S(1)}, f32[256,640]{1,0:T(8,128)S(1)}, u32[]{:S(2)}, u32[]{:S(2)}) %collective-permute-start) | collective-permute-done | bytes 655392 | tf_op jit(solution)/shard_map/ppermute | solution.py:349
  4.9 0.6 %shard_map.42 = (f32[256,256]{1,0:T(8,128)S(1)}, f32[384,256]{1,0:T(8,128)S(1)}, f32[224,256]{1,0:T(8,128)S(1)}) custom-call(f32[256,640]{1,0:T(8,128)S(1)} %get-tuple-element.38.own_ref, f32[256,640]{1,0:T(8,128)S(1)} %collective-permute-done.other_ref), custom_call_target="tpu_custom_call" | custom-call | tf_op jit(solution)/shard_map/pallas_call | solution.py:34
  5.6 2.3 %collective-permute-start.2 = (f32[224,256]{1,0:T(8,128)S(1)}, f32[224,256]{1,0:T(8,128)S(1)}, u32[]{:S(2)}, u32[]{:S(2)}) collective-permute-start(f32[224,256]{1,0:T(8,128)S(1)} %get-tuple-element.48), channel_id=1, source_target_pairs={{6,2},{7,3},{0,4},{1,5},{2,0},{3,1},{4,6},{5,7},{14,10},{15,11},{8... | collective-permute-start | bytes 688136 | tf_op jit(solution)/shard_map/ppermute | solution.py:352
  8.0 0.7 %collective-permute-start.3 = (f32[224,256]{1,0:T(8,128)S(1)}, f32[224,256]{1,0:T(8,128)S(1)}, u32[]{:S(2)}, u32[]{:S(2)}) collective-permute-start(f32[224,256]{1,0:T(8,128)S(1)} %get-tuple-element.50), channel_id=1, source_target_pairs={{4,2},{5,3},{2,4},{3,5},{0,1},{1,0},{6,7},{7,6},{12,10},{13,11},{1... | collective-permute-start | bytes 688136 | tf_op jit(solution)/shard_map/ppermute | solution.py:352
  8.7 1.0 %shard_map.44 = (bf16[2,2,256,256]{3,2,1,0:T(8,128)(2,1)S(1)}, f32[2,256,384]{2,1,0:T(8,128)S(1)}) custom-call(f32[256,640]{1,0:T(8,128)S(1)} %collective-permute-done.other_ref, f32[256,640]{1,0:T(8,128)S(1)} %get-tuple-element.61.first_ref, f32[1,256,640]{2,1,0:T(8,128)S(1)} %get-tuple-element.45.rest_ref), custom_call_target="tpu_custom_call" | custom-call | flops 3000000000 | tf_op jit(solution)/shard_map/pallas_call | solution.py:34
  9.7 2.8 %collective-permute-done.2.refs_3_ = f32[224,256]{1,0:T(8,128)S(1)} collective-permute-done((f32[224,256]{1,0:T(8,128)S(1)}, f32[224,256]{1,0:T(8,128)S(1)}, u32[]{:S(2)}, u32[]{:S(2)}) %collective-permute-start.2) | collective-permute-done | bytes 229408 | tf_op jit(solution)/shard_map/ppermute | solution.py:352
  12.6 2.0 %collective-permute-start.5 = (f32[224,256]{1,0:T(8,128)S(1)}, f32[224,256]{1,0:T(8,128)S(1)}, u32[]{:S(2)}, u32[]{:S(2)}) collective-permute-start(f32[224,256]{1,0:T(8,128)S(1)} %collective-permute-done.2.refs_3_), channel_id=1, source_target_pairs={{0,1},{1,0},{2,3},{3,2},{4,5},{5,4},{6,7},{7,6},{8,9},{9,8},{10,11... | collective-permute-start | bytes 688136 | tf_op jit(solution)/shard_map/ppermute | solution.py:349
  14.6 2.9 %collective-permute-done.1.refs_2_ = f32[224,256]{1,0:T(8,128)S(1)} collective-permute-done((f32[224,256]{1,0:T(8,128)S(1)}, f32[224,256]{1,0:T(8,128)S(1)}, u32[]{:S(2)}, u32[]{:S(2)}) %collective-permute-start.1) | collective-permute-done | bytes 229408 | tf_op jit(solution)/shard_map/ppermute | solution.py:352
  17.5 1.2 %collective-permute-start.4 = (f32[224,256]{1,0:T(8,128)S(1)}, f32[224,256]{1,0:T(8,128)S(1)}, u32[]{:S(2)}, u32[]{:S(2)}) collective-permute-start(f32[224,256]{1,0:T(8,128)S(1)} %collective-permute-done.1.refs_2_), channel_id=1, source_target_pairs={{0,1},{1,0},{2,3},{3,2},{4,5},{5,4},{6,7},{7,6},{8,9},{9,8},{10,11... | collective-permute-start | bytes 688136 | tf_op jit(solution)/shard_map/ppermute | solution.py:349
  19.2 0.6 %collective-permute-done.4.refs_5_ = f32[224,256]{1,0:T(8,128)S(1)} collective-permute-done((f32[224,256]{1,0:T(8,128)S(1)}, f32[224,256]{1,0:T(8,128)S(1)}, u32[]{:S(2)}, u32[]{:S(2)}) %collective-permute-start.4) | collective-permute-done | bytes 229408 | tf_op jit(solution)/shard_map/ppermute | solution.py:349
  20.2 2.2 %collective-permute-start.7 = (f32[96,256]{1,0:T(8,128)S(1)}, f32[96,256]{1,0:T(8,128)S(1)}, u32[]{:S(2)}, u32[]{:S(2)}) collective-permute-start(f32[96,256]{1,0:T(8,128)S(1)} %get-tuple-element.52.state_ref.refs_2_), channel_id=1, source_target_pairs={{0,1},{1,0},{2,10},{3,11},{4,12},{5,13},{6,7},{7,6},{8,9},{9,8},{1... | collective-permute-start | bytes 294920 | tf_op jit(solution)/shard_map/ppermute | solution.py:372
  22.5 0.8 %collective-permute-done.7.refs_0_.refs_2_ = f32[96,256]{1,0:T(8,128)S(1)} collective-permute-done((f32[96,256]{1,0:T(8,128)S(1)}, f32[96,256]{1,0:T(8,128)S(1)}, u32[]{:S(2)}, u32[]{:S(2)}) %collective-permute-start.7) | collective-permute-done | bytes 98336 | tf_op jit(solution)/shard_map/ppermute | solution.py:372
  24.1 0.8 %collective-permute-done.9.refs_1_ = f32[96,256]{1,0:T(8,128)S(1)} collective-permute-done((f32[96,256]{1,0:T(8,128)S(1)}, f32[96,256]{1,0:T(8,128)S(1)}, u32[]{:S(2)}, u32[]{:S(2)}) %collective-permute-start.9) | collective-permute-done | bytes 98336 | tf_op jit(solution)/shard_map/ppermute | solution.py:372
  25.2 0.7 %shard_map.48 = (f32[96,256]{1,0:T(8,128)S(1)}, f32[96,256]{1,0:T(8,128)S(1)}, f32[96,256]{1,0:T(8,128)S(1)}) custom-call(f32[96,256]{1,0:T(8,128)S(1)} %collective-permute-done.8.refs_0_, f32[96,256]{1,0:T(8,128)S(1)} %collective-permute-done.9.refs_1_, f32[96,256]{1,0:T(8,128)S(1)} %collective-permute-done.7.refs_0_.refs_2_, ...), custom_call_target="tpu_custom_call" | custom-call | tf_op jit(solution)/shard_map/pallas_call | solution.py:34
  25.9 9.0 %collective-permute-start.14 = (f32[96,256]{1,0:T(8,128)S(1)}, f32[96,256]{1,0:T(8,128)S(1)}, u32[]{:S(2)}, u32[]{:S(2)}) collective-permute-start(f32[96,256]{1,0:T(8,128)S(1)} %get-tuple-element.65), channel_id=1, source_target_pairs={{2,6},{3,7},{4,0},{5,1},{0,2},{1,3},{6,4},{7,5},{10,14},{11,15},{1... | collective-permute-start | bytes 294920 | tf_op jit(solution)/shard_map/ppermute | solution.py:355
  34.9 1.3 %collective-permute-start.16 = (f32[96,256]{1,0:T(8,128)S(1)}, f32[96,256]{1,0:T(8,128)S(1)}, u32[]{:S(2)}, u32[]{:S(2)}) collective-permute-start(f32[96,256]{1,0:T(8,128)S(1)} %get-tuple-element.67), channel_id=1, source_target_pairs={{2,4},{3,5},{4,2},{5,3},{0,1},{1,0},{6,7},{7,6},{10,12},{11,13},{1... | collective-permute-start | bytes 294920 | tf_op jit(solution)/shard_map/ppermute | solution.py:355
  36.5 1.0 %collective-permute-start.13 = (f32[96,256]{1,0:T(8,128)S(1)}, f32[96,256]{1,0:T(8,128)S(1)}, u32[]{:S(2)}, u32[]{:S(2)}) collective-permute-start(f32[96,256]{1,0:T(8,128)S(1)} %get-tuple-element.58.refs_0_), channel_id=1, source_target_pairs={{0,1},{1,0},{2,3},{3,2},{4,5},{5,4},{6,7},{7,6},{8,9},{9,8},{10,11... | collective-permute-start | bytes 294920 | tf_op jit(solution)/shard_map/ppermute | solution.py:349
  37.9 2.2 %collective-permute-start.15 = (f32[96,256]{1,0:T(8,128)S(1)}, f32[96,256]{1,0:T(8,128)S(1)}, u32[]{:S(2)}, u32[]{:S(2)}) collective-permute-start(f32[96,256]{1,0:T(8,128)S(1)} %collective-permute-done.14.refs_2_), channel_id=1, source_target_pairs={{0,1},{1,0},{2,3},{3,2},{4,5},{5,4},{6,7},{7,6},{8,9},{9,8},{10,11... | collective-permute-start | bytes 294920 | tf_op jit(solution)/shard_map/ppermute | solution.py:349
  40.1 1.1 %collective-permute-done.11.refs_1_ = f32[96,256]{1,0:T(8,128)S(1)} collective-permute-done((f32[96,256]{1,0:T(8,128)S(1)}, f32[96,256]{1,0:T(8,128)S(1)}, u32[]{:S(2)}, u32[]{:S(2)}) %collective-permute-start.11) | collective-permute-done | bytes 98336 | tf_op jit(solution)/shard_map/ppermute | solution.py:355
  41.4 0.6 %collective-permute-start.18 = (f32[96,256]{1,0:T(8,128)S(1)}, f32[96,256]{1,0:T(8,128)S(1)}, u32[]{:S(2)}, u32[]{:S(2)}) collective-permute-start(f32[96,256]{1,0:T(8,128)S(1)} %collective-permute-done.11.refs_1_), channel_id=1, source_target_pairs={{0,1},{1,0},{2,3},{3,2},{4,5},{5,4},{6,7},{7,6},{8,9},{9,8},{10,11... | collective-permute-start | bytes 294920 | tf_op jit(solution)/shard_map/ppermute | solution.py:349
  42.0 0.9 %collective-permute-done.18.refs_5_ = f32[96,256]{1,0:T(8,128)S(1)} collective-permute-done((f32[96,256]{1,0:T(8,128)S(1)}, f32[96,256]{1,0:T(8,128)S(1)}, u32[]{:S(2)}, u32[]{:S(2)}) %collective-permute-start.18) | collective-permute-done | bytes 98336 | tf_op jit(solution)/shard_map/ppermute | solution.py:349
  43.0 1.7 %shard_map.51 = (f32[2,256,384]{2,1,0:T(8,128)}, f32[2,256,384]{2,1,0:T(8,128)}) custom-call(f32[96,256]{1,0:T(8,128)S(1)} %get-tuple-element.58.refs_0_, f32[96,256]{1,0:T(8,128)S(1)} %collective-permute-done.11.refs_1_, f32[96,256]{1,0:T(8,128)S(1)} %collective-permute-done.14.refs_2_, f32[96,256]{1,0:T(8,128)S(1)} %collective-permute-done.16.refs_3_, ...), custom_call_target="tpu_custom_call" | custom-call | tf_op jit(solution)/shard_map/pallas_call | solution.py:34
  (25 shorter events, 3.2 us)
Async XLA Ops:
  2.5 2.5 %collective-permute-start = (f32[256,640]{1,0:T(8,128)S(1)}, f32[256,640]{1,0:T(8,128)S(1)}, u32[]{:S(2)}, u32[]{:S(2)}) collective-permute-start(f32[256,640]{1,0:T(8,128)S(1)} %get-tuple-element.38.own_ref), channel_id=1, source_target_pairs={{0,1},{1,0},{2,3},{3,2},{4,5},{5,4},{6,7},{7,6},{8,9},{9,8},{10,11... | collective-permute-start | bytes 1966088 | tf_op jit(solution)/shard_map/ppermute | solution.py:349
  5.6 7.0 %collective-permute-start.2 = (f32[224,256]{1,0:T(8,128)S(1)}, f32[224,256]{1,0:T(8,128)S(1)}, u32[]{:S(2)}, u32[]{:S(2)}) collective-permute-start(f32[224,256]{1,0:T(8,128)S(1)} %get-tuple-element.48), channel_id=1, source_target_pairs={{6,2},{7,3},{0,4},{1,5},{2,0},{3,1},{4,6},{5,7},{14,10},{15,11},{8... | collective-permute-start | bytes 688136 | tf_op jit(solution)/shard_map/ppermute | solution.py:352
  7.9 9.5 %collective-permute-start.1 = (f32[224,256]{1,0:T(8,128)S(1)}, f32[224,256]{1,0:T(8,128)S(1)}, u32[]{:S(2)}, u32[]{:S(2)}) collective-permute-start(f32[224,256]{1,0:T(8,128)S(1)} %get-tuple-element.42), channel_id=1, source_target_pairs={{0,2},{1,3},{6,4},{7,5},{2,0},{3,1},{4,6},{5,7},{8,10},{9,11},{14,... | collective-permute-start | bytes 688136 | tf_op jit(solution)/shard_map/ppermute | solution.py:352
  8.0 10.7 %collective-permute-start.3 = (f32[224,256]{1,0:T(8,128)S(1)}, f32[224,256]{1,0:T(8,128)S(1)}, u32[]{:S(2)}, u32[]{:S(2)}) collective-permute-start(f32[224,256]{1,0:T(8,128)S(1)} %get-tuple-element.50), channel_id=1, source_target_pairs={{4,2},{5,3},{2,4},{3,5},{0,1},{1,0},{6,7},{7,6},{12,10},{13,11},{1... | collective-permute-start | bytes 688136 | tf_op jit(solution)/shard_map/ppermute | solution.py:352
  12.6 6.7 %collective-permute-start.5 = (f32[224,256]{1,0:T(8,128)S(1)}, f32[224,256]{1,0:T(8,128)S(1)}, u32[]{:S(2)}, u32[]{:S(2)}) collective-permute-start(f32[224,256]{1,0:T(8,128)S(1)} %collective-permute-done.2.refs_3_), channel_id=1, source_target_pairs={{0,1},{1,0},{2,3},{3,2},{4,5},{5,4},{6,7},{7,6},{8,9},{9,8},{10,11... | collective-permute-start | bytes 688136 | tf_op jit(solution)/shard_map/ppermute | solution.py:349
  17.5 2.3 %collective-permute-start.4 = (f32[224,256]{1,0:T(8,128)S(1)}, f32[224,256]{1,0:T(8,128)S(1)}, u32[]{:S(2)}, u32[]{:S(2)}) collective-permute-start(f32[224,256]{1,0:T(8,128)S(1)} %collective-permute-done.1.refs_2_), channel_id=1, source_target_pairs={{0,1},{1,0},{2,3},{3,2},{4,5},{5,4},{6,7},{7,6},{8,9},{9,8},{10,11... | collective-permute-start | bytes 688136 | tf_op jit(solution)/shard_map/ppermute | solution.py:349
  18.7 1.5 %collective-permute-start.6 = (f32[224,256]{1,0:T(8,128)S(1)}, f32[224,256]{1,0:T(8,128)S(1)}, u32[]{:S(2)}, u32[]{:S(2)}) collective-permute-start(f32[224,256]{1,0:T(8,128)S(1)} %collective-permute-done.3.refs_4_), channel_id=1, source_target_pairs={{0,1},{1,0},{2,3},{3,2},{4,5},{5,4},{6,7},{7,6},{8,9},{9,8},{10,11... | collective-permute-start | bytes 688136 | tf_op jit(solution)/shard_map/ppermute | solution.py:349
  18.7 18.7 %collective-permute-start.12 = (f32[256,640]{1,0:T(8,128)S(1)}, f32[256,640]{1,0:T(8,128)S(1)}, u32[]{:S(2)}, u32[]{:S(2)}) collective-permute-start(f32[256,640]{1,0:T(8,128)S(1)} %get-tuple-element.61.first_ref), channel_id=1, source_target_pairs={{0,31},{1,0},{2,1},{3,2},{4,3},{5,4},{6,5},{7,6},{8,7},{9,8},{10,9... | collective-permute-start | bytes 1966088 | tf_op jit(solution)/shard_map/ppermute | solution.py:404
  20.2 3.1 %collective-permute-start.7 = (f32[96,256]{1,0:T(8,128)S(1)}, f32[96,256]{1,0:T(8,128)S(1)}, u32[]{:S(2)}, u32[]{:S(2)}) collective-permute-start(f32[96,256]{1,0:T(8,128)S(1)} %get-tuple-element.52.state_ref.refs_2_), channel_id=1, source_target_pairs={{0,1},{1,0},{2,10},{3,11},{4,12},{5,13},{6,7},{7,6},{8,9},{9,8},{1... | collective-permute-start | bytes 294920 | tf_op jit(solution)/shard_map/ppermute | solution.py:372
  22.4 2.9 %collective-permute-start.10 = (f32[352,256]{1,0:T(8,128)S(1)}, f32[352,256]{1,0:T(8,128)S(1)}, u32[]{:S(2)}, u32[]{:S(2)}) collective-permute-start(f32[352,256]{1,0:T(8,128)S(1)} %get-tuple-element.55), channel_id=1, source_target_pairs={{0,1},{1,0},{2,3},{3,2},{4,5},{5,4},{6,7},{7,6},{8,9},{9,8},{10,11... | collective-permute-start | bytes 1081352 | tf_op jit(solution)/shard_map/ppermute | solution.py:372
  23.5 1.4 %collective-permute-start.9 = (f32[96,256]{1,0:T(8,128)S(1)}, f32[96,256]{1,0:T(8,128)S(1)}, u32[]{:S(2)}, u32[]{:S(2)}) collective-permute-start(f32[96,256]{1,0:T(8,128)S(1)} %shard_map.47), channel_id=1, source_target_pairs={{0,1},{1,0},{2,3},{3,2},{4,5},{5,4},{6,7},{7,6},{8,9},{9,8},{10,26... | collective-permute-start | bytes 294920 | tf_op jit(solution)/shard_map/ppermute | solution.py:372
  23.9 1.3 %collective-permute-start.8 = (f32[96,256]{1,0:T(8,128)S(1)}, f32[96,256]{1,0:T(8,128)S(1)}, u32[]{:S(2)}, u32[]{:S(2)}) collective-permute-start(f32[96,256]{1,0:T(8,128)S(1)} %shard_map.47), channel_id=1, source_target_pairs={{0,1},{1,0},{2,10},{3,11},{4,12},{5,13},{6,7},{7,6},{8,9},{9,8},{1... | collective-permute-start | bytes 294920 | tf_op jit(solution)/shard_map/ppermute | solution.py:372
  25.9 12.0 %collective-permute-start.14 = (f32[96,256]{1,0:T(8,128)S(1)}, f32[96,256]{1,0:T(8,128)S(1)}, u32[]{:S(2)}, u32[]{:S(2)}) collective-permute-start(f32[96,256]{1,0:T(8,128)S(1)} %get-tuple-element.65), channel_id=1, source_target_pairs={{2,6},{3,7},{4,0},{5,1},{0,2},{1,3},{6,4},{7,5},{10,14},{11,15},{1... | collective-permute-start | bytes 294920 | tf_op jit(solution)/shard_map/ppermute | solution.py:355
  34.9 3.0 %collective-permute-start.16 = (f32[96,256]{1,0:T(8,128)S(1)}, f32[96,256]{1,0:T(8,128)S(1)}, u32[]{:S(2)}, u32[]{:S(2)}) collective-permute-start(f32[96,256]{1,0:T(8,128)S(1)} %get-tuple-element.67), channel_id=1, source_target_pairs={{2,4},{3,5},{4,2},{5,3},{0,1},{1,0},{6,7},{7,6},{10,12},{11,13},{1... | collective-permute-start | bytes 294920 | tf_op jit(solution)/shard_map/ppermute | solution.py:355
  36.4 4.9 %collective-permute-start.11 = (f32[96,256]{1,0:T(8,128)S(1)}, f32[96,256]{1,0:T(8,128)S(1)}, u32[]{:S(2)}, u32[]{:S(2)}) collective-permute-start(f32[96,256]{1,0:T(8,128)S(1)} %get-tuple-element.59), channel_id=1, source_target_pairs={{2,0},{3,1},{4,6},{5,7},{0,2},{1,3},{6,4},{7,5},{10,8},{11,9},{12,... | collective-permute-start | bytes 294920 | tf_op jit(solution)/shard_map/ppermute | solution.py:355
  36.5 4.8 %collective-permute-start.13 = (f32[96,256]{1,0:T(8,128)S(1)}, f32[96,256]{1,0:T(8,128)S(1)}, u32[]{:S(2)}, u32[]{:S(2)}) collective-permute-start(f32[96,256]{1,0:T(8,128)S(1)} %get-tuple-element.58.refs_0_), channel_id=1, source_target_pairs={{0,1},{1,0},{2,3},{3,2},{4,5},{5,4},{6,7},{7,6},{8,9},{9,8},{10,11... | collective-permute-start | bytes 294920 | tf_op jit(solution)/shard_map/ppermute | solution.py:349
  37.9 3.4 %collective-permute-start.15 = (f32[96,256]{1,0:T(8,128)S(1)}, f32[96,256]{1,0:T(8,128)S(1)}, u32[]{:S(2)}, u32[]{:S(2)}) collective-permute-start(f32[96,256]{1,0:T(8,128)S(1)} %collective-permute-done.14.refs_2_), channel_id=1, source_target_pairs={{0,1},{1,0},{2,3},{3,2},{4,5},{5,4},{6,7},{7,6},{8,9},{9,8},{10,11... | collective-permute-start | bytes 294920 | tf_op jit(solution)/shard_map/ppermute | solution.py:349
  40.1 1.3 %collective-permute-start.17 = (f32[96,256]{1,0:T(8,128)S(1)}, f32[96,256]{1,0:T(8,128)S(1)}, u32[]{:S(2)}, u32[]{:S(2)}) collective-permute-start(f32[96,256]{1,0:T(8,128)S(1)} %collective-permute-done.16.refs_3_), channel_id=1, source_target_pairs={{0,1},{1,0},{2,3},{3,2},{4,5},{5,4},{6,7},{7,6},{8,9},{9,8},{10,11... | collective-permute-start | bytes 294920 | tf_op jit(solution)/shard_map/ppermute | solution.py:349
  41.4 1.5 %collective-permute-start.18 = (f32[96,256]{1,0:T(8,128)S(1)}, f32[96,256]{1,0:T(8,128)S(1)}, u32[]{:S(2)}, u32[]{:S(2)}) collective-permute-start(f32[96,256]{1,0:T(8,128)S(1)} %collective-permute-done.11.refs_1_), channel_id=1, source_target_pairs={{0,1},{1,0},{2,3},{3,2},{4,5},{5,4},{6,7},{7,6},{8,9},{9,8},{10,11... | collective-permute-start | bytes 294920 | tf_op jit(solution)/shard_map/ppermute | solution.py:349

commit v5 on v4

--- a/solution.py
+++ b/solution.py
@@ -157,21 +157,18 @@
     on_head(heads, body)
 
 
-def line_map_kernel(heads, chips, steps_ref, state_ref, pre_ref, total_ref):
-    b = steps_ref.shape[2]
+def line_map_kernel(heads, chips, steps_ref, state_ref, pre_ref, total_ref, all_ref):
+    half = steps_ref.shape[2] // 2
 
     def body():
-        if chips == 1:
-            pre_ref[0] = steps_ref[0]
-            total_ref[:b] = steps_ref[0, 0].astype(F32) + steps_ref[0, 1].astype(F32)
-        else:
-            pre_ref[1] = steps_ref[0]
+        pre_ref[1 % chips] = steps_ref[0]
+        total = steps_ref[0, 0].astype(F32) + steps_ref[0, 1].astype(F32)
         for c in range(1, chips):
             total = product(get(pre_ref, c), get(steps_ref, c))
             put(pre_ref, total, (c + 1) % chips)
-            if c == chips - 1:
-                total_ref[:b] = total
-        total_ref[b:] = state_ref[...]
+        all_ref[...] = total
+        total_ref[:half] = all_ref[rows(where()[2] * half, half)]
+        total_ref[half:] = state_ref[...]
 
     on_head(heads, body)
 
@@ -183,9 +180,10 @@
     step = get(line_ref, 0)
     outs[0][...] = product(split(pre0_ref[...]), step) + f_ref[...]
     if whole:
-        total = product(split(pre[0][...]), step)
-        outs[1][:b] = total[:b]
-        outs[1][b:] = total[b:] + f_ref[...]
+        half = b // 2
+        outs[2][...] = product(split(pre[0][:b]), step)
+        outs[1][:half] = outs[2][rows(where()[2] * half, half)]
+        outs[1][half:] = product(split(pre[0][b:]), step) + f_ref[...]
 
 
 def choose(refs, width, out_ref):
@@ -214,6 +212,23 @@
         @pl.when(g // width % 2 == 0)
         def _():
             out_ref[...] = pre0[0][...]
+
+
+def pieces_kernel(in_ref, *outs):
+    size = outs[0].shape[0]
+    for i, out in enumerate(outs):
+        out[...] = in_ref[i * size : (i + 1) * size]
+
+
+def whole_kernel(own_ref, *refs):
+    others, out_ref = refs[:-1], refs[-1]
+    core = where()[2]
+    b = out_ref.shape[1]
+    half, size = b // 2, b // 2 // len(others)
+    out_ref[rows(core * half, half)] = own_ref[:half]
+    for i, other_ref in enumerate(others):
+        out_ref[rows(half - core * half + i * size, size)] = other_ref[:size]
+    out_ref[b:] = own_ref[half:]
 
 
 def prefix_kernel(width, *refs):
@@ -238,10 +253,12 @@
 
 def start_kernel(width, count, with_pre, ds, *refs):
     states, refs = refs[:count], refs[count:]
-    pre, refs = refs[: 2 * with_pre], refs[2 * with_pre :]
-    lineP_ref, lineF_ref, start_ref, *outs = refs
+    pre, refs = refs[:with_pre], refs[with_pre:]
+    lineP_ref, lineF_ref, start_ref, *outs, pre_ref = refs
+    if with_pre > 2:
+        whole_kernel(*pre[1:], pre_ref)
     if count:
-        advance(width, states, pre[:1], pre[1:], start_ref)
+        advance(width, states, pre[:1], [pre_ref] if with_pre > 2 else pre[1:], start_ref)
 
     @pl.when(where()[0] == 0)
     def _():
@@ -360,10 +377,15 @@
             to = {}
             for block in range(0 if first else 2 * width, 2 * width if first else lines, 2 * width):
                 source, target = block + width - 1, block + width + j
-                back = block + j if j < width - 1 else target
+                back = target
                 to[source], to[target] = target, source
                 if back != target:
                     to[target], to[back] = back, source
+            if j < width - 1:
+                at = [2 * head + core for head in heads for core in range(2)]
+                pairs = [(s * places + i, t * places + i) for s, t in to.items() if s < t for i in at]
+                out.append(lax.ppermute(value, ("rx", "ry"), pairs))
+                continue
             pairs = []
             for g in range(lines):
                 for i in range(places):
@@ -408,30 +430,37 @@
         [pltpu.VMEM((chips, b, b), F32)],
     )(chip_map, cuts[0], *gathered, *swapped)
     lineP, line_map = call(
-        functools.partial(line_map_kernel, heads, chips), [halved(chips, 2, b, b), (b + part, b)], cost=SHADOW
+        functools.partial(line_map_kernel, heads, chips), [halved(chips, 2, b, b), (b // 2 + part, b)], [pltpu.VMEM((b, b), F32)], cost=SHADOW
     )(steps, line_state)
 
-    total_map, total_state, pre = line_map, line_state, []
+    total_map, total_state, pre, late = line_map, line_state, [], False
     width, states = 1, []
     while width < lines:
         last = 2 * width >= lines
         if width > 1:
             total_state, *more = call(
-                functools.partial(total_kernel, not last), [(part, b)] + [(b + part, b)] * (not last), cost=SHADOW
+                functools.partial(total_kernel, not last), [(part, b)] + [(b // 2 + part, b), (b, b)] * (not last), cost=SHADOW
             )(*pre[: 2 - last], lineP, line_state)
             total_map = more and more[0]
         states = hops(total_state, width)
         if last:
             break
         maps = hops(total_map, width, first=False)
+        late = width == 1 and 4 * width >= lines
+        if not late:
+            maps = [call(whole_kernel, [(b + part, b)])(value, swap(value))[0] for value in maps]
         if width == 1:
             pre = [*states, *maps]
         else:
             pre = call(functools.partial(prefix_kernel, width), [(part, b), (b + part, b)])(*states, *maps, *pre)
         width *= 2
+    if late:
+        pre[1], _ = lax.optimization_barrier((pre[1], total_state))
+        pre += [swap(piece) for piece in call(pieces_kernel, [(b // 4, b)] * 2, cost=1)(pre[1])]
     near, far = range(max(chips // 2, 1)), range(max(chips // 2, 1), chips)
     start, *later = call(
-        functools.partial(start_kernel, width, len(states), bool(pre), far), [(part, b)] * (1 + len(far))
+        functools.partial(start_kernel, width, len(states), len(pre), far), [(part, b)] * (1 + len(far)),
+        [pltpu.VMEM((b + part, b), F32)],
     )(*states, *pre, lineP, lineF)
     entering = call(functools.partial(enter_kernel, near), [(part, b)] * len(near), cost=SHADOW)(start, lineP, lineF)
     entering = [*entering, *later]

time: 44.8 us -> 44.1 us (0.984); the launches traced: 44.7 us -> 43.4 us
  starting transfers between devices: 24.6 us -> 22.4 us
  waiting for transfers between devices: 12.6 us -> 13.5 us
    ppermute x3, starting transfers between devices: 10.3 us -> 8.41 us  [from_heads(): return lax.ppermute(value, 'ry', filled([(h, h ^ d) for h in heads], chips))]
    ppermute x4, waiting for transfers between devices: 1.99 us -> 0.85 us  [hops(): out.append(lax.ppermute(value, ('rx', 'ry'), pairs))]
    ppermute x3, waiting for transfers between devices: 1.15 us -> 2.29 us  [from_heads(): return lax.ppermute(value, 'ry', filled([(h, h ^ d) for h in heads], chips))]
    ppermute x8 -> x10, waiting for transfers between devices: 3.8 us -> 4.68 us  [swap(): return lax.ppermute(value, 'ry', [(i, i ^ 1) for i in range(places)])]
    ppermute x8 -> x10, starting transfers between devices: 7.75 us -> 6.96 us  [swap(): return lax.ppermute(value, 'ry', [(i, i ^ 1) for i in range(places)])]
    ppermute x4, starting transfers between devices: 2.85 us -> 3.36 us  [hops(): out.append(lax.ppermute(value, ('rx', 'ry'), pairs))]
    pallas_call x11 -> x12, Pallas kernels: 6.73 us -> 6.78 us  [run(): pl.pallas_call(kernel, in_specs=specs, out_specs=[out_spec] * len(outs),...]
  transfers between devices with their start and end apart: 19 -> 21, of which waited for: 11 -> 12; matrix products, arithmetic and copies ran while one was open for 0% -> 0% of each run, Pallas kernels for 6% -> 6%
where the time goes in v5:
time: 44.1 us; the launch traced here: 43.4 us
  starting transfers between devices  22.4 us (51%)
  waiting for transfers between devices  13.5 us (31%)
  Pallas kernels  6.78 us (15%)
  between operations  0.75 us (2%)
    ppermute x3, starting transfers between devices, from_heads(): return lax.ppermute(value, 'ry', filled([(h, h ^ d) for h in heads], chips))  8.41 us
    ppermute x10, starting transfers between devices, swap(): return lax.ppermute(value, 'ry', [(i, i ^ 1) for i in range(places)])  6.96 us
    pallas_call x12, Pallas kernels, run(): pl.pallas_call(kernel, in_specs=specs, out_specs=[out_spec] * len(outs),...  6.78 us
    ppermute x3, waiting for transfers between devices, to_heads(): return lax.ppermute(value, 'ry', filled([(h ^ d, h) for h in heads], chips))  5.7 us
    ppermute x10, waiting for transfers between devices, swap(): return lax.ppermute(value, 'ry', [(i, i ^ 1) for i in range(places)])  4.68 us
    ppermute x4, starting transfers between devices, hops(): out.append(lax.ppermute(value, ('rx', 'ry'), pairs))  3.36 us
    ppermute x3, starting transfers between devices, to_heads(): return lax.ppermute(value, 'ry', filled([(h ^ d, h) for h in heads], chips))  3.14 us
    ppermute x3, waiting for transfers between devices, from_heads(): return lax.ppermute(value, 'ry', filled([(h, h ^ d) for h in heads], chips))  2.29 us
  transfers between devices with their start and end apart: 21, of which 12 were waited for; matrix products, arithmetic and copies ran while one was open for 0% of the time, Pallas kernels for 6%

profile of v5, /device:TPU:7, one launch (start us, length us, event | category | flops | bytes accessed | tf_op | source)
XLA Modules:
  0.0 43.4 jit_solution(11892923881624879447)
XLA Ops:
  0.6 1.8 %shard_map.41 = (f32[256,640]{1,0:T(8,128)S(1)}, f32[256,640]{1,0:T(8,128)S(1)}, f32[1,256,640]{2,1,0:T(8,128)S(1)}) custom-call(f32[2,256,256]{2,1,0:T(8,128)} %a_ref.1, f32[2,256,384]{2,1,0:T(8,128)} %f_ref.1), custom_call_target="tpu_custom_call" | custom-call | tf_op jit(solution)/shard_map/pallas_call | solution.py:34
  2.5 0.7 %collective-permute-start = (f32[256,640]{1,0:T(8,128)S(1)}, f32[256,640]{1,0:T(8,128)S(1)}, u32[]{:S(2)}, u32[]{:S(2)}) collective-permute-start(f32[256,640]{1,0:T(8,128)S(1)} %get-tuple-element.41.own_ref), channel_id=1, source_target_pairs={{0,1},{1,0},{2,3},{3,2},{4,5},{5,4},{6,7},{7,6},{8,9},{9,8},{10,11... | collective-permute-start | bytes 1966088 | tf_op jit(solution)/shard_map/ppermute | solution.py:366
  3.2 1.7 %collective-permute-done.other_ref = f32[256,640]{1,0:T(8,128)S(1)} collective-permute-done((f32[256,640]{1,0:T(8,128)S(1)}, f32[256,640]{1,0:T(8,128)S(1)}, u32[]{:S(2)}, u32[]{:S(2)}) %collective-permute-start) | collective-permute-done | bytes 655392 | tf_op jit(solution)/shard_map/ppermute | solution.py:366
  4.9 0.6 %shard_map.42 = (f32[256,256]{1,0:T(8,128)S(1)}, f32[384,256]{1,0:T(8,128)S(1)}, f32[224,256]{1,0:T(8,128)S(1)}) custom-call(f32[256,640]{1,0:T(8,128)S(1)} %get-tuple-element.41.own_ref, f32[256,640]{1,0:T(8,128)S(1)} %collective-permute-done.other_ref), custom_call_target="tpu_custom_call" | custom-call | tf_op jit(solution)/shard_map/pallas_call | solution.py:34
  5.6 2.3 %collective-permute-start.2 = (f32[224,256]{1,0:T(8,128)S(1)}, f32[224,256]{1,0:T(8,128)S(1)}, u32[]{:S(2)}, u32[]{:S(2)}) collective-permute-start(f32[224,256]{1,0:T(8,128)S(1)} %get-tuple-element.51), channel_id=1, source_target_pairs={{6,2},{7,3},{0,4},{1,5},{2,0},{3,1},{4,6},{5,7},{14,10},{15,11},{8... | collective-permute-start | bytes 688136 | tf_op jit(solution)/shard_map/ppermute | solution.py:369
  8.0 0.7 %collective-permute-start.3 = (f32[224,256]{1,0:T(8,128)S(1)}, f32[224,256]{1,0:T(8,128)S(1)}, u32[]{:S(2)}, u32[]{:S(2)}) collective-permute-start(f32[224,256]{1,0:T(8,128)S(1)} %get-tuple-element.53), channel_id=1, source_target_pairs={{4,2},{5,3},{2,4},{3,5},{0,1},{1,0},{6,7},{7,6},{12,10},{13,11},{1... | collective-permute-start | bytes 688136 | tf_op jit(solution)/shard_map/ppermute | solution.py:369
  8.7 1.0 %shard_map.44 = (bf16[2,2,256,256]{3,2,1,0:T(8,128)(2,1)S(1)}, f32[2,256,384]{2,1,0:T(8,128)S(1)}) custom-call(f32[256,640]{1,0:T(8,128)S(1)} %collective-permute-done.other_ref, f32[256,640]{1,0:T(8,128)S(1)} %get-tuple-element.67.first_ref, f32[1,256,640]{2,1,0:T(8,128)S(1)} %get-tuple-element.48.rest_ref), custom_call_target="tpu_custom_call" | custom-call | flops 3000000000 | tf_op jit(solution)/shard_map/pallas_call | solution.py:34
  9.7 2.8 %collective-permute-done.2.refs_3_ = f32[224,256]{1,0:T(8,128)S(1)} collective-permute-done((f32[224,256]{1,0:T(8,128)S(1)}, f32[224,256]{1,0:T(8,128)S(1)}, u32[]{:S(2)}, u32[]{:S(2)}) %collective-permute-start.2) | collective-permute-done | bytes 229408 | tf_op jit(solution)/shard_map/ppermute | solution.py:369
  12.6 2.0 %collective-permute-start.5 = (f32[224,256]{1,0:T(8,128)S(1)}, f32[224,256]{1,0:T(8,128)S(1)}, u32[]{:S(2)}, u32[]{:S(2)}) collective-permute-start(f32[224,256]{1,0:T(8,128)S(1)} %collective-permute-done.2.refs_3_), channel_id=1, source_target_pairs={{0,1},{1,0},{2,3},{3,2},{4,5},{5,4},{6,7},{7,6},{8,9},{9,8},{10,11... | collective-permute-start | bytes 688136 | tf_op jit(solution)/shard_map/ppermute | solution.py:366
  14.6 2.9 %collective-permute-done.1.refs_2_ = f32[224,256]{1,0:T(8,128)S(1)} collective-permute-done((f32[224,256]{1,0:T(8,128)S(1)}, f32[224,256]{1,0:T(8,128)S(1)}, u32[]{:S(2)}, u32[]{:S(2)}) %collective-permute-start.1) | collective-permute-done | bytes 229408 | tf_op jit(solution)/shard_map/ppermute | solution.py:369
  17.5 1.2 %collective-permute-start.4 = (f32[224,256]{1,0:T(8,128)S(1)}, f32[224,256]{1,0:T(8,128)S(1)}, u32[]{:S(2)}, u32[]{:S(2)}) collective-permute-start(f32[224,256]{1,0:T(8,128)S(1)} %collective-permute-done.1.refs_2_), channel_id=1, source_target_pairs={{0,1},{1,0},{2,3},{3,2},{4,5},{5,4},{6,7},{7,6},{8,9},{9,8},{10,11... | collective-permute-start | bytes 688136 | tf_op jit(solution)/shard_map/ppermute | solution.py:366
  20.2 2.2 %collective-permute-start.7 = (f32[96,256]{1,0:T(8,128)S(1)}, f32[96,256]{1,0:T(8,128)S(1)}, u32[]{:S(2)}, u32[]{:S(2)}) collective-permute-start(f32[96,256]{1,0:T(8,128)S(1)} %get-tuple-element.55.state_ref.refs_2_), channel_id=1, source_target_pairs={{0,1},{1,0},{2,10},{3,11},{4,12},{5,13},{6,7},{7,6},{8,9},{9,8},{1... | collective-permute-start | bytes 294920 | tf_op jit(solution)/shard_map/ppermute | solution.py:394
  22.5 0.8 %collective-permute-done.7.refs_0_.refs_2_ = f32[96,256]{1,0:T(8,128)S(1)} collective-permute-done((f32[96,256]{1,0:T(8,128)S(1)}, f32[96,256]{1,0:T(8,128)S(1)}, u32[]{:S(2)}, u32[]{:S(2)}) %collective-permute-start.7) | collective-permute-done | bytes 98336 | tf_op jit(solution)/shard_map/ppermute | solution.py:394
  23.9 0.7 %collective-permute-start.8 = (f32[96,256]{1,0:T(8,128)S(1)}, f32[96,256]{1,0:T(8,128)S(1)}, u32[]{:S(2)}, u32[]{:S(2)}) collective-permute-start(f32[96,256]{1,0:T(8,128)S(1)} %shard_map.47), channel_id=1, source_target_pairs={{10,18},{11,19},{12,20},{13,21}} | collective-permute-start | bytes 294920 | tf_op jit(solution)/shard_map/ppermute | solution.py:387
  25.2 0.7 %collective-permute-done.11.refs_4_ = f32[64,256]{1,0:T(8,128)S(1)} collective-permute-done((f32[64,256]{1,0:T(8,128)S(1)}, f32[64,256]{1,0:T(8,128)S(1)}, u32[]{:S(2)}, u32[]{:S(2)}) %collective-permute-start.11) | collective-permute-done | bytes 65568 | tf_op jit(solution)/shard_map/ppermute | solution.py:366
  26.1 0.7 %shard_map.49 = (f32[96,256]{1,0:T(8,128)S(1)}, f32[96,256]{1,0:T(8,128)S(1)}, f32[96,256]{1,0:T(8,128)S(1)}) custom-call(f32[96,256]{1,0:T(8,128)S(1)} %collective-permute-done.8.refs_0_, f32[96,256]{1,0:T(8,128)S(1)} %collective-permute-done.9.refs_1_, f32[96,256]{1,0:T(8,128)S(1)} %collective-permute-done.7.refs_0_.refs_2_, ...), custom_call_target="tpu_custom_call" | custom-call | tf_op jit(solution)/shard_map/pallas_call | solution.py:34
  26.8 7.7 %collective-permute-start.16 = (f32[96,256]{1,0:T(8,128)S(1)}, f32[96,256]{1,0:T(8,128)S(1)}, u32[]{:S(2)}, u32[]{:S(2)}) collective-permute-start(f32[96,256]{1,0:T(8,128)S(1)} %get-tuple-element.71), channel_id=1, source_target_pairs={{2,6},{3,7},{4,0},{5,1},{0,2},{1,3},{6,4},{7,5},{10,14},{11,15},{1... | collective-permute-start | bytes 294920 | tf_op jit(solution)/shard_map/ppermute | solution.py:372
  35.5 0.7 %collective-permute-start.15 = (f32[96,256]{1,0:T(8,128)S(1)}, f32[96,256]{1,0:T(8,128)S(1)}, u32[]{:S(2)}, u32[]{:S(2)}) collective-permute-start(f32[96,256]{1,0:T(8,128)S(1)} %get-tuple-element.64.refs_0_), channel_id=1, source_target_pairs={{0,1},{1,0},{2,3},{3,2},{4,5},{5,4},{6,7},{7,6},{8,9},{9,8},{10,11... | collective-permute-start | bytes 294920 | tf_op jit(solution)/shard_map/ppermute | solution.py:366
  36.7 1.1 %collective-permute-done.16.refs_2_ = f32[96,256]{1,0:T(8,128)S(1)} collective-permute-done((f32[96,256]{1,0:T(8,128)S(1)}, f32[96,256]{1,0:T(8,128)S(1)}, u32[]{:S(2)}, u32[]{:S(2)}) %collective-permute-start.16) | collective-permute-done | bytes 98336 | tf_op jit(solution)/shard_map/ppermute | solution.py:372
  37.8 1.1 %collective-permute-start.17 = (f32[96,256]{1,0:T(8,128)S(1)}, f32[96,256]{1,0:T(8,128)S(1)}, u32[]{:S(2)}, u32[]{:S(2)}) collective-permute-start(f32[96,256]{1,0:T(8,128)S(1)} %collective-permute-done.16.refs_2_), channel_id=1, source_target_pairs={{0,1},{1,0},{2,3},{3,2},{4,5},{5,4},{6,7},{7,6},{8,9},{9,8},{10,11... | collective-permute-start | bytes 294920 | tf_op jit(solution)/shard_map/ppermute | solution.py:366
  38.9 1.2 %collective-permute-done.13.refs_1_ = f32[96,256]{1,0:T(8,128)S(1)} collective-permute-done((f32[96,256]{1,0:T(8,128)S(1)}, f32[96,256]{1,0:T(8,128)S(1)}, u32[]{:S(2)}, u32[]{:S(2)}) %collective-permute-start.13) | collective-permute-done | bytes 98336 | tf_op jit(solution)/shard_map/ppermute | solution.py:372
  40.2 0.6 %collective-permute-start.20 = (f32[96,256]{1,0:T(8,128)S(1)}, f32[96,256]{1,0:T(8,128)S(1)}, u32[]{:S(2)}, u32[]{:S(2)}) collective-permute-start(f32[96,256]{1,0:T(8,128)S(1)} %collective-permute-done.13.refs_1_), channel_id=1, source_target_pairs={{0,1},{1,0},{2,3},{3,2},{4,5},{5,4},{6,7},{7,6},{8,9},{9,8},{10,11... | collective-permute-start | bytes 294920 | tf_op jit(solution)/shard_map/ppermute | solution.py:366
  40.8 0.9 %collective-permute-done.20.refs_5_ = f32[96,256]{1,0:T(8,128)S(1)} collective-permute-done((f32[96,256]{1,0:T(8,128)S(1)}, f32[96,256]{1,0:T(8,128)S(1)}, u32[]{:S(2)}, u32[]{:S(2)}) %collective-permute-start.20) | collective-permute-done | bytes 98336 | tf_op jit(solution)/shard_map/ppermute | solution.py:366
  41.7 1.7 %shard_map.52 = (f32[2,256,384]{2,1,0:T(8,128)}, f32[2,256,384]{2,1,0:T(8,128)}) custom-call(f32[96,256]{1,0:T(8,128)S(1)} %get-tuple-element.64.refs_0_, f32[96,256]{1,0:T(8,128)S(1)} %collective-permute-done.13.refs_1_, f32[96,256]{1,0:T(8,128)S(1)} %collective-permute-done.16.refs_2_, f32[96,256]{1,0:T(8,128)S(1)} %collective-permute-done.18.refs_3_, ...), custom_call_target="tpu_custom_call" | custom-call | tf_op jit(solution)/shard_map/pallas_call | solution.py:34
  (30 shorter events, 4.7 us)
Async XLA Ops:
  2.5 2.5 %collective-permute-start = (f32[256,640]{1,0:T(8,128)S(1)}, f32[256,640]{1,0:T(8,128)S(1)}, u32[]{:S(2)}, u32[]{:S(2)}) collective-permute-start(f32[256,640]{1,0:T(8,128)S(1)} %get-tuple-element.41.own_ref), channel_id=1, source_target_pairs={{0,1},{1,0},{2,3},{3,2},{4,5},{5,4},{6,7},{7,6},{8,9},{9,8},{10,11... | collective-permute-start | bytes 1966088 | tf_op jit(solution)/shard_map/ppermute | solution.py:366
  5.6 7.0 %collective-permute-start.2 = (f32[224,256]{1,0:T(8,128)S(1)}, f32[224,256]{1,0:T(8,128)S(1)}, u32[]{:S(2)}, u32[]{:S(2)}) collective-permute-start(f32[224,256]{1,0:T(8,128)S(1)} %get-tuple-element.51), channel_id=1, source_target_pairs={{6,2},{7,3},{0,4},{1,5},{2,0},{3,1},{4,6},{5,7},{14,10},{15,11},{8... | collective-permute-start | bytes 688136 | tf_op jit(solution)/shard_map/ppermute | solution.py:369
  7.9 9.5 %collective-permute-start.1 = (f32[224,256]{1,0:T(8,128)S(1)}, f32[224,256]{1,0:T(8,128)S(1)}, u32[]{:S(2)}, u32[]{:S(2)}) collective-permute-start(f32[224,256]{1,0:T(8,128)S(1)} %get-tuple-element.45), channel_id=1, source_target_pairs={{0,2},{1,3},{6,4},{7,5},{2,0},{3,1},{4,6},{5,7},{8,10},{9,11},{14,... | collective-permute-start | bytes 688136 | tf_op jit(solution)/shard_map/ppermute | solution.py:369
  8.0 10.7 %collective-permute-start.3 = (f32[224,256]{1,0:T(8,128)S(1)}, f32[224,256]{1,0:T(8,128)S(1)}, u32[]{:S(2)}, u32[]{:S(2)}) collective-permute-start(f32[224,256]{1,0:T(8,128)S(1)} %get-tuple-element.53), channel_id=1, source_target_pairs={{4,2},{5,3},{2,4},{3,5},{0,1},{1,0},{6,7},{7,6},{12,10},{13,11},{1... | collective-permute-start | bytes 688136 | tf_op jit(solution)/shard_map/ppermute | solution.py:369
  12.6 6.7 %collective-permute-start.5 = (f32[224,256]{1,0:T(8,128)S(1)}, f32[224,256]{1,0:T(8,128)S(1)}, u32[]{:S(2)}, u32[]{:S(2)}) collective-permute-start(f32[224,256]{1,0:T(8,128)S(1)} %collective-permute-done.2.refs_3_), channel_id=1, source_target_pairs={{0,1},{1,0},{2,3},{3,2},{4,5},{5,4},{6,7},{7,6},{8,9},{9,8},{10,11... | collective-permute-start | bytes 688136 | tf_op jit(solution)/shard_map/ppermute | solution.py:366
  17.5 2.3 %collective-permute-start.4 = (f32[224,256]{1,0:T(8,128)S(1)}, f32[224,256]{1,0:T(8,128)S(1)}, u32[]{:S(2)}, u32[]{:S(2)}) collective-permute-start(f32[224,256]{1,0:T(8,128)S(1)} %collective-permute-done.1.refs_2_), channel_id=1, source_target_pairs={{0,1},{1,0},{2,3},{3,2},{4,5},{5,4},{6,7},{7,6},{8,9},{9,8},{10,11... | collective-permute-start | bytes 688136 | tf_op jit(solution)/shard_map/ppermute | solution.py:366
  18.7 1.5 %collective-permute-start.6 = (f32[224,256]{1,0:T(8,128)S(1)}, f32[224,256]{1,0:T(8,128)S(1)}, u32[]{:S(2)}, u32[]{:S(2)}) collective-permute-start(f32[224,256]{1,0:T(8,128)S(1)} %collective-permute-done.3.refs_4_), channel_id=1, source_target_pairs={{0,1},{1,0},{2,3},{3,2},{4,5},{5,4},{6,7},{7,6},{8,9},{9,8},{10,11... | collective-permute-start | bytes 688136 | tf_op jit(solution)/shard_map/ppermute | solution.py:366
  18.7 17.5 %collective-permute-start.14 = (f32[256,640]{1,0:T(8,128)S(1)}, f32[256,640]{1,0:T(8,128)S(1)}, u32[]{:S(2)}, u32[]{:S(2)}) collective-permute-start(f32[256,640]{1,0:T(8,128)S(1)} %get-tuple-element.67.first_ref), channel_id=1, source_target_pairs={{0,31},{1,0},{2,1},{3,2},{4,3},{5,4},{6,5},{7,6},{8,7},{9,8},{10,9... | collective-permute-start | bytes 1966088 | tf_op jit(solution)/shard_map/ppermute | solution.py:426
  20.2 3.1 %collective-permute-start.7 = (f32[96,256]{1,0:T(8,128)S(1)}, f32[96,256]{1,0:T(8,128)S(1)}, u32[]{:S(2)}, u32[]{:S(2)}) collective-permute-start(f32[96,256]{1,0:T(8,128)S(1)} %get-tuple-element.55.state_ref.refs_2_), channel_id=1, source_target_pairs={{0,1},{1,0},{2,10},{3,11},{4,12},{5,13},{6,7},{7,6},{8,9},{9,8},{1... | collective-permute-start | bytes 294920 | tf_op jit(solution)/shard_map/ppermute | solution.py:394
  22.4 2.2 %collective-permute-start.10 = (f32[224,256]{1,0:T(8,128)S(1)}, f32[224,256]{1,0:T(8,128)S(1)}, u32[]{:S(2)}, u32[]{:S(2)}) collective-permute-start(f32[224,256]{1,0:T(8,128)S(1)} %get-tuple-element.58), channel_id=1, source_target_pairs={{0,1},{1,0},{2,3},{3,2},{4,5},{5,4},{6,7},{7,6},{8,9},{9,8},{10,11... | collective-permute-start | bytes 688136 | tf_op jit(solution)/shard_map/ppermute | solution.py:394
  23.5 1.7 %collective-permute-start.9 = (f32[96,256]{1,0:T(8,128)S(1)}, f32[96,256]{1,0:T(8,128)S(1)}, u32[]{:S(2)}, u32[]{:S(2)}) collective-permute-start(f32[96,256]{1,0:T(8,128)S(1)} %shard_map.47), channel_id=1, source_target_pairs={{0,1},{1,0},{2,3},{3,2},{4,5},{5,4},{6,7},{7,6},{8,9},{9,8},{10,26... | collective-permute-start | bytes 294920 | tf_op jit(solution)/shard_map/ppermute | solution.py:394
  23.9 1.3 %collective-permute-start.8 = (f32[96,256]{1,0:T(8,128)S(1)}, f32[96,256]{1,0:T(8,128)S(1)}, u32[]{:S(2)}, u32[]{:S(2)}) collective-permute-start(f32[96,256]{1,0:T(8,128)S(1)} %shard_map.47), channel_id=1, source_target_pairs={{10,18},{11,19},{12,20},{13,21}} | collective-permute-start | bytes 294920 | tf_op jit(solution)/shard_map/ppermute | solution.py:387
  24.6 1.3 %collective-permute-start.11 = (f32[64,256]{1,0:T(8,128)S(1)}, f32[64,256]{1,0:T(8,128)S(1)}, u32[]{:S(2)}, u32[]{:S(2)}) collective-permute-start(f32[64,256]{1,0:T(8,128)S(1)} %get-tuple-element.60), channel_id=1, source_target_pairs={{0,1},{1,0},{2,3},{3,2},{4,5},{5,4},{6,7},{7,6},{8,9},{9,8},{10,11... | collective-permute-start | bytes 196616 | tf_op jit(solution)/shard_map/ppermute | solution.py:366
  24.8 1.3 %collective-permute-start.12 = (f32[64,256]{1,0:T(8,128)S(1)}, f32[64,256]{1,0:T(8,128)S(1)}, u32[]{:S(2)}, u32[]{:S(2)}) collective-permute-start(f32[64,256]{1,0:T(8,128)S(1)} %get-tuple-element.61), channel_id=1, source_target_pairs={{0,1},{1,0},{2,3},{3,2},{4,5},{5,4},{6,7},{7,6},{8,9},{9,8},{10,11... | collective-permute-start | bytes 196616 | tf_op jit(solution)/shard_map/ppermute | solution.py:366
  26.8 11.0 %collective-permute-start.16 = (f32[96,256]{1,0:T(8,128)S(1)}, f32[96,256]{1,0:T(8,128)S(1)}, u32[]{:S(2)}, u32[]{:S(2)}) collective-permute-start(f32[96,256]{1,0:T(8,128)S(1)} %get-tuple-element.71), channel_id=1, source_target_pairs={{2,6},{3,7},{4,0},{5,1},{0,2},{1,3},{6,4},{7,5},{10,14},{11,15},{1... | collective-permute-start | bytes 294920 | tf_op jit(solution)/shard_map/ppermute | solution.py:372
  34.5 2.2 %collective-permute-start.18 = (f32[96,256]{1,0:T(8,128)S(1)}, f32[96,256]{1,0:T(8,128)S(1)}, u32[]{:S(2)}, u32[]{:S(2)}) collective-permute-start(f32[96,256]{1,0:T(8,128)S(1)} %get-tuple-element.73), channel_id=1, source_target_pairs={{2,4},{3,5},{4,2},{5,3},{0,1},{1,0},{6,7},{7,6},{10,12},{11,13},{1... | collective-permute-start | bytes 294920 | tf_op jit(solution)/shard_map/ppermute | solution.py:372
  35.1 4.9 %collective-permute-start.13 = (f32[96,256]{1,0:T(8,128)S(1)}, f32[96,256]{1,0:T(8,128)S(1)}, u32[]{:S(2)}, u32[]{:S(2)}) collective-permute-start(f32[96,256]{1,0:T(8,128)S(1)} %get-tuple-element.65), channel_id=1, source_target_pairs={{2,0},{3,1},{4,6},{5,7},{0,2},{1,3},{6,4},{7,5},{10,8},{11,9},{12,... | collective-permute-start | bytes 294920 | tf_op jit(solution)/shard_map/ppermute | solution.py:372
  35.5 4.6 %collective-permute-start.15 = (f32[96,256]{1,0:T(8,128)S(1)}, f32[96,256]{1,0:T(8,128)S(1)}, u32[]{:S(2)}, u32[]{:S(2)}) collective-permute-start(f32[96,256]{1,0:T(8,128)S(1)} %get-tuple-element.64.refs_0_), channel_id=1, source_target_pairs={{0,1},{1,0},{2,3},{3,2},{4,5},{5,4},{6,7},{7,6},{8,9},{9,8},{10,11... | collective-permute-start | bytes 294920 | tf_op jit(solution)/shard_map/ppermute | solution.py:366
  37.8 2.2 %collective-permute-start.17 = (f32[96,256]{1,0:T(8,128)S(1)}, f32[96,256]{1,0:T(8,128)S(1)}, u32[]{:S(2)}, u32[]{:S(2)}) collective-permute-start(f32[96,256]{1,0:T(8,128)S(1)} %collective-permute-done.16.refs_2_), channel_id=1, source_target_pairs={{0,1},{1,0},{2,3},{3,2},{4,5},{5,4},{6,7},{7,6},{8,9},{9,8},{10,11... | collective-permute-start | bytes 294920 | tf_op jit(solution)/shard_map/ppermute | solution.py:366
  38.9 1.3 %collective-permute-start.19 = (f32[96,256]{1,0:T(8,128)S(1)}, f32[96,256]{1,0:T(8,128)S(1)}, u32[]{:S(2)}, u32[]{:S(2)}) collective-permute-start(f32[96,256]{1,0:T(8,128)S(1)} %collective-permute-done.18.refs_3_), channel_id=1, source_target_pairs={{0,1},{1,0},{2,3},{3,2},{4,5},{5,4},{6,7},{7,6},{8,9},{9,8},{10,11... | collective-permute-start | bytes 294920 | tf_op jit(solution)/shard_map/ppermute | solution.py:366
  40.2 1.5 %collective-permute-start.20 = (f32[96,256]{1,0:T(8,128)S(1)}, f32[96,256]{1,0:T(8,128)S(1)}, u32[]{:S(2)}, u32[]{:S(2)}) collective-permute-start(f32[96,256]{1,0:T(8,128)S(1)} %collective-permute-done.13.refs_1_), channel_id=1, source_target_pairs={{0,1},{1,0},{2,3},{3,2},{4,5},{5,4},{6,7},{7,6},{8,9},{9,8},{10,11... | collective-permute-start | bytes 294920 | tf_op jit(solution)/shard_map/ppermute | solution.py:366

commit v6 on v5

--- a/solution.py
+++ b/solution.py
@@ -118,7 +118,7 @@
 def cut_kernel(heads, ds, map_ref, state_ref, *outs):
     _, z, core = where()
     half = map_ref.shape[0] // 2
-    part = outs[0].shape[0] - half
+    part = outs[0].shape[0] - half if outs else 0
     for d, out in zip(ds, outs, strict=True):
         for j, head in enumerate(heads):
 
@@ -157,7 +157,7 @@
     on_head(heads, body)
 
 
-def line_map_kernel(heads, chips, steps_ref, state_ref, pre_ref, total_ref, all_ref):
+def line_map_kernel(heads, chips, steps_ref, pre_ref, total_ref, all_ref):
     half = steps_ref.shape[2] // 2
 
     def body():
@@ -167,8 +167,7 @@
             total = product(get(pre_ref, c), get(steps_ref, c))
             put(pre_ref, total, (c + 1) % chips)
         all_ref[...] = total
-        total_ref[:half] = all_ref[rows(where()[2] * half, half)]
-        total_ref[half:] = state_ref[...]
+        total_ref[...] = all_ref[rows(where()[2] * half, half)]
 
     on_head(heads, body)
 
@@ -181,9 +180,9 @@
     outs[0][...] = product(split(pre0_ref[...]), step) + f_ref[...]
     if whole:
         half = b // 2
-        outs[2][...] = product(split(pre[0][:b]), step)
-        outs[1][:half] = outs[2][rows(where()[2] * half, half)]
-        outs[1][half:] = product(split(pre[0][b:]), step) + f_ref[...]
+        outs[3][...] = product(split(pre[0][:b]), step)
+        outs[1][...] = outs[3][rows(where()[2] * half, half)]
+        outs[2][...] = product(split(pre[0][b:]), step) + f_ref[...]
 
 
 def choose(refs, width, out_ref):
@@ -220,15 +219,15 @@
         out[...] = in_ref[i * size : (i + 1) * size]
 
 
-def whole_kernel(own_ref, *refs):
+def whole_kernel(own_ref, state_ref, *refs):
     others, out_ref = refs[:-1], refs[-1]
     core = where()[2]
     b = out_ref.shape[1]
     half, size = b // 2, b // 2 // len(others)
-    out_ref[rows(core * half, half)] = own_ref[:half]
+    out_ref[rows(core * half, half)] = own_ref[...]
     for i, other_ref in enumerate(others):
-        out_ref[rows(half - core * half + i * size, size)] = other_ref[:size]
-    out_ref[b:] = own_ref[half:]
+        out_ref[rows(half - core * half + i * size, size)] = other_ref[...]
+    out_ref[b:] = state_ref[...]
 
 
 def prefix_kernel(width, *refs):
@@ -252,7 +251,7 @@
 
 
 def start_kernel(width, count, with_pre, ds, *refs):
-    states, refs = refs[:count], refs[count:]
+    states, refs = refs[:count][::-1], refs[count:]
     pre, refs = refs[:with_pre], refs[with_pre:]
     lineP_ref, lineF_ref, start_ref, *outs, pre_ref = refs
     if with_pre > 2:
@@ -374,23 +373,17 @@
     def hops(value, width, first=True):
         out = []
         for j in range(width):
-            to = {}
+            to = {(g, i): (g, i ^ 1) for g in range(lines) for i in range(places)}
             for block in range(0 if first else 2 * width, 2 * width if first else lines, 2 * width):
                 source, target = block + width - 1, block + width + j
-                back = target
-                to[source], to[target] = target, source
-                if back != target:
-                    to[target], to[back] = back, source
-            if j < width - 1:
-                at = [2 * head + core for head in heads for core in range(2)]
-                pairs = [(s * places + i, t * places + i) for s, t in to.items() if s < t for i in at]
-                out.append(lax.ppermute(value, ("rx", "ry"), pairs))
-                continue
-            pairs = []
-            for g in range(lines):
-                for i in range(places):
-                    at = to.get(g) if i // 2 in heads else None
-                    pairs.append((g * places + i, g * places + (i ^ 1) if at is None else at * places + i))
+                for head in heads:
+                    end = head - 1 if head == heads[0] else head + 1
+                    for core in range(2):
+                        i, k = 2 * head + core, 2 * end + core
+                        to[source, i], to[target, i] = (target, i), (source, i)
+            if first and width > 1 and j == width - 1:
+                to = {at: there for at, there in to.items() if at[0] == width - 1 and there[0] != at[0]}
+            pairs = [(g * places + i, h * places + k) for (g, i), (h, k) in to.items()]
             out.append(lax.ppermute(value, ("rx", "ry"), pairs))
         return out
 
@@ -430,38 +423,43 @@
         [pltpu.VMEM((chips, b, b), F32)],
     )(chip_map, cuts[0], *gathered, *swapped)
     lineP, line_map = call(
-        functools.partial(line_map_kernel, heads, chips), [halved(chips, 2, b, b), (b // 2 + part, b)], [pltpu.VMEM((b, b), F32)], cost=SHADOW
-    )(steps, line_state)
-
-    total_map, total_state, pre, late = line_map, line_state, [], False
+        functools.partial(line_map_kernel, heads, chips), [halved(chips, 2, b, b), (b // 2, b)], [pltpu.VMEM((b, b), F32)], cost=SHADOW
+    )(steps)
+
+    total_map, total_state, other_state, pre, late = line_map, line_state, line_state, [], False
     width, states = 1, []
     while width < lines:
         last = 2 * width >= lines
         if width > 1:
             total_state, *more = call(
-                functools.partial(total_kernel, not last), [(part, b)] + [(b // 2 + part, b), (b, b)] * (not last), cost=SHADOW
+                functools.partial(total_kernel, not last), [(part, b)] + [(b // 2, b), (part, b), (b, b)] * (not last), cost=SHADOW
             )(*pre[: 2 - last], lineP, line_state)
-            total_map = more and more[0]
+            total_map, other_state = more[:2] if more else (None, None)
         states = hops(total_state, width)
         if last:
             break
-        maps = hops(total_map, width, first=False)
+        halves = hops(total_map, width, first=False)
+        maps = hops(other_state, width, first=False)
         late = width == 1 and 4 * width >= lines
         if not late:
-            maps = [call(whole_kernel, [(b + part, b)])(value, swap(value))[0] for value in maps]
+            maps = [
+                call(whole_kernel, [(b + part, b)])(mine, state, swap(mine))[0]
+                for mine, state in zip(halves, maps, strict=True)
+            ]
         if width == 1:
             pre = [*states, *maps]
         else:
             pre = call(functools.partial(prefix_kernel, width), [(part, b), (b + part, b)])(*states, *maps, *pre)
         width *= 2
     if late:
-        pre[1], _ = lax.optimization_barrier((pre[1], total_state))
-        pre += [swap(piece) for piece in call(pieces_kernel, [(b // 4, b)] * 2, cost=1)(pre[1])]
+        mine, _ = lax.optimization_barrier((halves[0], total_state))
+        pieces = call(pieces_kernel, [(b // 4, b)] * 2, cost=1)(mine)
+        pre = [pre[0], mine, pre[1], *[swap(piece) for piece in pieces]]
     near, far = range(max(chips // 2, 1)), range(max(chips // 2, 1), chips)
     start, *later = call(
         functools.partial(start_kernel, width, len(states), len(pre), far), [(part, b)] * (1 + len(far)),
         [pltpu.VMEM((b + part, b), F32)],
-    )(*states, *pre, lineP, lineF)
+    )(*states[::-1], *pre, lineP, lineF)
     entering = call(functools.partial(enter_kernel, near), [(part, b)] * len(near), cost=SHADOW)(start, lineP, lineF)
     entering = [*entering, *later]
     parts = [entering[0]] + [from_heads(entering[d], d) for d in range(1, chips)]

time: 44.1 us -> 43.7 us (level)
  waiting for transfers between devices: 13.5 us -> 12.6 us
  starting transfers between devices: 22.4 us -> 23.2 us
    ppermute x10, starting transfers between devices: 6.96 us -> 8.32 us  [swap(): return lax.ppermute(value, 'ry', [(i, i ^ 1) for i in range(places)])]
    ppermute x3, waiting for transfers between devices: 2.29 us -> 1.31 us  [from_heads(): return lax.ppermute(value, 'ry', filled([(h, h ^ d) for h in heads], chips))]
    ppermute x3, starting transfers between devices: 8.41 us -> 7.69 us  [from_heads(): return lax.ppermute(value, 'ry', filled([(h, h ^ d) for h in heads], chips))]
    ppermute x4 -> x5, starting transfers between devices: 3.36 us -> 3.56 us  [hops(): out.append(lax.ppermute(value, ('rx', 'ry'), pairs))]
  transfers between devices with their start and end apart: 21 -> 22, of which waited for: 12 -> 10; matrix products, arithmetic and copies ran while one was open for 0% -> 0% of each run, Pallas kernels for 6% -> 6%
where the time goes in v6:
time: 43.7 us; the launch traced here: 43.3 us
  starting transfers between devices  23.2 us (53%)
  waiting for transfers between devices  12.6 us (29%)
  Pallas kernels  6.78 us (16%)
  between operations  0.77 us (2%)
    ppermute x10, starting transfers between devices, swap(): return lax.ppermute(value, 'ry', [(i, i ^ 1) for i in range(places)])  8.32 us
    ppermute x3, starting transfers between devices, from_heads(): return lax.ppermute(value, 'ry', filled([(h, h ^ d) for h in heads], chips))  7.69 us
    pallas_call x12, Pallas kernels, run(): pl.pallas_call(kernel, in_specs=specs, out_specs=[out_spec] * len(outs),...  6.78 us
    ppermute x3, waiting for transfers between devices, to_heads(): return lax.ppermute(value, 'ry', filled([(h ^ d, h) for h in heads], chips))  5.7 us
    ppermute x10, waiting for transfers between devices, swap(): return lax.ppermute(value, 'ry', [(i, i ^ 1) for i in range(places)])  4.75 us
    ppermute x5, starting transfers between devices, hops(): out.append(lax.ppermute(value, ('rx', 'ry'), pairs))  3.56 us
    ppermute x3, starting transfers between devices, to_heads(): return lax.ppermute(value, 'ry', filled([(h ^ d, h) for h in heads], chips))  3.14 us
    ppermute x3, waiting for transfers between devices, from_heads(): return lax.ppermute(value, 'ry', filled([(h, h ^ d) for h in heads], chips))  1.31 us
  transfers between devices with their start and end apart: 22, of which 10 were waited for; matrix products, arithmetic and copies ran while one was open for 0% of the time, Pallas kernels for 6%

profile of v6, /device:TPU:7, one launch (start us, length us, event | category | flops | bytes accessed | tf_op | source)
XLA Modules:
  0.0 43.3 jit_solution(3252894451525948327)
XLA Ops:
  0.6 1.8 %shard_map.41 = (f32[256,640]{1,0:T(8,128)S(1)}, f32[256,640]{1,0:T(8,128)S(1)}, f32[1,256,640]{2,1,0:T(8,128)S(1)}) custom-call(f32[2,256,256]{2,1,0:T(8,128)} %a_ref.1, f32[2,256,384]{2,1,0:T(8,128)} %f_ref.1), custom_call_target="tpu_custom_call" | custom-call | tf_op jit(solution)/shard_map/pallas_call | solution.py:34
  2.5 0.7 %collective-permute-start = (f32[256,640]{1,0:T(8,128)S(1)}, f32[256,640]{1,0:T(8,128)S(1)}, u32[]{:S(2)}, u32[]{:S(2)}) collective-permute-start(f32[256,640]{1,0:T(8,128)S(1)} %get-tuple-element.41.own_ref), channel_id=1, source_target_pairs={{0,1},{1,0},{2,3},{3,2},{4,5},{5,4},{6,7},{7,6},{8,9},{9,8},{10,11... | collective-permute-start | bytes 1966088 | tf_op jit(solution)/shard_map/ppermute | solution.py:365
  3.2 1.7 %collective-permute-done.other_ref = f32[256,640]{1,0:T(8,128)S(1)} collective-permute-done((f32[256,640]{1,0:T(8,128)S(1)}, f32[256,640]{1,0:T(8,128)S(1)}, u32[]{:S(2)}, u32[]{:S(2)}) %collective-permute-start) | collective-permute-done | bytes 655392 | tf_op jit(solution)/shard_map/ppermute | solution.py:365
  4.9 0.6 %shard_map.42 = (f32[256,256]{1,0:T(8,128)S(1)}, f32[384,256]{1,0:T(8,128)S(1)}, f32[224,256]{1,0:T(8,128)S(1)}) custom-call(f32[256,640]{1,0:T(8,128)S(1)} %get-tuple-element.41.own_ref, f32[256,640]{1,0:T(8,128)S(1)} %collective-permute-done.other_ref), custom_call_target="tpu_custom_call" | custom-call | tf_op jit(solution)/shard_map/pallas_call | solution.py:34
  5.6 2.3 %collective-permute-start.2 = (f32[224,256]{1,0:T(8,128)S(1)}, f32[224,256]{1,0:T(8,128)S(1)}, u32[]{:S(2)}, u32[]{:S(2)}) collective-permute-start(f32[224,256]{1,0:T(8,128)S(1)} %get-tuple-element.51), channel_id=1, source_target_pairs={{6,2},{7,3},{0,4},{1,5},{2,0},{3,1},{4,6},{5,7},{14,10},{15,11},{8... | collective-permute-start | bytes 688136 | tf_op jit(solution)/shard_map/ppermute | solution.py:368
  8.0 0.7 %collective-permute-start.3 = (f32[224,256]{1,0:T(8,128)S(1)}, f32[224,256]{1,0:T(8,128)S(1)}, u32[]{:S(2)}, u32[]{:S(2)}) collective-permute-start(f32[224,256]{1,0:T(8,128)S(1)} %get-tuple-element.53), channel_id=1, source_target_pairs={{4,2},{5,3},{2,4},{3,5},{0,1},{1,0},{6,7},{7,6},{12,10},{13,11},{1... | collective-permute-start | bytes 688136 | tf_op jit(solution)/shard_map/ppermute | solution.py:368
  8.7 1.0 %shard_map.44 = (bf16[2,2,256,256]{3,2,1,0:T(8,128)(2,1)S(1)}, f32[2,256,384]{2,1,0:T(8,128)S(1)}) custom-call(f32[256,640]{1,0:T(8,128)S(1)} %collective-permute-done.other_ref, f32[256,640]{1,0:T(8,128)S(1)} %get-tuple-element.67.first_ref, f32[1,256,640]{2,1,0:T(8,128)S(1)} %get-tuple-element.48.rest_ref), custom_call_target="tpu_custom_call" | custom-call | flops 3000000000 | tf_op jit(solution)/shard_map/pallas_call | solution.py:34
  9.7 2.8 %collective-permute-done.2.refs_3_ = f32[224,256]{1,0:T(8,128)S(1)} collective-permute-done((f32[224,256]{1,0:T(8,128)S(1)}, f32[224,256]{1,0:T(8,128)S(1)}, u32[]{:S(2)}, u32[]{:S(2)}) %collective-permute-start.2) | collective-permute-done | bytes 229408 | tf_op jit(solution)/shard_map/ppermute | solution.py:368
  12.6 2.0 %collective-permute-start.5 = (f32[224,256]{1,0:T(8,128)S(1)}, f32[224,256]{1,0:T(8,128)S(1)}, u32[]{:S(2)}, u32[]{:S(2)}) collective-permute-start(f32[224,256]{1,0:T(8,128)S(1)} %collective-permute-done.2.refs_3_), channel_id=1, source_target_pairs={{0,1},{1,0},{2,3},{3,2},{4,5},{5,4},{6,7},{7,6},{8,9},{9,8},{10,11... | collective-permute-start | bytes 688136 | tf_op jit(solution)/shard_map/ppermute | solution.py:365
  14.6 2.9 %collective-permute-done.1.refs_2_ = f32[224,256]{1,0:T(8,128)S(1)} collective-permute-done((f32[224,256]{1,0:T(8,128)S(1)}, f32[224,256]{1,0:T(8,128)S(1)}, u32[]{:S(2)}, u32[]{:S(2)}) %collective-permute-start.1) | collective-permute-done | bytes 229408 | tf_op jit(solution)/shard_map/ppermute | solution.py:368
  17.5 1.2 %collective-permute-start.4 = (f32[224,256]{1,0:T(8,128)S(1)}, f32[224,256]{1,0:T(8,128)S(1)}, u32[]{:S(2)}, u32[]{:S(2)}) collective-permute-start(f32[224,256]{1,0:T(8,128)S(1)} %collective-permute-done.1.refs_2_), channel_id=1, source_target_pairs={{0,1},{1,0},{2,3},{3,2},{4,5},{5,4},{6,7},{7,6},{8,9},{9,8},{10,11... | collective-permute-start | bytes 688136 | tf_op jit(solution)/shard_map/ppermute | solution.py:365
  20.2 2.2 %collective-permute-start.11 = (f32[96,256]{1,0:T(8,128)S(1)}, f32[96,256]{1,0:T(8,128)S(1)}, u32[]{:S(2)}, u32[]{:S(2)}) collective-permute-start(f32[96,256]{1,0:T(8,128)S(1)} %get-tuple-element.55.refs_2_), channel_id=1, source_target_pairs={{0,1},{1,0},{2,3},{3,2},{4,5},{5,4},{6,7},{7,6},{8,9},{9,8},{10,11... | collective-permute-start | bytes 294920 | tf_op jit(solution)/shard_map/ppermute | solution.py:387
  22.9 0.8 %collective-permute-done.7.refs_0_.refs_2_ = f32[96,256]{1,0:T(8,128)S(1)} collective-permute-done((f32[96,256]{1,0:T(8,128)S(1)}, f32[96,256]{1,0:T(8,128)S(1)}, u32[]{:S(2)}, u32[]{:S(2)}) %collective-permute-start.7) | collective-permute-done | bytes 98336 | tf_op jit(solution)/shard_map/ppermute | solution.py:387
  24.1 0.7 %collective-permute-start.8 = (f32[96,256]{1,0:T(8,128)S(1)}, f32[96,256]{1,0:T(8,128)S(1)}, u32[]{:S(2)}, u32[]{:S(2)}) collective-permute-start(f32[96,256]{1,0:T(8,128)S(1)} %shard_map.47), channel_id=1, source_target_pairs={{10,26},{11,27},{12,28},{13,29}} | collective-permute-start | bytes 294920 | tf_op jit(solution)/shard_map/ppermute | solution.py:387
  25.4 0.7 %collective-permute-done.12.refs_5_ = f32[64,256]{1,0:T(8,128)S(1)} collective-permute-done((f32[64,256]{1,0:T(8,128)S(1)}, f32[64,256]{1,0:T(8,128)S(1)}, u32[]{:S(2)}, u32[]{:S(2)}) %collective-permute-start.12) | collective-permute-done | bytes 65568 | tf_op jit(solution)/shard_map/ppermute | solution.py:365
  26.5 0.7 %shard_map.49 = (f32[96,256]{1,0:T(8,128)S(1)}, f32[96,256]{1,0:T(8,128)S(1)}, f32[96,256]{1,0:T(8,128)S(1)}) custom-call(f32[96,256]{1,0:T(8,128)S(1)} %collective-permute-done.8.refs_0_, f32[96,256]{1,0:T(8,128)S(1)} %collective-permute-done.9.refs_1_, f32[96,256]{1,0:T(8,128)S(1)} %collective-permute-done.7.refs_0_.refs_2_, ...), custom_call_target="tpu_custom_call" | custom-call | tf_op jit(solution)/shard_map/pallas_call | solution.py:34
  27.2 6.3 %collective-permute-start.17 = (f32[96,256]{1,0:T(8,128)S(1)}, f32[96,256]{1,0:T(8,128)S(1)}, u32[]{:S(2)}, u32[]{:S(2)}) collective-permute-start(f32[96,256]{1,0:T(8,128)S(1)} %get-tuple-element.71), channel_id=1, source_target_pairs={{2,6},{3,7},{4,0},{5,1},{0,2},{1,3},{6,4},{7,5},{10,14},{11,15},{1... | collective-permute-start | bytes 294920 | tf_op jit(solution)/shard_map/ppermute | solution.py:371
  33.5 1.3 %collective-permute-start.19 = (f32[96,256]{1,0:T(8,128)S(1)}, f32[96,256]{1,0:T(8,128)S(1)}, u32[]{:S(2)}, u32[]{:S(2)}) collective-permute-start(f32[96,256]{1,0:T(8,128)S(1)} %get-tuple-element.73), channel_id=1, source_target_pairs={{2,4},{3,5},{4,2},{5,3},{0,1},{1,0},{6,7},{7,6},{10,12},{11,13},{1... | collective-permute-start | bytes 294920 | tf_op jit(solution)/shard_map/ppermute | solution.py:371
  35.1 1.0 %collective-permute-start.16 = (f32[96,256]{1,0:T(8,128)S(1)}, f32[96,256]{1,0:T(8,128)S(1)}, u32[]{:S(2)}, u32[]{:S(2)}) collective-permute-start(f32[96,256]{1,0:T(8,128)S(1)} %get-tuple-element.64.refs_0_), channel_id=1, source_target_pairs={{0,1},{1,0},{2,3},{3,2},{4,5},{5,4},{6,7},{7,6},{8,9},{9,8},{10,11... | collective-permute-start | bytes 294920 | tf_op jit(solution)/shard_map/ppermute | solution.py:365
  36.6 2.1 %collective-permute-start.18 = (f32[96,256]{1,0:T(8,128)S(1)}, f32[96,256]{1,0:T(8,128)S(1)}, u32[]{:S(2)}, u32[]{:S(2)}) collective-permute-start(f32[96,256]{1,0:T(8,128)S(1)} %collective-permute-done.17.refs_2_), channel_id=1, source_target_pairs={{0,1},{1,0},{2,3},{3,2},{4,5},{5,4},{6,7},{7,6},{8,9},{9,8},{10,11... | collective-permute-start | bytes 294920 | tf_op jit(solution)/shard_map/ppermute | solution.py:365
  38.7 1.3 %collective-permute-done.14.refs_1_ = f32[96,256]{1,0:T(8,128)S(1)} collective-permute-done((f32[96,256]{1,0:T(8,128)S(1)}, f32[96,256]{1,0:T(8,128)S(1)}, u32[]{:S(2)}, u32[]{:S(2)}) %collective-permute-start.14) | collective-permute-done | bytes 98336 | tf_op jit(solution)/shard_map/ppermute | solution.py:371
  40.0 0.7 %collective-permute-start.21 = (f32[96,256]{1,0:T(8,128)S(1)}, f32[96,256]{1,0:T(8,128)S(1)}, u32[]{:S(2)}, u32[]{:S(2)}) collective-permute-start(f32[96,256]{1,0:T(8,128)S(1)} %collective-permute-done.14.refs_1_), channel_id=1, source_target_pairs={{0,1},{1,0},{2,3},{3,2},{4,5},{5,4},{6,7},{7,6},{8,9},{9,8},{10,11... | collective-permute-start | bytes 294920 | tf_op jit(solution)/shard_map/ppermute | solution.py:365
  40.7 0.9 %collective-permute-done.21.refs_5_ = f32[96,256]{1,0:T(8,128)S(1)} collective-permute-done((f32[96,256]{1,0:T(8,128)S(1)}, f32[96,256]{1,0:T(8,128)S(1)}, u32[]{:S(2)}, u32[]{:S(2)}) %collective-permute-start.21) | collective-permute-done | bytes 98336 | tf_op jit(solution)/shard_map/ppermute | solution.py:365
  41.6 1.7 %shard_map.52 = (f32[2,256,384]{2,1,0:T(8,128)}, f32[2,256,384]{2,1,0:T(8,128)}) custom-call(f32[96,256]{1,0:T(8,128)S(1)} %get-tuple-element.64.refs_0_, f32[96,256]{1,0:T(8,128)S(1)} %collective-permute-done.14.refs_1_, f32[96,256]{1,0:T(8,128)S(1)} %collective-permute-done.17.refs_2_, f32[96,256]{1,0:T(8,128)S(1)} %collective-permute-done.19.refs_3_, ...), custom_call_target="tpu_custom_call" | custom-call | tf_op jit(solution)/shard_map/pallas_call | solution.py:34
  (32 shorter events, 4.3 us)
Async XLA Ops:
  2.5 2.5 %collective-permute-start = (f32[256,640]{1,0:T(8,128)S(1)}, f32[256,640]{1,0:T(8,128)S(1)}, u32[]{:S(2)}, u32[]{:S(2)}) collective-permute-start(f32[256,640]{1,0:T(8,128)S(1)} %get-tuple-element.41.own_ref), channel_id=1, source_target_pairs={{0,1},{1,0},{2,3},{3,2},{4,5},{5,4},{6,7},{7,6},{8,9},{9,8},{10,11... | collective-permute-start | bytes 1966088 | tf_op jit(solution)/shard_map/ppermute | solution.py:365
  5.6 7.0 %collective-permute-start.2 = (f32[224,256]{1,0:T(8,128)S(1)}, f32[224,256]{1,0:T(8,128)S(1)}, u32[]{:S(2)}, u32[]{:S(2)}) collective-permute-start(f32[224,256]{1,0:T(8,128)S(1)} %get-tuple-element.51), channel_id=1, source_target_pairs={{6,2},{7,3},{0,4},{1,5},{2,0},{3,1},{4,6},{5,7},{14,10},{15,11},{8... | collective-permute-start | bytes 688136 | tf_op jit(solution)/shard_map/ppermute | solution.py:368
  7.9 9.5 %collective-permute-start.1 = (f32[224,256]{1,0:T(8,128)S(1)}, f32[224,256]{1,0:T(8,128)S(1)}, u32[]{:S(2)}, u32[]{:S(2)}) collective-permute-start(f32[224,256]{1,0:T(8,128)S(1)} %get-tuple-element.45), channel_id=1, source_target_pairs={{0,2},{1,3},{6,4},{7,5},{2,0},{3,1},{4,6},{5,7},{8,10},{9,11},{14,... | collective-permute-start | bytes 688136 | tf_op jit(solution)/shard_map/ppermute | solution.py:368
  8.0 10.7 %collective-permute-start.3 = (f32[224,256]{1,0:T(8,128)S(1)}, f32[224,256]{1,0:T(8,128)S(1)}, u32[]{:S(2)}, u32[]{:S(2)}) collective-permute-start(f32[224,256]{1,0:T(8,128)S(1)} %get-tuple-element.53), channel_id=1, source_target_pairs={{4,2},{5,3},{2,4},{3,5},{0,1},{1,0},{6,7},{7,6},{12,10},{13,11},{1... | collective-permute-start | bytes 688136 | tf_op jit(solution)/shard_map/ppermute | solution.py:368
  12.6 6.7 %collective-permute-start.5 = (f32[224,256]{1,0:T(8,128)S(1)}, f32[224,256]{1,0:T(8,128)S(1)}, u32[]{:S(2)}, u32[]{:S(2)}) collective-permute-start(f32[224,256]{1,0:T(8,128)S(1)} %collective-permute-done.2.refs_3_), channel_id=1, source_target_pairs={{0,1},{1,0},{2,3},{3,2},{4,5},{5,4},{6,7},{7,6},{8,9},{9,8},{10,11... | collective-permute-start | bytes 688136 | tf_op jit(solution)/shard_map/ppermute | solution.py:365
  17.5 2.3 %collective-permute-start.4 = (f32[224,256]{1,0:T(8,128)S(1)}, f32[224,256]{1,0:T(8,128)S(1)}, u32[]{:S(2)}, u32[]{:S(2)}) collective-permute-start(f32[224,256]{1,0:T(8,128)S(1)} %collective-permute-done.1.refs_2_), channel_id=1, source_target_pairs={{0,1},{1,0},{2,3},{3,2},{4,5},{5,4},{6,7},{7,6},{8,9},{9,8},{10,11... | collective-permute-start | bytes 688136 | tf_op jit(solution)/shard_map/ppermute | solution.py:365
  18.7 1.5 %collective-permute-start.6 = (f32[224,256]{1,0:T(8,128)S(1)}, f32[224,256]{1,0:T(8,128)S(1)}, u32[]{:S(2)}, u32[]{:S(2)}) collective-permute-start(f32[224,256]{1,0:T(8,128)S(1)} %collective-permute-done.3.refs_4_), channel_id=1, source_target_pairs={{0,1},{1,0},{2,3},{3,2},{4,5},{5,4},{6,7},{7,6},{8,9},{9,8},{10,11... | collective-permute-start | bytes 688136 | tf_op jit(solution)/shard_map/ppermute | solution.py:365
  18.7 17.4 %collective-permute-start.15 = (f32[256,640]{1,0:T(8,128)S(1)}, f32[256,640]{1,0:T(8,128)S(1)}, u32[]{:S(2)}, u32[]{:S(2)}) collective-permute-start(f32[256,640]{1,0:T(8,128)S(1)} %get-tuple-element.67.first_ref), channel_id=1, source_target_pairs={{0,31},{1,0},{2,1},{3,2},{4,3},{5,4},{6,5},{7,6},{8,7},{9,8},{10,9... | collective-permute-start | bytes 1966088 | tf_op jit(solution)/shard_map/ppermute | solution.py:419
  20.2 5.0 %collective-permute-start.11 = (f32[96,256]{1,0:T(8,128)S(1)}, f32[96,256]{1,0:T(8,128)S(1)}, u32[]{:S(2)}, u32[]{:S(2)}) collective-permute-start(f32[96,256]{1,0:T(8,128)S(1)} %get-tuple-element.55.refs_2_), channel_id=1, source_target_pairs={{0,1},{1,0},{2,3},{3,2},{4,5},{5,4},{6,7},{7,6},{8,9},{9,8},{10,11... | collective-permute-start | bytes 294920 | tf_op jit(solution)/shard_map/ppermute | solution.py:387
  22.4 1.3 %collective-permute-start.7 = (f32[96,256]{1,0:T(8,128)S(1)}, f32[96,256]{1,0:T(8,128)S(1)}, u32[]{:S(2)}, u32[]{:S(2)}) collective-permute-start(f32[96,256]{1,0:T(8,128)S(1)} %get-tuple-element.55.refs_2_), channel_id=1, source_target_pairs={{0,1},{1,0},{2,10},{3,11},{4,12},{5,13},{6,7},{7,6},{8,9},{9,8},{1... | collective-permute-start | bytes 294920 | tf_op jit(solution)/shard_map/ppermute | solution.py:387
  22.4 2.3 %collective-permute-start.10 = (f32[128,256]{1,0:T(8,128)S(1)}, f32[128,256]{1,0:T(8,128)S(1)}, u32[]{:S(2)}, u32[]{:S(2)}) collective-permute-start(f32[128,256]{1,0:T(8,128)S(1)} %get-tuple-element.58), channel_id=1, source_target_pairs={{0,1},{1,0},{2,3},{3,2},{4,5},{5,4},{6,7},{7,6},{8,9},{9,8},{10,11... | collective-permute-start | bytes 393224 | tf_op jit(solution)/shard_map/ppermute | solution.py:387
  23.9 2.6 %collective-permute-start.9 = (f32[96,256]{1,0:T(8,128)S(1)}, f32[96,256]{1,0:T(8,128)S(1)}, u32[]{:S(2)}, u32[]{:S(2)}) collective-permute-start(f32[96,256]{1,0:T(8,128)S(1)} %shard_map.47), channel_id=1, source_target_pairs={{0,1},{1,0},{2,3},{3,2},{4,5},{5,4},{6,7},{7,6},{8,9},{9,8},{10,18... | collective-permute-start | bytes 294920 | tf_op jit(solution)/shard_map/ppermute | solution.py:387
  24.1 2.4 %collective-permute-start.8 = (f32[96,256]{1,0:T(8,128)S(1)}, f32[96,256]{1,0:T(8,128)S(1)}, u32[]{:S(2)}, u32[]{:S(2)}) collective-permute-start(f32[96,256]{1,0:T(8,128)S(1)} %shard_map.47), channel_id=1, source_target_pairs={{10,26},{11,27},{12,28},{13,29}} | collective-permute-start | bytes 294920 | tf_op jit(solution)/shard_map/ppermute | solution.py:387
  24.8 1.3 %collective-permute-start.12 = (f32[64,256]{1,0:T(8,128)S(1)}, f32[64,256]{1,0:T(8,128)S(1)}, u32[]{:S(2)}, u32[]{:S(2)}) collective-permute-start(f32[64,256]{1,0:T(8,128)S(1)} %get-tuple-element.60), channel_id=1, source_target_pairs={{0,1},{1,0},{2,3},{3,2},{4,5},{5,4},{6,7},{7,6},{8,9},{9,8},{10,11... | collective-permute-start | bytes 196616 | tf_op jit(solution)/shard_map/ppermute | solution.py:365
  25.2 1.3 %collective-permute-start.13 = (f32[64,256]{1,0:T(8,128)S(1)}, f32[64,256]{1,0:T(8,128)S(1)}, u32[]{:S(2)}, u32[]{:S(2)}) collective-permute-start(f32[64,256]{1,0:T(8,128)S(1)} %get-tuple-element.61), channel_id=1, source_target_pairs={{0,1},{1,0},{2,3},{3,2},{4,5},{5,4},{6,7},{7,6},{8,9},{9,8},{10,11... | collective-permute-start | bytes 196616 | tf_op jit(solution)/shard_map/ppermute | solution.py:365
  27.2 9.4 %collective-permute-start.17 = (f32[96,256]{1,0:T(8,128)S(1)}, f32[96,256]{1,0:T(8,128)S(1)}, u32[]{:S(2)}, u32[]{:S(2)}) collective-permute-start(f32[96,256]{1,0:T(8,128)S(1)} %get-tuple-element.71), channel_id=1, source_target_pairs={{2,6},{3,7},{4,0},{5,1},{0,2},{1,3},{6,4},{7,5},{10,14},{11,15},{1... | collective-permute-start | bytes 294920 | tf_op jit(solution)/shard_map/ppermute | solution.py:371
  33.5 3.1 %collective-permute-start.19 = (f32[96,256]{1,0:T(8,128)S(1)}, f32[96,256]{1,0:T(8,128)S(1)}, u32[]{:S(2)}, u32[]{:S(2)}) collective-permute-start(f32[96,256]{1,0:T(8,128)S(1)} %get-tuple-element.73), channel_id=1, source_target_pairs={{2,4},{3,5},{4,2},{5,3},{0,1},{1,0},{6,7},{7,6},{10,12},{11,13},{1... | collective-permute-start | bytes 294920 | tf_op jit(solution)/shard_map/ppermute | solution.py:371
  35.0 5.0 %collective-permute-start.14 = (f32[96,256]{1,0:T(8,128)S(1)}, f32[96,256]{1,0:T(8,128)S(1)}, u32[]{:S(2)}, u32[]{:S(2)}) collective-permute-start(f32[96,256]{1,0:T(8,128)S(1)} %get-tuple-element.65), channel_id=1, source_target_pairs={{2,0},{3,1},{4,6},{5,7},{0,2},{1,3},{6,4},{7,5},{10,8},{11,9},{12,... | collective-permute-start | bytes 294920 | tf_op jit(solution)/shard_map/ppermute | solution.py:371
  35.1 4.9 %collective-permute-start.16 = (f32[96,256]{1,0:T(8,128)S(1)}, f32[96,256]{1,0:T(8,128)S(1)}, u32[]{:S(2)}, u32[]{:S(2)}) collective-permute-start(f32[96,256]{1,0:T(8,128)S(1)} %get-tuple-element.64.refs_0_), channel_id=1, source_target_pairs={{0,1},{1,0},{2,3},{3,2},{4,5},{5,4},{6,7},{7,6},{8,9},{9,8},{10,11... | collective-permute-start | bytes 294920 | tf_op jit(solution)/shard_map/ppermute | solution.py:365
  36.6 3.4 %collective-permute-start.18 = (f32[96,256]{1,0:T(8,128)S(1)}, f32[96,256]{1,0:T(8,128)S(1)}, u32[]{:S(2)}, u32[]{:S(2)}) collective-permute-start(f32[96,256]{1,0:T(8,128)S(1)} %collective-permute-done.17.refs_2_), channel_id=1, source_target_pairs={{0,1},{1,0},{2,3},{3,2},{4,5},{5,4},{6,7},{7,6},{8,9},{9,8},{10,11... | collective-permute-start | bytes 294920 | tf_op jit(solution)/shard_map/ppermute | solution.py:365
  38.7 1.3 %collective-permute-start.20 = (f32[96,256]{1,0:T(8,128)S(1)}, f32[96,256]{1,0:T(8,128)S(1)}, u32[]{:S(2)}, u32[]{:S(2)}) collective-permute-start(f32[96,256]{1,0:T(8,128)S(1)} %collective-permute-done.19.refs_3_), channel_id=1, source_target_pairs={{0,1},{1,0},{2,3},{3,2},{4,5},{5,4},{6,7},{7,6},{8,9},{9,8},{10,11... | collective-permute-start | bytes 294920 | tf_op jit(solution)/shard_map/ppermute | solution.py:365
  40.0 1.6 %collective-permute-start.21 = (f32[96,256]{1,0:T(8,128)S(1)}, f32[96,256]{1,0:T(8,128)S(1)}, u32[]{:S(2)}, u32[]{:S(2)}) collective-permute-start(f32[96,256]{1,0:T(8,128)S(1)} %collective-permute-done.14.refs_1_), channel_id=1, source_target_pairs={{0,1},{1,0},{2,3},{3,2},{4,5},{5,4},{6,7},{7,6},{8,9},{9,8},{10,11... | collective-permute-start | bytes 294920 | tf_op jit(solution)/shard_map/ppermute | solution.py:365

commit v7 on v6

--- a/solution.py
+++ b/solution.py
@@ -327,21 +327,24 @@
 
     entering = split(in_ref[...])
     copies = [pltpu.make_async_copy(xs_ref.at[i], x_ref.at[i], sems.at[0, i]) for i in range(n)]
-    copies += [pltpu.make_async_copy(ss_ref.at[i], s_ref.at[i], sems.at[1, i]) for i in range(n)]
+    copies += [pltpu.make_async_copy(ss_ref.at[i], s_ref.at[i], sems.at[1, i]) for i in range(n - 1)]
     for i in range(n):
         xs_ref[i] = product(get(m_ref, i), entering, NT) + c_ref[i]
         copies[i].start()
         if i:
             ss_ref[i - 1] = xs_ref[i] - xs_ref[i - 1]
             copies[n + i - 1].start()
-    ss_ref[n - 1] = product(get(next_ref), entering, NT) + add_ref[...] - xs_ref[n - 1]
-
-    @pl.when(g * lax.axis_size("ry") + 2 * z + core == lax.axis_size("rx") * lax.axis_size("ry") - 1)
-    def _():
-        ss_ref[n - 1] = -xs_ref[n - 1]
-
-    copies[2 * n - 1].start()
-    for copy in copies:
+    last = g * lax.axis_size("ry") + 2 * z + core == lax.axis_size("rx") * lax.axis_size("ry") - 1
+    half = xs_ref.shape[1] // 2
+    ends = []
+    for k in range(2):
+        at = slice(k * half, (k + 1) * half)
+        following = product((next_ref[0, at], next_ref[1, at]), entering, NT) + add_ref[at]
+        ss_ref[n - 1, at] = jnp.where(last, 0.0, following) - xs_ref[n - 1, at]
+        span = pl.ds(k * half, half)
+        ends.append(pltpu.make_async_copy(ss_ref.at[n - 1, span], s_ref.at[n - 1, span], sems.at[1, n - 1 + k]))
+        ends[-1].start()
+    for copy in [*copies[: 2 * n - 1], *ends]:
         copy.wait()
 
 
@@ -481,7 +484,7 @@
                 pltpu.VMEM((r, b), F32),
                 pltpu.VMEM((intervals, b, r), F32),
                 pltpu.VMEM((intervals, b, r), F32),
-                pltpu.SemaphoreType.DMA((2, intervals)),
+                pltpu.SemaphoreType.DMA((2, intervals + 1)),
             ],
             out_spec=HBM,
         )(*parts, *[shared[d] for d in range(chips)], matrices, constants, next_matrix, next_constant)

time: 43.7 us -> 43.7 us (level)
  no operation moved by 1% of the time
where the time goes in v7:
time: 43.7 us; the launch traced here: 43.3 us
  starting transfers between devices  23.2 us (53%)
  waiting for transfers between devices  12.6 us (29%)
  Pallas kernels  6.79 us (16%)
  between operations  0.77 us (2%)
    ppermute x10, starting transfers between devices, swap(): return lax.ppermute(value, 'ry', [(i, i ^ 1) for i in range(places)])  8.32 us
    ppermute x3, starting transfers between devices, from_heads(): return lax.ppermute(value, 'ry', filled([(h, h ^ d) for h in heads], chips))  7.69 us
    pallas_call x12, Pallas kernels, run(): pl.pallas_call(kernel, in_specs=specs, out_specs=[out_spec] * len(outs),...  6.79 us
    ppermute x3, waiting for transfers between devices, to_heads(): return lax.ppermute(value, 'ry', filled([(h ^ d, h) for h in heads], chips))  5.7 us
    ppermute x10, waiting for transfers between devices, swap(): return lax.ppermute(value, 'ry', [(i, i ^ 1) for i in range(places)])  4.75 us
    ppermute x5, starting transfers between devices, hops(): out.append(lax.ppermute(value, ('rx', 'ry'), pairs))  3.56 us
    ppermute x3, starting transfers between devices, to_heads(): return lax.ppermute(value, 'ry', filled([(h ^ d, h) for h in heads], chips))  3.14 us
    ppermute x3, waiting for transfers between devices, from_heads(): return lax.ppermute(value, 'ry', filled([(h, h ^ d) for h in heads], chips))  1.31 us
  transfers between devices with their start and end apart: 22, of which 10 were waited for; matrix products, arithmetic and copies ran while one was open for 0% of the time, Pallas kernels for 6%

profile of v7, /device:TPU:7, one launch (start us, length us, event | category | flops | bytes accessed | tf_op | source)
XLA Modules:
  0.0 43.3 jit_solution(7254100117791163969)
XLA Ops:
  0.6 1.8 %shard_map.41 = (f32[256,640]{1,0:T(8,128)S(1)}, f32[256,640]{1,0:T(8,128)S(1)}, f32[1,256,640]{2,1,0:T(8,128)S(1)}) custom-call(f32[2,256,256]{2,1,0:T(8,128)} %a_ref.1, f32[2,256,384]{2,1,0:T(8,128)} %f_ref.1), custom_call_target="tpu_custom_call" | custom-call | tf_op jit(solution)/shard_map/pallas_call | solution.py:34
  2.5 0.7 %collective-permute-start = (f32[256,640]{1,0:T(8,128)S(1)}, f32[256,640]{1,0:T(8,128)S(1)}, u32[]{:S(2)}, u32[]{:S(2)}) collective-permute-start(f32[256,640]{1,0:T(8,128)S(1)} %get-tuple-element.41.own_ref), channel_id=1, source_target_pairs={{0,1},{1,0},{2,3},{3,2},{4,5},{5,4},{6,7},{7,6},{8,9},{9,8},{10,11... | collective-permute-start | bytes 1966088 | tf_op jit(solution)/shard_map/ppermute | solution.py:368
  3.2 1.7 %collective-permute-done.other_ref = f32[256,640]{1,0:T(8,128)S(1)} collective-permute-done((f32[256,640]{1,0:T(8,128)S(1)}, f32[256,640]{1,0:T(8,128)S(1)}, u32[]{:S(2)}, u32[]{:S(2)}) %collective-permute-start) | collective-permute-done | bytes 655392 | tf_op jit(solution)/shard_map/ppermute | solution.py:368
  4.9 0.6 %shard_map.42 = (f32[256,256]{1,0:T(8,128)S(1)}, f32[384,256]{1,0:T(8,128)S(1)}, f32[224,256]{1,0:T(8,128)S(1)}) custom-call(f32[256,640]{1,0:T(8,128)S(1)} %get-tuple-element.41.own_ref, f32[256,640]{1,0:T(8,128)S(1)} %collective-permute-done.other_ref), custom_call_target="tpu_custom_call" | custom-call | tf_op jit(solution)/shard_map/pallas_call | solution.py:34
  5.6 2.3 %collective-permute-start.2 = (f32[224,256]{1,0:T(8,128)S(1)}, f32[224,256]{1,0:T(8,128)S(1)}, u32[]{:S(2)}, u32[]{:S(2)}) collective-permute-start(f32[224,256]{1,0:T(8,128)S(1)} %get-tuple-element.51), channel_id=1, source_target_pairs={{6,2},{7,3},{0,4},{1,5},{2,0},{3,1},{4,6},{5,7},{14,10},{15,11},{8... | collective-permute-start | bytes 688136 | tf_op jit(solution)/shard_map/ppermute | solution.py:371
  8.0 0.7 %collective-permute-start.3 = (f32[224,256]{1,0:T(8,128)S(1)}, f32[224,256]{1,0:T(8,128)S(1)}, u32[]{:S(2)}, u32[]{:S(2)}) collective-permute-start(f32[224,256]{1,0:T(8,128)S(1)} %get-tuple-element.53), channel_id=1, source_target_pairs={{4,2},{5,3},{2,4},{3,5},{0,1},{1,0},{6,7},{7,6},{12,10},{13,11},{1... | collective-permute-start | bytes 688136 | tf_op jit(solution)/shard_map/ppermute | solution.py:371
  8.7 1.0 %shard_map.44 = (bf16[2,2,256,256]{3,2,1,0:T(8,128)(2,1)S(1)}, f32[2,256,384]{2,1,0:T(8,128)S(1)}) custom-call(f32[256,640]{1,0:T(8,128)S(1)} %collective-permute-done.other_ref, f32[256,640]{1,0:T(8,128)S(1)} %get-tuple-element.67.first_ref, f32[1,256,640]{2,1,0:T(8,128)S(1)} %get-tuple-element.48.rest_ref), custom_call_target="tpu_custom_call" | custom-call | flops 3000000000 | tf_op jit(solution)/shard_map/pallas_call | solution.py:34
  9.7 2.8 %collective-permute-done.2.refs_3_ = f32[224,256]{1,0:T(8,128)S(1)} collective-permute-done((f32[224,256]{1,0:T(8,128)S(1)}, f32[224,256]{1,0:T(8,128)S(1)}, u32[]{:S(2)}, u32[]{:S(2)}) %collective-permute-start.2) | collective-permute-done | bytes 229408 | tf_op jit(solution)/shard_map/ppermute | solution.py:371
  12.6 2.0 %collective-permute-start.5 = (f32[224,256]{1,0:T(8,128)S(1)}, f32[224,256]{1,0:T(8,128)S(1)}, u32[]{:S(2)}, u32[]{:S(2)}) collective-permute-start(f32[224,256]{1,0:T(8,128)S(1)} %collective-permute-done.2.refs_3_), channel_id=1, source_target_pairs={{0,1},{1,0},{2,3},{3,2},{4,5},{5,4},{6,7},{7,6},{8,9},{9,8},{10,11... | collective-permute-start | bytes 688136 | tf_op jit(solution)/shard_map/ppermute | solution.py:368
  14.6 2.9 %collective-permute-done.1.refs_2_ = f32[224,256]{1,0:T(8,128)S(1)} collective-permute-done((f32[224,256]{1,0:T(8,128)S(1)}, f32[224,256]{1,0:T(8,128)S(1)}, u32[]{:S(2)}, u32[]{:S(2)}) %collective-permute-start.1) | collective-permute-done | bytes 229408 | tf_op jit(solution)/shard_map/ppermute | solution.py:371
  17.5 1.2 %collective-permute-start.4 = (f32[224,256]{1,0:T(8,128)S(1)}, f32[224,256]{1,0:T(8,128)S(1)}, u32[]{:S(2)}, u32[]{:S(2)}) collective-permute-start(f32[224,256]{1,0:T(8,128)S(1)} %collective-permute-done.1.refs_2_), channel_id=1, source_target_pairs={{0,1},{1,0},{2,3},{3,2},{4,5},{5,4},{6,7},{7,6},{8,9},{9,8},{10,11... | collective-permute-start | bytes 688136 | tf_op jit(solution)/shard_map/ppermute | solution.py:368
  20.2 2.2 %collective-permute-start.11 = (f32[96,256]{1,0:T(8,128)S(1)}, f32[96,256]{1,0:T(8,128)S(1)}, u32[]{:S(2)}, u32[]{:S(2)}) collective-permute-start(f32[96,256]{1,0:T(8,128)S(1)} %get-tuple-element.55.refs_2_), channel_id=1, source_target_pairs={{0,1},{1,0},{2,3},{3,2},{4,5},{5,4},{6,7},{7,6},{8,9},{9,8},{10,11... | collective-permute-start | bytes 294920 | tf_op jit(solution)/shard_map/ppermute | solution.py:390
  22.9 0.8 %collective-permute-done.7.refs_0_.refs_2_ = f32[96,256]{1,0:T(8,128)S(1)} collective-permute-done((f32[96,256]{1,0:T(8,128)S(1)}, f32[96,256]{1,0:T(8,128)S(1)}, u32[]{:S(2)}, u32[]{:S(2)}) %collective-permute-start.7) | collective-permute-done | bytes 98336 | tf_op jit(solution)/shard_map/ppermute | solution.py:390
  24.1 0.7 %collective-permute-start.8 = (f32[96,256]{1,0:T(8,128)S(1)}, f32[96,256]{1,0:T(8,128)S(1)}, u32[]{:S(2)}, u32[]{:S(2)}) collective-permute-start(f32[96,256]{1,0:T(8,128)S(1)} %shard_map.47), channel_id=1, source_target_pairs={{10,26},{11,27},{12,28},{13,29}} | collective-permute-start | bytes 294920 | tf_op jit(solution)/shard_map/ppermute | solution.py:390
  25.4 0.7 %collective-permute-done.12.refs_5_ = f32[64,256]{1,0:T(8,128)S(1)} collective-permute-done((f32[64,256]{1,0:T(8,128)S(1)}, f32[64,256]{1,0:T(8,128)S(1)}, u32[]{:S(2)}, u32[]{:S(2)}) %collective-permute-start.12) | collective-permute-done | bytes 65568 | tf_op jit(solution)/shard_map/ppermute | solution.py:368
  26.5 0.7 %shard_map.49 = (f32[96,256]{1,0:T(8,128)S(1)}, f32[96,256]{1,0:T(8,128)S(1)}, f32[96,256]{1,0:T(8,128)S(1)}) custom-call(f32[96,256]{1,0:T(8,128)S(1)} %collective-permute-done.8.refs_0_, f32[96,256]{1,0:T(8,128)S(1)} %collective-permute-done.9.refs_1_, f32[96,256]{1,0:T(8,128)S(1)} %collective-permute-done.7.refs_0_.refs_2_, ...), custom_call_target="tpu_custom_call" | custom-call | tf_op jit(solution)/shard_map/pallas_call | solution.py:34
  27.2 6.3 %collective-permute-start.17 = (f32[96,256]{1,0:T(8,128)S(1)}, f32[96,256]{1,0:T(8,128)S(1)}, u32[]{:S(2)}, u32[]{:S(2)}) collective-permute-start(f32[96,256]{1,0:T(8,128)S(1)} %get-tuple-element.71), channel_id=1, source_target_pairs={{2,6},{3,7},{4,0},{5,1},{0,2},{1,3},{6,4},{7,5},{10,14},{11,15},{1... | collective-permute-start | bytes 294920 | tf_op jit(solution)/shard_map/ppermute | solution.py:374
  33.5 1.3 %collective-permute-start.19 = (f32[96,256]{1,0:T(8,128)S(1)}, f32[96,256]{1,0:T(8,128)S(1)}, u32[]{:S(2)}, u32[]{:S(2)}) collective-permute-start(f32[96,256]{1,0:T(8,128)S(1)} %get-tuple-element.73), channel_id=1, source_target_pairs={{2,4},{3,5},{4,2},{5,3},{0,1},{1,0},{6,7},{7,6},{10,12},{11,13},{1... | collective-permute-start | bytes 294920 | tf_op jit(solution)/shard_map/ppermute | solution.py:374
  35.1 1.0 %collective-permute-start.16 = (f32[96,256]{1,0:T(8,128)S(1)}, f32[96,256]{1,0:T(8,128)S(1)}, u32[]{:S(2)}, u32[]{:S(2)}) collective-permute-start(f32[96,256]{1,0:T(8,128)S(1)} %get-tuple-element.64.refs_0_), channel_id=1, source_target_pairs={{0,1},{1,0},{2,3},{3,2},{4,5},{5,4},{6,7},{7,6},{8,9},{9,8},{10,11... | collective-permute-start | bytes 294920 | tf_op jit(solution)/shard_map/ppermute | solution.py:368
  36.6 2.1 %collective-permute-start.18 = (f32[96,256]{1,0:T(8,128)S(1)}, f32[96,256]{1,0:T(8,128)S(1)}, u32[]{:S(2)}, u32[]{:S(2)}) collective-permute-start(f32[96,256]{1,0:T(8,128)S(1)} %collective-permute-done.17.refs_2_), channel_id=1, source_target_pairs={{0,1},{1,0},{2,3},{3,2},{4,5},{5,4},{6,7},{7,6},{8,9},{9,8},{10,11... | collective-permute-start | bytes 294920 | tf_op jit(solution)/shard_map/ppermute | solution.py:368
  38.7 1.3 %collective-permute-done.14.refs_1_ = f32[96,256]{1,0:T(8,128)S(1)} collective-permute-done((f32[96,256]{1,0:T(8,128)S(1)}, f32[96,256]{1,0:T(8,128)S(1)}, u32[]{:S(2)}, u32[]{:S(2)}) %collective-permute-start.14) | collective-permute-done | bytes 98336 | tf_op jit(solution)/shard_map/ppermute | solution.py:374
  40.0 0.7 %collective-permute-start.21 = (f32[96,256]{1,0:T(8,128)S(1)}, f32[96,256]{1,0:T(8,128)S(1)}, u32[]{:S(2)}, u32[]{:S(2)}) collective-permute-start(f32[96,256]{1,0:T(8,128)S(1)} %collective-permute-done.14.refs_1_), channel_id=1, source_target_pairs={{0,1},{1,0},{2,3},{3,2},{4,5},{5,4},{6,7},{7,6},{8,9},{9,8},{10,11... | collective-permute-start | bytes 294920 | tf_op jit(solution)/shard_map/ppermute | solution.py:368
  40.7 0.9 %collective-permute-done.21.refs_5_ = f32[96,256]{1,0:T(8,128)S(1)} collective-permute-done((f32[96,256]{1,0:T(8,128)S(1)}, f32[96,256]{1,0:T(8,128)S(1)}, u32[]{:S(2)}, u32[]{:S(2)}) %collective-permute-start.21) | collective-permute-done | bytes 98336 | tf_op jit(solution)/shard_map/ppermute | solution.py:368
  41.6 1.7 %shard_map.52 = (f32[2,256,384]{2,1,0:T(8,128)}, f32[2,256,384]{2,1,0:T(8,128)}) custom-call(f32[96,256]{1,0:T(8,128)S(1)} %get-tuple-element.64.refs_0_, f32[96,256]{1,0:T(8,128)S(1)} %collective-permute-done.14.refs_1_, f32[96,256]{1,0:T(8,128)S(1)} %collective-permute-done.17.refs_2_, f32[96,256]{1,0:T(8,128)S(1)} %collective-permute-done.19.refs_3_, ...), custom_call_target="tpu_custom_call" | custom-call | tf_op jit(solution)/shard_map/pallas_call | solution.py:34
  (32 shorter events, 4.3 us)
Async XLA Ops:
  2.5 2.5 %collective-permute-start = (f32[256,640]{1,0:T(8,128)S(1)}, f32[256,640]{1,0:T(8,128)S(1)}, u32[]{:S(2)}, u32[]{:S(2)}) collective-permute-start(f32[256,640]{1,0:T(8,128)S(1)} %get-tuple-element.41.own_ref), channel_id=1, source_target_pairs={{0,1},{1,0},{2,3},{3,2},{4,5},{5,4},{6,7},{7,6},{8,9},{9,8},{10,11... | collective-permute-start | bytes 1966088 | tf_op jit(solution)/shard_map/ppermute | solution.py:368
  5.6 7.0 %collective-permute-start.2 = (f32[224,256]{1,0:T(8,128)S(1)}, f32[224,256]{1,0:T(8,128)S(1)}, u32[]{:S(2)}, u32[]{:S(2)}) collective-permute-start(f32[224,256]{1,0:T(8,128)S(1)} %get-tuple-element.51), channel_id=1, source_target_pairs={{6,2},{7,3},{0,4},{1,5},{2,0},{3,1},{4,6},{5,7},{14,10},{15,11},{8... | collective-permute-start | bytes 688136 | tf_op jit(solution)/shard_map/ppermute | solution.py:371
  7.9 9.5 %collective-permute-start.1 = (f32[224,256]{1,0:T(8,128)S(1)}, f32[224,256]{1,0:T(8,128)S(1)}, u32[]{:S(2)}, u32[]{:S(2)}) collective-permute-start(f32[224,256]{1,0:T(8,128)S(1)} %get-tuple-element.45), channel_id=1, source_target_pairs={{0,2},{1,3},{6,4},{7,5},{2,0},{3,1},{4,6},{5,7},{8,10},{9,11},{14,... | collective-permute-start | bytes 688136 | tf_op jit(solution)/shard_map/ppermute | solution.py:371
  8.0 10.7 %collective-permute-start.3 = (f32[224,256]{1,0:T(8,128)S(1)}, f32[224,256]{1,0:T(8,128)S(1)}, u32[]{:S(2)}, u32[]{:S(2)}) collective-permute-start(f32[224,256]{1,0:T(8,128)S(1)} %get-tuple-element.53), channel_id=1, source_target_pairs={{4,2},{5,3},{2,4},{3,5},{0,1},{1,0},{6,7},{7,6},{12,10},{13,11},{1... | collective-permute-start | bytes 688136 | tf_op jit(solution)/shard_map/ppermute | solution.py:371
  12.6 6.7 %collective-permute-start.5 = (f32[224,256]{1,0:T(8,128)S(1)}, f32[224,256]{1,0:T(8,128)S(1)}, u32[]{:S(2)}, u32[]{:S(2)}) collective-permute-start(f32[224,256]{1,0:T(8,128)S(1)} %collective-permute-done.2.refs_3_), channel_id=1, source_target_pairs={{0,1},{1,0},{2,3},{3,2},{4,5},{5,4},{6,7},{7,6},{8,9},{9,8},{10,11... | collective-permute-start | bytes 688136 | tf_op jit(solution)/shard_map/ppermute | solution.py:368
  17.5 2.3 %collective-permute-start.4 = (f32[224,256]{1,0:T(8,128)S(1)}, f32[224,256]{1,0:T(8,128)S(1)}, u32[]{:S(2)}, u32[]{:S(2)}) collective-permute-start(f32[224,256]{1,0:T(8,128)S(1)} %collective-permute-done.1.refs_2_), channel_id=1, source_target_pairs={{0,1},{1,0},{2,3},{3,2},{4,5},{5,4},{6,7},{7,6},{8,9},{9,8},{10,11... | collective-permute-start | bytes 688136 | tf_op jit(solution)/shard_map/ppermute | solution.py:368
  18.7 1.5 %collective-permute-start.6 = (f32[224,256]{1,0:T(8,128)S(1)}, f32[224,256]{1,0:T(8,128)S(1)}, u32[]{:S(2)}, u32[]{:S(2)}) collective-permute-start(f32[224,256]{1,0:T(8,128)S(1)} %collective-permute-done.3.refs_4_), channel_id=1, source_target_pairs={{0,1},{1,0},{2,3},{3,2},{4,5},{5,4},{6,7},{7,6},{8,9},{9,8},{10,11... | collective-permute-start | bytes 688136 | tf_op jit(solution)/shard_map/ppermute | solution.py:368
  18.7 17.4 %collective-permute-start.15 = (f32[256,640]{1,0:T(8,128)S(1)}, f32[256,640]{1,0:T(8,128)S(1)}, u32[]{:S(2)}, u32[]{:S(2)}) collective-permute-start(f32[256,640]{1,0:T(8,128)S(1)} %get-tuple-element.67.first_ref), channel_id=1, source_target_pairs={{0,31},{1,0},{2,1},{3,2},{4,3},{5,4},{6,5},{7,6},{8,7},{9,8},{10,9... | collective-permute-start | bytes 1966088 | tf_op jit(solution)/shard_map/ppermute | solution.py:422
  20.2 5.0 %collective-permute-start.11 = (f32[96,256]{1,0:T(8,128)S(1)}, f32[96,256]{1,0:T(8,128)S(1)}, u32[]{:S(2)}, u32[]{:S(2)}) collective-permute-start(f32[96,256]{1,0:T(8,128)S(1)} %get-tuple-element.55.refs_2_), channel_id=1, source_target_pairs={{0,1},{1,0},{2,3},{3,2},{4,5},{5,4},{6,7},{7,6},{8,9},{9,8},{10,11... | collective-permute-start | bytes 294920 | tf_op jit(solution)/shard_map/ppermute | solution.py:390
  22.4 1.3 %collective-permute-start.7 = (f32[96,256]{1,0:T(8,128)S(1)}, f32[96,256]{1,0:T(8,128)S(1)}, u32[]{:S(2)}, u32[]{:S(2)}) collective-permute-start(f32[96,256]{1,0:T(8,128)S(1)} %get-tuple-element.55.refs_2_), channel_id=1, source_target_pairs={{0,1},{1,0},{2,10},{3,11},{4,12},{5,13},{6,7},{7,6},{8,9},{9,8},{1... | collective-permute-start | bytes 294920 | tf_op jit(solution)/shard_map/ppermute | solution.py:390
  22.4 2.3 %collective-permute-start.10 = (f32[128,256]{1,0:T(8,128)S(1)}, f32[128,256]{1,0:T(8,128)S(1)}, u32[]{:S(2)}, u32[]{:S(2)}) collective-permute-start(f32[128,256]{1,0:T(8,128)S(1)} %get-tuple-element.58), channel_id=1, source_target_pairs={{0,1},{1,0},{2,3},{3,2},{4,5},{5,4},{6,7},{7,6},{8,9},{9,8},{10,11... | collective-permute-start | bytes 393224 | tf_op jit(solution)/shard_map/ppermute | solution.py:390
  23.9 2.6 %collective-permute-start.9 = (f32[96,256]{1,0:T(8,128)S(1)}, f32[96,256]{1,0:T(8,128)S(1)}, u32[]{:S(2)}, u32[]{:S(2)}) collective-permute-start(f32[96,256]{1,0:T(8,128)S(1)} %shard_map.47), channel_id=1, source_target_pairs={{0,1},{1,0},{2,3},{3,2},{4,5},{5,4},{6,7},{7,6},{8,9},{9,8},{10,18... | collective-permute-start | bytes 294920 | tf_op jit(solution)/shard_map/ppermute | solution.py:390
  24.1 2.4 %collective-permute-start.8 = (f32[96,256]{1,0:T(8,128)S(1)}, f32[96,256]{1,0:T(8,128)S(1)}, u32[]{:S(2)}, u32[]{:S(2)}) collective-permute-start(f32[96,256]{1,0:T(8,128)S(1)} %shard_map.47), channel_id=1, source_target_pairs={{10,26},{11,27},{12,28},{13,29}} | collective-permute-start | bytes 294920 | tf_op jit(solution)/shard_map/ppermute | solution.py:390
  24.8 1.3 %collective-permute-start.12 = (f32[64,256]{1,0:T(8,128)S(1)}, f32[64,256]{1,0:T(8,128)S(1)}, u32[]{:S(2)}, u32[]{:S(2)}) collective-permute-start(f32[64,256]{1,0:T(8,128)S(1)} %get-tuple-element.60), channel_id=1, source_target_pairs={{0,1},{1,0},{2,3},{3,2},{4,5},{5,4},{6,7},{7,6},{8,9},{9,8},{10,11... | collective-permute-start | bytes 196616 | tf_op jit(solution)/shard_map/ppermute | solution.py:368
  25.2 1.3 %collective-permute-start.13 = (f32[64,256]{1,0:T(8,128)S(1)}, f32[64,256]{1,0:T(8,128)S(1)}, u32[]{:S(2)}, u32[]{:S(2)}) collective-permute-start(f32[64,256]{1,0:T(8,128)S(1)} %get-tuple-element.61), channel_id=1, source_target_pairs={{0,1},{1,0},{2,3},{3,2},{4,5},{5,4},{6,7},{7,6},{8,9},{9,8},{10,11... | collective-permute-start | bytes 196616 | tf_op jit(solution)/shard_map/ppermute | solution.py:368
  27.2 9.4 %collective-permute-start.17 = (f32[96,256]{1,0:T(8,128)S(1)}, f32[96,256]{1,0:T(8,128)S(1)}, u32[]{:S(2)}, u32[]{:S(2)}) collective-permute-start(f32[96,256]{1,0:T(8,128)S(1)} %get-tuple-element.71), channel_id=1, source_target_pairs={{2,6},{3,7},{4,0},{5,1},{0,2},{1,3},{6,4},{7,5},{10,14},{11,15},{1... | collective-permute-start | bytes 294920 | tf_op jit(solution)/shard_map/ppermute | solution.py:374
  33.5 3.1 %collective-permute-start.19 = (f32[96,256]{1,0:T(8,128)S(1)}, f32[96,256]{1,0:T(8,128)S(1)}, u32[]{:S(2)}, u32[]{:S(2)}) collective-permute-start(f32[96,256]{1,0:T(8,128)S(1)} %get-tuple-element.73), channel_id=1, source_target_pairs={{2,4},{3,5},{4,2},{5,3},{0,1},{1,0},{6,7},{7,6},{10,12},{11,13},{1... | collective-permute-start | bytes 294920 | tf_op jit(solution)/shard_map/ppermute | solution.py:374
  35.0 5.0 %collective-permute-start.14 = (f32[96,256]{1,0:T(8,128)S(1)}, f32[96,256]{1,0:T(8,128)S(1)}, u32[]{:S(2)}, u32[]{:S(2)}) collective-permute-start(f32[96,256]{1,0:T(8,128)S(1)} %get-tuple-element.65), channel_id=1, source_target_pairs={{2,0},{3,1},{4,6},{5,7},{0,2},{1,3},{6,4},{7,5},{10,8},{11,9},{12,... | collective-permute-start | bytes 294920 | tf_op jit(solution)/shard_map/ppermute | solution.py:374
  35.1 4.9 %collective-permute-start.16 = (f32[96,256]{1,0:T(8,128)S(1)}, f32[96,256]{1,0:T(8,128)S(1)}, u32[]{:S(2)}, u32[]{:S(2)}) collective-permute-start(f32[96,256]{1,0:T(8,128)S(1)} %get-tuple-element.64.refs_0_), channel_id=1, source_target_pairs={{0,1},{1,0},{2,3},{3,2},{4,5},{5,4},{6,7},{7,6},{8,9},{9,8},{10,11... | collective-permute-start | bytes 294920 | tf_op jit(solution)/shard_map/ppermute | solution.py:368
  36.6 3.4 %collective-permute-start.18 = (f32[96,256]{1,0:T(8,128)S(1)}, f32[96,256]{1,0:T(8,128)S(1)}, u32[]{:S(2)}, u32[]{:S(2)}) collective-permute-start(f32[96,256]{1,0:T(8,128)S(1)} %collective-permute-done.17.refs_2_), channel_id=1, source_target_pairs={{0,1},{1,0},{2,3},{3,2},{4,5},{5,4},{6,7},{7,6},{8,9},{9,8},{10,11... | collective-permute-start | bytes 294920 | tf_op jit(solution)/shard_map/ppermute | solution.py:368
  38.7 1.3 %collective-permute-start.20 = (f32[96,256]{1,0:T(8,128)S(1)}, f32[96,256]{1,0:T(8,128)S(1)}, u32[]{:S(2)}, u32[]{:S(2)}) collective-permute-start(f32[96,256]{1,0:T(8,128)S(1)} %collective-permute-done.19.refs_3_), channel_id=1, source_target_pairs={{0,1},{1,0},{2,3},{3,2},{4,5},{5,4},{6,7},{7,6},{8,9},{9,8},{10,11... | collective-permute-start | bytes 294920 | tf_op jit(solution)/shard_map/ppermute | solution.py:368
  40.0 1.6 %collective-permute-start.21 = (f32[96,256]{1,0:T(8,128)S(1)}, f32[96,256]{1,0:T(8,128)S(1)}, u32[]{:S(2)}, u32[]{:S(2)}) collective-permute-start(f32[96,256]{1,0:T(8,128)S(1)} %collective-permute-done.14.refs_1_), channel_id=1, source_target_pairs={{0,1},{1,0},{2,3},{3,2},{4,5},{5,4},{6,7},{7,6},{8,9},{9,8},{10,11... | collective-permute-start | bytes 294920 | tf_op jit(solution)/shard_map/ppermute | solution.py:368

commit v8 on v6

--- a/solution.py
+++ b/solution.py
@@ -255,7 +255,12 @@
     pre, refs = refs[:with_pre], refs[with_pre:]
     lineP_ref, lineF_ref, start_ref, *outs, pre_ref = refs
     if with_pre > 2:
-        whole_kernel(*pre[1:], pre_ref)
+        g = where()[0]
+
+        @pl.when((g // width % 2 == 1) & (g % width != 0))
+        def _():
+            whole_kernel(*pre[1:], pre_ref)
+
     if count:
         advance(width, states, pre[:1], [pre_ref] if with_pre > 2 else pre[1:], start_ref)
 

time: 43.7 us -> 43.7 us (level)
  no operation moved by 1% of the time
where the time goes in v8:
time: 43.7 us; the launch traced here: 43.3 us
  starting transfers between devices  23.2 us (53%)
  waiting for transfers between devices  12.6 us (29%)
  Pallas kernels  6.78 us (16%)
  between operations  0.77 us (2%)
    ppermute x10, starting transfers between devices, swap(): return lax.ppermute(value, 'ry', [(i, i ^ 1) for i in range(places)])  8.32 us
    ppermute x3, starting transfers between devices, from_heads(): return lax.ppermute(value, 'ry', filled([(h, h ^ d) for h in heads], chips))  7.68 us
    pallas_call x12, Pallas kernels, run(): pl.pallas_call(kernel, in_specs=specs, out_specs=[out_spec] * len(outs),...  6.78 us
    ppermute x3, waiting for transfers between devices, to_heads(): return lax.ppermute(value, 'ry', filled([(h ^ d, h) for h in heads], chips))  5.7 us
    ppermute x10, waiting for transfers between devices, swap(): return lax.ppermute(value, 'ry', [(i, i ^ 1) for i in range(places)])  4.75 us
    ppermute x5, starting transfers between devices, hops(): out.append(lax.ppermute(value, ('rx', 'ry'), pairs))  3.56 us
    ppermute x3, starting transfers between devices, to_heads(): return lax.ppermute(value, 'ry', filled([(h ^ d, h) for h in heads], chips))  3.14 us
    ppermute x3, waiting for transfers between devices, from_heads(): return lax.ppermute(value, 'ry', filled([(h, h ^ d) for h in heads], chips))  1.31 us
  transfers between devices with their start and end apart: 22, of which 10 were waited for; matrix products, arithmetic and copies ran while one was open for 0% of the time, Pallas kernels for 6%

profile of v8, /device:TPU:7, one launch (start us, length us, event | category | flops | bytes accessed | tf_op | source)
XLA Modules:
  0.0 43.3 jit_solution(570221249817961223)
XLA Ops:
  0.6 1.8 %shard_map.41 = (f32[256,640]{1,0:T(8,128)S(1)}, f32[256,640]{1,0:T(8,128)S(1)}, f32[1,256,640]{2,1,0:T(8,128)S(1)}) custom-call(f32[2,256,256]{2,1,0:T(8,128)} %a_ref.1, f32[2,256,384]{2,1,0:T(8,128)} %f_ref.1), custom_call_target="tpu_custom_call" | custom-call | tf_op jit(solution)/shard_map/pallas_call | solution.py:34
  2.5 0.7 %collective-permute-start = (f32[256,640]{1,0:T(8,128)S(1)}, f32[256,640]{1,0:T(8,128)S(1)}, u32[]{:S(2)}, u32[]{:S(2)}) collective-permute-start(f32[256,640]{1,0:T(8,128)S(1)} %get-tuple-element.41.own_ref), channel_id=1, source_target_pairs={{0,1},{1,0},{2,3},{3,2},{4,5},{5,4},{6,7},{7,6},{8,9},{9,8},{10,11... | collective-permute-start | bytes 1966088 | tf_op jit(solution)/shard_map/ppermute | solution.py:370
  3.2 1.7 %collective-permute-done.other_ref = f32[256,640]{1,0:T(8,128)S(1)} collective-permute-done((f32[256,640]{1,0:T(8,128)S(1)}, f32[256,640]{1,0:T(8,128)S(1)}, u32[]{:S(2)}, u32[]{:S(2)}) %collective-permute-start) | collective-permute-done | bytes 655392 | tf_op jit(solution)/shard_map/ppermute | solution.py:370
  4.9 0.6 %shard_map.42 = (f32[256,256]{1,0:T(8,128)S(1)}, f32[384,256]{1,0:T(8,128)S(1)}, f32[224,256]{1,0:T(8,128)S(1)}) custom-call(f32[256,640]{1,0:T(8,128)S(1)} %get-tuple-element.41.own_ref, f32[256,640]{1,0:T(8,128)S(1)} %collective-permute-done.other_ref), custom_call_target="tpu_custom_call" | custom-call | tf_op jit(solution)/shard_map/pallas_call | solution.py:34
  5.6 2.3 %collective-permute-start.2 = (f32[224,256]{1,0:T(8,128)S(1)}, f32[224,256]{1,0:T(8,128)S(1)}, u32[]{:S(2)}, u32[]{:S(2)}) collective-permute-start(f32[224,256]{1,0:T(8,128)S(1)} %get-tuple-element.51), channel_id=1, source_target_pairs={{6,2},{7,3},{0,4},{1,5},{2,0},{3,1},{4,6},{5,7},{14,10},{15,11},{8... | collective-permute-start | bytes 688136 | tf_op jit(solution)/shard_map/ppermute | solution.py:373
  8.0 0.7 %collective-permute-start.3 = (f32[224,256]{1,0:T(8,128)S(1)}, f32[224,256]{1,0:T(8,128)S(1)}, u32[]{:S(2)}, u32[]{:S(2)}) collective-permute-start(f32[224,256]{1,0:T(8,128)S(1)} %get-tuple-element.53), channel_id=1, source_target_pairs={{4,2},{5,3},{2,4},{3,5},{0,1},{1,0},{6,7},{7,6},{12,10},{13,11},{1... | collective-permute-start | bytes 688136 | tf_op jit(solution)/shard_map/ppermute | solution.py:373
  8.7 1.0 %shard_map.44 = (bf16[2,2,256,256]{3,2,1,0:T(8,128)(2,1)S(1)}, f32[2,256,384]{2,1,0:T(8,128)S(1)}) custom-call(f32[256,640]{1,0:T(8,128)S(1)} %collective-permute-done.other_ref, f32[256,640]{1,0:T(8,128)S(1)} %get-tuple-element.67.first_ref, f32[1,256,640]{2,1,0:T(8,128)S(1)} %get-tuple-element.48.rest_ref), custom_call_target="tpu_custom_call" | custom-call | flops 3000000000 | tf_op jit(solution)/shard_map/pallas_call | solution.py:34
  9.7 2.8 %collective-permute-done.2.refs_3_ = f32[224,256]{1,0:T(8,128)S(1)} collective-permute-done((f32[224,256]{1,0:T(8,128)S(1)}, f32[224,256]{1,0:T(8,128)S(1)}, u32[]{:S(2)}, u32[]{:S(2)}) %collective-permute-start.2) | collective-permute-done | bytes 229408 | tf_op jit(solution)/shard_map/ppermute | solution.py:373
  12.6 2.0 %collective-permute-start.5 = (f32[224,256]{1,0:T(8,128)S(1)}, f32[224,256]{1,0:T(8,128)S(1)}, u32[]{:S(2)}, u32[]{:S(2)}) collective-permute-start(f32[224,256]{1,0:T(8,128)S(1)} %collective-permute-done.2.refs_3_), channel_id=1, source_target_pairs={{0,1},{1,0},{2,3},{3,2},{4,5},{5,4},{6,7},{7,6},{8,9},{9,8},{10,11... | collective-permute-start | bytes 688136 | tf_op jit(solution)/shard_map/ppermute | solution.py:370
  14.6 2.9 %collective-permute-done.1.refs_2_ = f32[224,256]{1,0:T(8,128)S(1)} collective-permute-done((f32[224,256]{1,0:T(8,128)S(1)}, f32[224,256]{1,0:T(8,128)S(1)}, u32[]{:S(2)}, u32[]{:S(2)}) %collective-permute-start.1) | collective-permute-done | bytes 229408 | tf_op jit(solution)/shard_map/ppermute | solution.py:373
  17.5 1.2 %collective-permute-start.4 = (f32[224,256]{1,0:T(8,128)S(1)}, f32[224,256]{1,0:T(8,128)S(1)}, u32[]{:S(2)}, u32[]{:S(2)}) collective-permute-start(f32[224,256]{1,0:T(8,128)S(1)} %collective-permute-done.1.refs_2_), channel_id=1, source_target_pairs={{0,1},{1,0},{2,3},{3,2},{4,5},{5,4},{6,7},{7,6},{8,9},{9,8},{10,11... | collective-permute-start | bytes 688136 | tf_op jit(solution)/shard_map/ppermute | solution.py:370
  20.2 2.2 %collective-permute-start.11 = (f32[96,256]{1,0:T(8,128)S(1)}, f32[96,256]{1,0:T(8,128)S(1)}, u32[]{:S(2)}, u32[]{:S(2)}) collective-permute-start(f32[96,256]{1,0:T(8,128)S(1)} %get-tuple-element.55.refs_2_), channel_id=1, source_target_pairs={{0,1},{1,0},{2,3},{3,2},{4,5},{5,4},{6,7},{7,6},{8,9},{9,8},{10,11... | collective-permute-start | bytes 294920 | tf_op jit(solution)/shard_map/ppermute | solution.py:392
  22.9 0.8 %collective-permute-done.7.refs_0_.refs_2_ = f32[96,256]{1,0:T(8,128)S(1)} collective-permute-done((f32[96,256]{1,0:T(8,128)S(1)}, f32[96,256]{1,0:T(8,128)S(1)}, u32[]{:S(2)}, u32[]{:S(2)}) %collective-permute-start.7) | collective-permute-done | bytes 98336 | tf_op jit(solution)/shard_map/ppermute | solution.py:392
  24.1 0.7 %collective-permute-start.8 = (f32[96,256]{1,0:T(8,128)S(1)}, f32[96,256]{1,0:T(8,128)S(1)}, u32[]{:S(2)}, u32[]{:S(2)}) collective-permute-start(f32[96,256]{1,0:T(8,128)S(1)} %shard_map.47), channel_id=1, source_target_pairs={{10,26},{11,27},{12,28},{13,29}} | collective-permute-start | bytes 294920 | tf_op jit(solution)/shard_map/ppermute | solution.py:392
  25.4 0.7 %collective-permute-done.12.refs_5_ = f32[64,256]{1,0:T(8,128)S(1)} collective-permute-done((f32[64,256]{1,0:T(8,128)S(1)}, f32[64,256]{1,0:T(8,128)S(1)}, u32[]{:S(2)}, u32[]{:S(2)}) %collective-permute-start.12) | collective-permute-done | bytes 65568 | tf_op jit(solution)/shard_map/ppermute | solution.py:370
  26.5 0.7 %shard_map.49 = (f32[96,256]{1,0:T(8,128)S(1)}, f32[96,256]{1,0:T(8,128)S(1)}, f32[96,256]{1,0:T(8,128)S(1)}) custom-call(f32[96,256]{1,0:T(8,128)S(1)} %collective-permute-done.8.refs_0_, f32[96,256]{1,0:T(8,128)S(1)} %collective-permute-done.9.refs_1_, f32[96,256]{1,0:T(8,128)S(1)} %collective-permute-done.7.refs_0_.refs_2_, ...), custom_call_target="tpu_custom_call" | custom-call | tf_op jit(solution)/shard_map/pallas_call | solution.py:34
  27.2 6.3 %collective-permute-start.17 = (f32[96,256]{1,0:T(8,128)S(1)}, f32[96,256]{1,0:T(8,128)S(1)}, u32[]{:S(2)}, u32[]{:S(2)}) collective-permute-start(f32[96,256]{1,0:T(8,128)S(1)} %get-tuple-element.71), channel_id=1, source_target_pairs={{2,6},{3,7},{4,0},{5,1},{0,2},{1,3},{6,4},{7,5},{10,14},{11,15},{1... | collective-permute-start | bytes 294920 | tf_op jit(solution)/shard_map/ppermute | solution.py:376
  33.5 1.3 %collective-permute-start.19 = (f32[96,256]{1,0:T(8,128)S(1)}, f32[96,256]{1,0:T(8,128)S(1)}, u32[]{:S(2)}, u32[]{:S(2)}) collective-permute-start(f32[96,256]{1,0:T(8,128)S(1)} %get-tuple-element.73), channel_id=1, source_target_pairs={{2,4},{3,5},{4,2},{5,3},{0,1},{1,0},{6,7},{7,6},{10,12},{11,13},{1... | collective-permute-start | bytes 294920 | tf_op jit(solution)/shard_map/ppermute | solution.py:376
  35.1 1.0 %collective-permute-start.16 = (f32[96,256]{1,0:T(8,128)S(1)}, f32[96,256]{1,0:T(8,128)S(1)}, u32[]{:S(2)}, u32[]{:S(2)}) collective-permute-start(f32[96,256]{1,0:T(8,128)S(1)} %get-tuple-element.64.refs_0_), channel_id=1, source_target_pairs={{0,1},{1,0},{2,3},{3,2},{4,5},{5,4},{6,7},{7,6},{8,9},{9,8},{10,11... | collective-permute-start | bytes 294920 | tf_op jit(solution)/shard_map/ppermute | solution.py:370
  36.6 2.1 %collective-permute-start.18 = (f32[96,256]{1,0:T(8,128)S(1)}, f32[96,256]{1,0:T(8,128)S(1)}, u32[]{:S(2)}, u32[]{:S(2)}) collective-permute-start(f32[96,256]{1,0:T(8,128)S(1)} %collective-permute-done.17.refs_2_), channel_id=1, source_target_pairs={{0,1},{1,0},{2,3},{3,2},{4,5},{5,4},{6,7},{7,6},{8,9},{9,8},{10,11... | collective-permute-start | bytes 294920 | tf_op jit(solution)/shard_map/ppermute | solution.py:370
  38.7 1.3 %collective-permute-done.14.refs_1_ = f32[96,256]{1,0:T(8,128)S(1)} collective-permute-done((f32[96,256]{1,0:T(8,128)S(1)}, f32[96,256]{1,0:T(8,128)S(1)}, u32[]{:S(2)}, u32[]{:S(2)}) %collective-permute-start.14) | collective-permute-done | bytes 98336 | tf_op jit(solution)/shard_map/ppermute | solution.py:376
  40.0 0.7 %collective-permute-start.21 = (f32[96,256]{1,0:T(8,128)S(1)}, f32[96,256]{1,0:T(8,128)S(1)}, u32[]{:S(2)}, u32[]{:S(2)}) collective-permute-start(f32[96,256]{1,0:T(8,128)S(1)} %collective-permute-done.14.refs_1_), channel_id=1, source_target_pairs={{0,1},{1,0},{2,3},{3,2},{4,5},{5,4},{6,7},{7,6},{8,9},{9,8},{10,11... | collective-permute-start | bytes 294920 | tf_op jit(solution)/shard_map/ppermute | solution.py:370
  40.7 0.9 %collective-permute-done.21.refs_5_ = f32[96,256]{1,0:T(8,128)S(1)} collective-permute-done((f32[96,256]{1,0:T(8,128)S(1)}, f32[96,256]{1,0:T(8,128)S(1)}, u32[]{:S(2)}, u32[]{:S(2)}) %collective-permute-start.21) | collective-permute-done | bytes 98336 | tf_op jit(solution)/shard_map/ppermute | solution.py:370
  41.6 1.7 %shard_map.52 = (f32[2,256,384]{2,1,0:T(8,128)}, f32[2,256,384]{2,1,0:T(8,128)}) custom-call(f32[96,256]{1,0:T(8,128)S(1)} %get-tuple-element.64.refs_0_, f32[96,256]{1,0:T(8,128)S(1)} %collective-permute-done.14.refs_1_, f32[96,256]{1,0:T(8,128)S(1)} %collective-permute-done.17.refs_2_, f32[96,256]{1,0:T(8,128)S(1)} %collective-permute-done.19.refs_3_, ...), custom_call_target="tpu_custom_call" | custom-call | tf_op jit(solution)/shard_map/pallas_call | solution.py:34
  (32 shorter events, 4.3 us)
Async XLA Ops:
  2.5 2.5 %collective-permute-start = (f32[256,640]{1,0:T(8,128)S(1)}, f32[256,640]{1,0:T(8,128)S(1)}, u32[]{:S(2)}, u32[]{:S(2)}) collective-permute-start(f32[256,640]{1,0:T(8,128)S(1)} %get-tuple-element.41.own_ref), channel_id=1, source_target_pairs={{0,1},{1,0},{2,3},{3,2},{4,5},{5,4},{6,7},{7,6},{8,9},{9,8},{10,11... | collective-permute-start | bytes 1966088 | tf_op jit(solution)/shard_map/ppermute | solution.py:370
  5.6 7.0 %collective-permute-start.2 = (f32[224,256]{1,0:T(8,128)S(1)}, f32[224,256]{1,0:T(8,128)S(1)}, u32[]{:S(2)}, u32[]{:S(2)}) collective-permute-start(f32[224,256]{1,0:T(8,128)S(1)} %get-tuple-element.51), channel_id=1, source_target_pairs={{6,2},{7,3},{0,4},{1,5},{2,0},{3,1},{4,6},{5,7},{14,10},{15,11},{8... | collective-permute-start | bytes 688136 | tf_op jit(solution)/shard_map/ppermute | solution.py:373
  7.9 9.5 %collective-permute-start.1 = (f32[224,256]{1,0:T(8,128)S(1)}, f32[224,256]{1,0:T(8,128)S(1)}, u32[]{:S(2)}, u32[]{:S(2)}) collective-permute-start(f32[224,256]{1,0:T(8,128)S(1)} %get-tuple-element.45), channel_id=1, source_target_pairs={{0,2},{1,3},{6,4},{7,5},{2,0},{3,1},{4,6},{5,7},{8,10},{9,11},{14,... | collective-permute-start | bytes 688136 | tf_op jit(solution)/shard_map/ppermute | solution.py:373
  8.0 10.7 %collective-permute-start.3 = (f32[224,256]{1,0:T(8,128)S(1)}, f32[224,256]{1,0:T(8,128)S(1)}, u32[]{:S(2)}, u32[]{:S(2)}) collective-permute-start(f32[224,256]{1,0:T(8,128)S(1)} %get-tuple-element.53), channel_id=1, source_target_pairs={{4,2},{5,3},{2,4},{3,5},{0,1},{1,0},{6,7},{7,6},{12,10},{13,11},{1... | collective-permute-start | bytes 688136 | tf_op jit(solution)/shard_map/ppermute | solution.py:373
  12.6 6.7 %collective-permute-start.5 = (f32[224,256]{1,0:T(8,128)S(1)}, f32[224,256]{1,0:T(8,128)S(1)}, u32[]{:S(2)}, u32[]{:S(2)}) collective-permute-start(f32[224,256]{1,0:T(8,128)S(1)} %collective-permute-done.2.refs_3_), channel_id=1, source_target_pairs={{0,1},{1,0},{2,3},{3,2},{4,5},{5,4},{6,7},{7,6},{8,9},{9,8},{10,11... | collective-permute-start | bytes 688136 | tf_op jit(solution)/shard_map/ppermute | solution.py:370
  17.5 2.3 %collective-permute-start.4 = (f32[224,256]{1,0:T(8,128)S(1)}, f32[224,256]{1,0:T(8,128)S(1)}, u32[]{:S(2)}, u32[]{:S(2)}) collective-permute-start(f32[224,256]{1,0:T(8,128)S(1)} %collective-permute-done.1.refs_2_), channel_id=1, source_target_pairs={{0,1},{1,0},{2,3},{3,2},{4,5},{5,4},{6,7},{7,6},{8,9},{9,8},{10,11... | collective-permute-start | bytes 688136 | tf_op jit(solution)/shard_map/ppermute | solution.py:370
  18.7 1.5 %collective-permute-start.6 = (f32[224,256]{1,0:T(8,128)S(1)}, f32[224,256]{1,0:T(8,128)S(1)}, u32[]{:S(2)}, u32[]{:S(2)}) collective-permute-start(f32[224,256]{1,0:T(8,128)S(1)} %collective-permute-done.3.refs_4_), channel_id=1, source_target_pairs={{0,1},{1,0},{2,3},{3,2},{4,5},{5,4},{6,7},{7,6},{8,9},{9,8},{10,11... | collective-permute-start | bytes 688136 | tf_op jit(solution)/shard_map/ppermute | solution.py:370
  18.7 17.4 %collective-permute-start.15 = (f32[256,640]{1,0:T(8,128)S(1)}, f32[256,640]{1,0:T(8,128)S(1)}, u32[]{:S(2)}, u32[]{:S(2)}) collective-permute-start(f32[256,640]{1,0:T(8,128)S(1)} %get-tuple-element.67.first_ref), channel_id=1, source_target_pairs={{0,31},{1,0},{2,1},{3,2},{4,3},{5,4},{6,5},{7,6},{8,7},{9,8},{10,9... | collective-permute-start | bytes 1966088 | tf_op jit(solution)/shard_map/ppermute | solution.py:424
  20.2 5.0 %collective-permute-start.11 = (f32[96,256]{1,0:T(8,128)S(1)}, f32[96,256]{1,0:T(8,128)S(1)}, u32[]{:S(2)}, u32[]{:S(2)}) collective-permute-start(f32[96,256]{1,0:T(8,128)S(1)} %get-tuple-element.55.refs_2_), channel_id=1, source_target_pairs={{0,1},{1,0},{2,3},{3,2},{4,5},{5,4},{6,7},{7,6},{8,9},{9,8},{10,11... | collective-permute-start | bytes 294920 | tf_op jit(solution)/shard_map/ppermute | solution.py:392
  22.4 1.3 %collective-permute-start.7 = (f32[96,256]{1,0:T(8,128)S(1)}, f32[96,256]{1,0:T(8,128)S(1)}, u32[]{:S(2)}, u32[]{:S(2)}) collective-permute-start(f32[96,256]{1,0:T(8,128)S(1)} %get-tuple-element.55.refs_2_), channel_id=1, source_target_pairs={{0,1},{1,0},{2,10},{3,11},{4,12},{5,13},{6,7},{7,6},{8,9},{9,8},{1... | collective-permute-start | bytes 294920 | tf_op jit(solution)/shard_map/ppermute | solution.py:392
  22.4 2.3 %collective-permute-start.10 = (f32[128,256]{1,0:T(8,128)S(1)}, f32[128,256]{1,0:T(8,128)S(1)}, u32[]{:S(2)}, u32[]{:S(2)}) collective-permute-start(f32[128,256]{1,0:T(8,128)S(1)} %get-tuple-element.58), channel_id=1, source_target_pairs={{0,1},{1,0},{2,3},{3,2},{4,5},{5,4},{6,7},{7,6},{8,9},{9,8},{10,11... | collective-permute-start | bytes 393224 | tf_op jit(solution)/shard_map/ppermute | solution.py:392
  23.9 2.6 %collective-permute-start.9 = (f32[96,256]{1,0:T(8,128)S(1)}, f32[96,256]{1,0:T(8,128)S(1)}, u32[]{:S(2)}, u32[]{:S(2)}) collective-permute-start(f32[96,256]{1,0:T(8,128)S(1)} %shard_map.47), channel_id=1, source_target_pairs={{0,1},{1,0},{2,3},{3,2},{4,5},{5,4},{6,7},{7,6},{8,9},{9,8},{10,18... | collective-permute-start | bytes 294920 | tf_op jit(solution)/shard_map/ppermute | solution.py:392
  24.1 2.4 %collective-permute-start.8 = (f32[96,256]{1,0:T(8,128)S(1)}, f32[96,256]{1,0:T(8,128)S(1)}, u32[]{:S(2)}, u32[]{:S(2)}) collective-permute-start(f32[96,256]{1,0:T(8,128)S(1)} %shard_map.47), channel_id=1, source_target_pairs={{10,26},{11,27},{12,28},{13,29}} | collective-permute-start | bytes 294920 | tf_op jit(solution)/shard_map/ppermute | solution.py:392
  24.8 1.3 %collective-permute-start.12 = (f32[64,256]{1,0:T(8,128)S(1)}, f32[64,256]{1,0:T(8,128)S(1)}, u32[]{:S(2)}, u32[]{:S(2)}) collective-permute-start(f32[64,256]{1,0:T(8,128)S(1)} %get-tuple-element.60), channel_id=1, source_target_pairs={{0,1},{1,0},{2,3},{3,2},{4,5},{5,4},{6,7},{7,6},{8,9},{9,8},{10,11... | collective-permute-start | bytes 196616 | tf_op jit(solution)/shard_map/ppermute | solution.py:370
  25.2 1.3 %collective-permute-start.13 = (f32[64,256]{1,0:T(8,128)S(1)}, f32[64,256]{1,0:T(8,128)S(1)}, u32[]{:S(2)}, u32[]{:S(2)}) collective-permute-start(f32[64,256]{1,0:T(8,128)S(1)} %get-tuple-element.61), channel_id=1, source_target_pairs={{0,1},{1,0},{2,3},{3,2},{4,5},{5,4},{6,7},{7,6},{8,9},{9,8},{10,11... | collective-permute-start | bytes 196616 | tf_op jit(solution)/shard_map/ppermute | solution.py:370
  27.2 9.4 %collective-permute-start.17 = (f32[96,256]{1,0:T(8,128)S(1)}, f32[96,256]{1,0:T(8,128)S(1)}, u32[]{:S(2)}, u32[]{:S(2)}) collective-permute-start(f32[96,256]{1,0:T(8,128)S(1)} %get-tuple-element.71), channel_id=1, source_target_pairs={{2,6},{3,7},{4,0},{5,1},{0,2},{1,3},{6,4},{7,5},{10,14},{11,15},{1... | collective-permute-start | bytes 294920 | tf_op jit(solution)/shard_map/ppermute | solution.py:376
  33.5 3.1 %collective-permute-start.19 = (f32[96,256]{1,0:T(8,128)S(1)}, f32[96,256]{1,0:T(8,128)S(1)}, u32[]{:S(2)}, u32[]{:S(2)}) collective-permute-start(f32[96,256]{1,0:T(8,128)S(1)} %get-tuple-element.73), channel_id=1, source_target_pairs={{2,4},{3,5},{4,2},{5,3},{0,1},{1,0},{6,7},{7,6},{10,12},{11,13},{1... | collective-permute-start | bytes 294920 | tf_op jit(solution)/shard_map/ppermute | solution.py:376
  35.0 5.0 %collective-permute-start.14 = (f32[96,256]{1,0:T(8,128)S(1)}, f32[96,256]{1,0:T(8,128)S(1)}, u32[]{:S(2)}, u32[]{:S(2)}) collective-permute-start(f32[96,256]{1,0:T(8,128)S(1)} %get-tuple-element.65), channel_id=1, source_target_pairs={{2,0},{3,1},{4,6},{5,7},{0,2},{1,3},{6,4},{7,5},{10,8},{11,9},{12,... | collective-permute-start | bytes 294920 | tf_op jit(solution)/shard_map/ppermute | solution.py:376
  35.1 4.9 %collective-permute-start.16 = (f32[96,256]{1,0:T(8,128)S(1)}, f32[96,256]{1,0:T(8,128)S(1)}, u32[]{:S(2)}, u32[]{:S(2)}) collective-permute-start(f32[96,256]{1,0:T(8,128)S(1)} %get-tuple-element.64.refs_0_), channel_id=1, source_target_pairs={{0,1},{1,0},{2,3},{3,2},{4,5},{5,4},{6,7},{7,6},{8,9},{9,8},{10,11... | collective-permute-start | bytes 294920 | tf_op jit(solution)/shard_map/ppermute | solution.py:370
  36.6 3.4 %collective-permute-start.18 = (f32[96,256]{1,0:T(8,128)S(1)}, f32[96,256]{1,0:T(8,128)S(1)}, u32[]{:S(2)}, u32[]{:S(2)}) collective-permute-start(f32[96,256]{1,0:T(8,128)S(1)} %collective-permute-done.17.refs_2_), channel_id=1, source_target_pairs={{0,1},{1,0},{2,3},{3,2},{4,5},{5,4},{6,7},{7,6},{8,9},{9,8},{10,11... | collective-permute-start | bytes 294920 | tf_op jit(solution)/shard_map/ppermute | solution.py:370
  38.7 1.3 %collective-permute-start.20 = (f32[96,256]{1,0:T(8,128)S(1)}, f32[96,256]{1,0:T(8,128)S(1)}, u32[]{:S(2)}, u32[]{:S(2)}) collective-permute-start(f32[96,256]{1,0:T(8,128)S(1)} %collective-permute-done.19.refs_3_), channel_id=1, source_target_pairs={{0,1},{1,0},{2,3},{3,2},{4,5},{5,4},{6,7},{7,6},{8,9},{9,8},{10,11... | collective-permute-start | bytes 294920 | tf_op jit(solution)/shard_map/ppermute | solution.py:370
  40.0 1.6 %collective-permute-start.21 = (f32[96,256]{1,0:T(8,128)S(1)}, f32[96,256]{1,0:T(8,128)S(1)}, u32[]{:S(2)}, u32[]{:S(2)}) collective-permute-start(f32[96,256]{1,0:T(8,128)S(1)} %collective-permute-done.14.refs_1_), channel_id=1, source_target_pairs={{0,1},{1,0},{2,3},{3,2},{4,5},{5,4},{6,7},{7,6},{8,9},{9,8},{10,11... | collective-permute-start | bytes 294920 | tf_op jit(solution)/shard_map/ppermute | solution.py:370
